TPU v7x, 32 devices: a whole 2x2x4 slice. The times are simulated.
32 devices in a mesh: dp: 8 (over z, x), ctx: 4 (over y, core).
Axes of the slice: x: 2, y: 2, z: 4, core: 2. Of those that a mesh axis runs over, the one named last changes fastest.
Arguments:
- patches: bfloat16 [1024, 5120], P('dp'), may hold values from -6 to 6
- vit_gain: float32 [1280], replicated, may hold values from 0.1 to 1.9
- merge_up: bfloat16 [5120, 3072], P(None, 'ctx'), may hold values from -0.078125 to 0.078125
- merge_down: bfloat16 [3072, 8192], P('ctx'), may hold values from -0.109375 to 0.109375
- dest: int32 [1024], P(('dp', 'ctx')), may hold values from 0 to 4095, as said below
- text: bfloat16 [8, 512, 8192], P('dp', 'ctx'), may hold values from -6 to 6
- norm_gain: float32 [8192], replicated, may hold values from 0.5 to 1.5
- kv_weight: bfloat16 [8192, 1024], P(('dp', 'ctx')), may hold values from -0.0625 to 0.0625
- queries: bfloat16 [8, 512, 4096], P('dp', 'ctx'), may hold values from -256 to 256
- out_grad: bfloat16 [8, 512, 4096], P('dp', 'ctx'), may hold values from -6 to 6
- assign: int32 [8], replicated, may hold values from 0 to 7, each once
- docs: int32 [8, 512], P('dp'), may hold values from 0 to 3, never falling along the last dimension, each value on 1 to 256 neighbouring positions
Outputs:
- attn_out: bfloat16 [8, 512, 4096], P('dp', 'ctx')
- q_grad: bfloat16 [8, 512, 4096], P('dp', 'ctx')
- hidden_grad: bfloat16 [8, 512, 8192], P('dp', 'ctx')
- visual_grad: bfloat16 [1024, 8192], P(('dp', 'ctx'))
Inputs may be any that keep to these rules, and one draw needn't show every extreme that they name: `dest`: all entries are distinct. The 32 entries held by one device name rows of 32 devices' blocks of 128 rows per device (row // 128 names the device), each such device named by exactly one entry of the holding device. Every device's block receives exactly 32 entries, which fill one run of consecutive rows, in the order of the entries' index within their holding device.
All inputs are finite; a program needn't handle non-finite values.
Results may differ from a plain program's by a relative error of at most 0.035.
Values may be sent and summed in bfloat16 or wider, within the bound.
No kernel may reach another device: no remote copies, remote signals or barrier semaphores. Data moves between devices by JAX's collectives and lax.ppermute only.
A program may use at most 192 MiB of HBM per device.

v0:
```python
import jax
import jax.numpy as jnp
from jax import lax
from jax.sharding import PartitionSpec as P

HEADS = 32
KVH = 4
HD = 128


epsilon = 1e-06


def merger_norm(patches, vit_gain):
    pieces = patches.astype(jnp.float32).reshape(patches.shape[0], 4, vit_gain.shape[0])
    center = pieces - jnp.mean(pieces, axis=-1, keepdims=True)
    spread = jnp.mean(center * center, axis=-1, keepdims=True)
    scaled = center * lax.rsqrt(spread + epsilon) * vit_gain
    return scaled.reshape(patches.shape[0], -1).astype(jnp.bfloat16)


def rms_scale(hidden32, norm_gain):
    square = jnp.mean(hidden32 * hidden32, axis=-1, keepdims=True)
    return hidden32 * lax.rsqrt(square + epsilon) * norm_gain


def attend(query_rows, pair_rows, upstream_rows, query_pos, query_doc, key_pos, key_doc):
    row_count = query_rows.shape[0]
    key_count = pair_rows.shape[0]
    group_size = HEADS // KVH
    score_scale = HD ** (-0.5)
    query_heads = query_rows.reshape(row_count, KVH, group_size, HD)
    key_heads = pair_rows[:, : KVH * HD].reshape(key_count, KVH, HD)
    value_heads = pair_rows[:, KVH * HD :].reshape(key_count, KVH, HD)
    scores = (
        jnp.einsum("qhgd,khd->hgqk", query_heads, key_heads, preferred_element_type=jnp.float32)
        * score_scale
    )
    allowed = (key_pos[None, :] <= query_pos[:, None]) & (key_doc[None, :] == query_doc[:, None])
    scores = jnp.where(allowed, scores, -jnp.inf)
    weights = jnp.exp(scores - jnp.max(scores, axis=-1, keepdims=True))
    weights = weights / jnp.sum(weights, axis=-1, keepdims=True)
    light_weights = weights.astype(jnp.bfloat16)
    output = jnp.einsum(
        "hgqk,khd->qhgd", light_weights, value_heads, preferred_element_type=jnp.float32
    )
    upstream = upstream_rows.reshape(row_count, KVH, group_size, HD)
    value_grad = jnp.einsum(
        "hgqk,qhgd->khd", light_weights, upstream, preferred_element_type=jnp.float32
    )
    weight_grad = jnp.einsum(
        "qhgd,khd->hgqk", upstream, value_heads, preferred_element_type=jnp.float32
    )
    inner_sum = jnp.sum(weights * weight_grad, axis=-1, keepdims=True)
    score_grad = (weights * (weight_grad - inner_sum) * score_scale).astype(jnp.bfloat16)
    query_grad = jnp.einsum(
        "hgqk,khd->qhgd", score_grad, key_heads, preferred_element_type=jnp.float32
    )
    key_grad = jnp.einsum(
        "hgqk,qhgd->khd", score_grad, query_heads, preferred_element_type=jnp.float32
    )
    output = output.reshape(row_count, HEADS * HD).astype(jnp.bfloat16)
    query_grad = query_grad.reshape(row_count, HEADS * HD).astype(jnp.bfloat16)
    return (
        output,
        query_grad,
        key_grad.reshape(key_count, KVH * HD),
        value_grad.reshape(key_count, KVH * HD),
    )


def local(
    patches,
    vit_gain,
    merge_up,
    merge_down,
    dest,
    text,
    norm_gain,
    kv_weight,
    queries,
    out_grad,
    assign,
    docs,
):
    ctx_count = lax.axis_size("ctx")
    data_count = lax.axis_size("dp")
    device_count = ctx_count * data_count
    token_rows = text.shape[1]
    visual_rows = dest.shape[0]
    capacity = max(1, visual_rows // device_count)
    slot_total = device_count * capacity
    normed = merger_norm(patches, vit_gain)
    inner_hidden = jax.nn.gelu(
        jnp.dot(normed, merge_up, preferred_element_type=jnp.float32), approximate=False
    ).astype(jnp.bfloat16)
    visual = lax.psum_scatter(
        jnp.dot(inner_hidden, merge_down, preferred_element_type=jnp.float32).astype(jnp.bfloat16),
        "ctx",
        scatter_dimension=0,
        tiled=True,
    )
    target = dest // token_rows
    local_row = dest % token_rows
    token_order = jnp.arange(visual_rows, dtype=jnp.int32)
    before = (target[:, None] == target[None, :]) & (token_order[None, :] < token_order[:, None])
    slot_index = target * capacity + jnp.sum(before.astype(jnp.int32), axis=1)
    picking = jnp.arange(slot_total, dtype=jnp.int32)[:, None] == slot_index[None, :]
    outgoing = jnp.dot(
        picking.astype(jnp.bfloat16), visual, preferred_element_type=jnp.float32
    ).astype(jnp.bfloat16)
    outgoing_rows = jnp.sum(jnp.where(picking, local_row[None, :] + 1, 0), axis=1) - 1
    arrived, arrived_rows = (
        lax.all_to_all(outgoing, ("dp", "ctx"), split_axis=0, concat_axis=0, tiled=True),
        lax.all_to_all(outgoing_rows, ("dp", "ctx"), split_axis=0, concat_axis=0, tiled=True),
    )
    placing = jnp.arange(token_rows, dtype=jnp.int32)[:, None] == arrived_rows[None, :]
    placed = jnp.dot(
        placing.astype(jnp.bfloat16), arrived, preferred_element_type=jnp.float32
    ).astype(jnp.bfloat16)
    marked = jnp.any(placing, axis=1)
    hidden = jnp.where(marked[:, None], placed, text[0])
    hidden32 = hidden.astype(jnp.float32)
    normed_hidden = rms_scale(hidden32, norm_gain).astype(jnp.bfloat16)
    projected = jnp.dot(
        normed_hidden,
        lax.all_gather(kv_weight, ("dp", "ctx"), axis=0, tiled=True),
        preferred_element_type=jnp.float32,
    )
    pairs_local = projected.astype(jnp.bfloat16)
    pairs_all = lax.all_gather(pairs_local, "ctx", axis=0, tiled=True)
    halves = token_rows // 2
    length = token_rows * ctx_count
    positions = (assign[:, None] * halves + jnp.arange(halves, dtype=jnp.int32)[None, :]).reshape(
        length
    )
    labels = docs[0].reshape(-1, halves)[assign].reshape(length)
    own_start = lax.axis_index("ctx") * token_rows
    query_pos = lax.dynamic_slice_in_dim(positions, own_start, token_rows, 0)
    query_doc = lax.dynamic_slice_in_dim(labels, own_start, token_rows, 0)
    attention, query_grad, key_grad, value_grad = attend(
        queries[0], pairs_all, out_grad[0], query_pos, query_doc, positions, labels
    )
    key_grad, value_grad = (
        lax.psum_scatter(
            key_grad.astype(jnp.bfloat16), "ctx", scatter_dimension=0, tiled=True
        ).astype(jnp.float32),
        lax.psum_scatter(
            value_grad.astype(jnp.bfloat16), "ctx", scatter_dimension=0, tiled=True
        ).astype(jnp.float32),
    )
    pair_grad = jnp.concatenate([key_grad, value_grad], axis=1).astype(jnp.bfloat16)
    contract = (((1,), (1,)), ((), ()))
    normed_grad = lax.dot_general(
        pair_grad,
        lax.all_gather(kv_weight, ("dp", "ctx"), axis=0, tiled=True),
        contract,
        preferred_element_type=jnp.float32,
    )
    forward_value, pullback = jax.vjp(lambda values: rms_scale(values, norm_gain), hidden32)
    full_grad = pullback(normed_grad)[0]
    hidden_grad = jnp.where(marked[:, None], jnp.float32(0.0), full_grad).astype(jnp.bfloat16)
    returning = jnp.dot(
        placing.T.astype(jnp.bfloat16),
        full_grad.astype(jnp.bfloat16),
        preferred_element_type=jnp.float32,
    ).astype(jnp.bfloat16)
    returned = lax.all_to_all(returning, ("dp", "ctx"), split_axis=0, concat_axis=0, tiled=True)
    visual_grad = jnp.dot(
        picking.T.astype(jnp.bfloat16), returned, preferred_element_type=jnp.float32
    ).astype(jnp.bfloat16)
    return (attention[None], query_grad[None], hidden_grad[None], visual_grad)


def solution(mesh):
    placed = (
        P("dp", None),
        P(),
        P(None, "ctx"),
        P("ctx", None),
        P(("dp", "ctx")),
        P("dp", "ctx", None),
        P(),
        P(("dp", "ctx"), None),
        P("dp", "ctx", None),
        P("dp", "ctx", None),
        P(),
        P("dp", None),
    )
    return jax.shard_map(
        local,
        mesh=mesh,
        in_specs=placed,
        out_specs=(
            P("dp", "ctx", None),
            P("dp", "ctx", None),
            P("dp", "ctx", None),
            P(("dp", "ctx"), None),
        ),
        check_vma=False,
    )
```

profile of v0, /device:TPU:0, one launch (start us, length us, event | category | flops | bytes accessed | tf_op | source)
XLA Modules:
  0.0 298.7 jit_solution(4922381389353539666)
XLA Ops:
  8.0 0.7 mul.122
  8.8 2.9 reshape.128
  11.6 0.4 reduce_sum.82
  12.0 0.8 multiply_reduce_fusion.2
  12.9 0.4 mul.119
  13.3 0.5 copy.108
  13.8 0.4 sub.44
  14.2 2.0 copy.107
  16.1 13.6 %convolution_convert_fusion.1 = bf16[128,8192]{1,0:T(8,128)(2,1)} fusion(bf16[768,8192]{1,0:T(8,128)(2,1)} %param.15, bf16[5120,768]{1,0:T(8,128)(2,1)} %param.14, f32[128,5120]{1,0:T(8,128)S(1)} %bitcast.116, f32[128,5120]{1,0:T(8,128)} %bitcast.117, f32[5120]{0:T(1024)S(1)} %mul.123, bf16[128,5120]{1,0:T(8,128)(2,1)} %param.12), kind=kOutput, calls=%fused_computation.5 | convolution fusion | flops 2627960832 | bytes 29118464 | tf_op jit(solution)/shard_map/dot_general | solution.py:98
  29.8 0.5 all-gather.3.cloned.1.call-update
  30.4 0.2 convert_reduce_fusion
  30.6 0.1 select_reduce_fusion
  30.7 0.7 copy.64
  31.4 7.3 %all-to-all-start = ((s32[32,1,1]{2,1,0:T(1,128)}), s32[32,1,1]{2,1,0:T(1,128)S(1)}, u32[]{:S(2)}, u32[]{:S(2)}) async-start(s32[32,1,1]{2,1,0:T(1,128)} %copy.64), calls=%async_computation | async-start | bytes 32768 | tf_op jit(solution)/shard_map/all_to_all | solution.py:115
  38.7 25.4 %reduce-scatter.8.cloned.1.call-done = bf16[32,8192]{1,0:T(8,128)(2,1)} async-done(((bf16[128,8192]{1,0:T(8,128)(2,1)}), bf16[32,8192]{1,0:T(8,128)(2,1)}) %reduce-scatter.8.cloned.1.call-update) | async-done | bytes 524304 | tf_op jit(solution)/shard_map/reduce_scatter | solution.py:97
  64.1 1.3 fusion.4
  65.5 0.5 broadcast.191
  66.0 0.9 reduce.5
  66.9 1.2 reshape.160
  68.1 4.6 %all-to-all-start.1 = ((bf16[32,2,4096]{2,1,0:T(2,128)(2,1)}), bf16[32,2,4096]{2,1,0:T(2,128)(2,1)S(1)}, u32[]{:S(2)}, u32[]{:S(2)}) async-start(bf16[32,2,4096]{2,1,0:T(2,128)(2,1)} %reshape.160), calls=%async_computation.2 | async-start | bytes 1048576 | tf_op jit(solution)/shard_map/all_to_all | solution.py:114
  72.7 0.2 all-gather.5.cloned.1.call-start
  72.9 0.7 reduce
  73.6 0.1 fusion.91
  73.7 27.4 %all-to-all-done.1 = bf16[32,2,4096]{2,1,0:T(2,128)(2,1)S(1)} async-done(((bf16[32,2,4096]{2,1,0:T(2,128)(2,1)}), bf16[32,2,4096]{2,1,0:T(2,128)(2,1)S(1)}, u32[]{:S(2)}, u32[]{:S(2)}) %all-to-all-start.1) | async-done | bytes 524320 | tf_op jit(solution)/shard_map/all_to_all | solution.py:114
  101.1 0.5 reshape.161
  101.7 4.9 %multiply_reduce_fusion.1 = (f32[128]{0:T(128)S(1)}, f32[128,8192]{1,0:T(8,128)}) fusion(bf16[1,128,8192]{2,1,0:T(8,128)(2,1)} %param.17, bf16[32,1,8192]{2,1,0:T(2,128)(2,1)S(1)} %reshape.161, s32[32]{0:T(128)S(1)} %reduce, pred[128]{0:T(512)(128)(4,1)S(1)} %fusion.91), kind=kOutput, calls=%fused_computation.28 | convolution fusion | flops 72355712 | bytes 6816512 | tf_op jit(solution)/shard_map/dot_general | solution.py:118
  106.6 54.1 %all-gather.3.cloned.1.call-done = bf16[8192,1024]{1,0:T(8,128)(2,1)} async-done(((bf16[256,1024]{1,0:T(8,128)(2,1)}), bf16[8192,1024]{1,0:T(8,128)(2,1)}) %all-gather.3.cloned.1.call-update) | async-done | bytes 16777232 | tf_op jit(solution)/shard_map/all_gather | solution.py:127
  160.7 10.3 %fusion.39 = bf16[128,1024]{1,0:T(8,128)(2,1)} fusion(bf16[8192,1024]{1,0:T(8,128)(2,1)} %all-gather.3.cloned.1.call-done, f32[128,8192]{1,0:T(8,128)} %get-tuple-element.27, f32[8192]{0:T(1024)S(1)} %copy-done.3, f32[128]{0:T(128)S(1)} %fusion.104), kind=kOutput, calls=%fused_computation.52 | convolution fusion | flops 2150760448 | bytes 21266944 | tf_op jit(solution)/shard_map/dot_general | solution.py:125
  171.1 0.5 broadcast.188
  171.6 0.7 reduce.4
  172.3 0.1 reshape_squeeze.9
  172.4 0.1 add.89
  172.5 0.6 gather_fusion
  173.1 0.1 eq.71
  173.3 1.3 copy.105
  174.6 0.7 copy.106
  175.3 0.2 compare_and_fusion
  175.5 10.6 %all-gather.5.cloned.1.call-done = bf16[512,1024]{1,0:T(8,128)(2,1)} async-done(((bf16[128,1024]{1,0:T(8,128)(2,1)}), bf16[512,1024]{1,0:T(8,128)(2,1)}) %all-gather.5.cloned.1.call-update) | async-done | bytes 1048592 | tf_op jit(solution)/shard_map/all_gather | solution.py:131
  186.1 1.3 fusion.138
  187.4 0.1 reshape.130
  187.5 0.3 copy.85
  187.8 7.1 %fusion.139 = (f32[4,8,128]{2,1,0:T(8,128)S(1)}, f32[4,8,128,512]{2,3,1,0:T(8,128)}) fusion(pred[128,512]{0,1:T(8,128)(4,1)S(1)} %compare_and_fusion, bf16[512,4,128,1]{0,2,3,1:T(8,128)(2,1)S(1)} %copy.85, bf16[128,4,8,128]{0,3,2,1:T(8,128)(2,1)} %bitcast.119), kind=kOutput, calls=%fused_computation.180 | convolution fusion | flops 545260032 | bytes 10043392 | tf_op jit(solution)/shard_map/sub | solution.py:41
  194.9 4.9 %fusion.35 = bf16[4,512,128]{1,2,0:T(8,128)(2,1)S(1)} fusion(bf16[128,4,8,128]{0,3,2,1:T(8,128)(2,1)S(1)} %bitcast.112, f32[4,8,128,512]{2,3,1,0:T(8,128)} %get-tuple-element.29, f32[4,8,128]{2,1,0:T(8,128)S(1)} %get-tuple-element.28), kind=kOutput, calls=%fused_computation.50 | convolution fusion | flops 541327360 | bytes 9977856 | tf_op jit(solution)/shard_map/hgqk,qhgd->khd/dot_general | solution.py:48
  199.8 1.0 copy.101
  200.9 0.1 reshape.129
  201.0 4.4 %fusion.46 = f32[4,512,128,8]{2,1,3,0:T(8,128)} fusion(bf16[128,4,8,128]{0,3,2,1:T(8,128)(2,1)S(1)} %bitcast.113, bf16[512,4,128,1]{2,1,0,3:T(4,128)(2,1)S(1)} %bitcast.114), kind=kOutput, calls=%fused_computation.60 | convolution fusion | flops 536870912 | bytes 9961472 | tf_op jit(solution)/shard_map/qhgd,khd->hgqk/dot_general | solution.py:51
  205.5 12.4 %fusion.38 = bf16[4,512,128]{1,2,0:T(8,128)(2,1)S(1)} fusion(bf16[128,4,8,128]{0,3,2,1:T(8,128)(2,1)S(1)} %bitcast.120, f32[4,512,128,8]{2,1,3,0:T(8,128)} %fusion.46, f32[4,8,128,512]{2,3,1,0:T(8,128)} %get-tuple-element.29, f32[4,8,128]{2,1,0:T(8,128)S(1)} %get-tuple-element.28), kind=kOutput, calls=%fused_computation.51 | convolution fusion | flops 551817728 | bytes 18366464 | tf_op jit(solution)/shard_map/hgqk,qhgd->khd/dot_general | solution.py:59
  217.9 1.0 copy.99
  218.9 4.3 %fusion.25 = bf16[4,128,8,128]{3,1,2,0:T(8,128)(2,1)S(1)} fusion(bf16[512,4,128,1]{2,1,0,3:T(4,128)(2,1)S(1)} %bitcast.115, f32[4,8,128,512]{2,3,1,0:T(8,128)} %get-tuple-element.29, f32[4,8,128]{2,1,0:T(8,128)S(1)} %get-tuple-element.28), kind=kOutput, calls=%fused_computation.44 | convolution fusion | flops 541589504 | bytes 9977856 | tf_op jit(solution)/shard_map/hgqk,khd->qhgd/dot_general | solution.py:44
  223.2 1.3 copy.79
  224.5 13.5 %fusion.28 = bf16[4,128,8,128]{3,1,2,0:T(8,128)(2,1)S(1)} fusion(bf16[512,4,128,1]{0,2,3,1:T(8,128)(2,1)S(1)} %copy.85, f32[4,512,128,8]{2,1,3,0:T(8,128)} %fusion.46, f32[4,8,128,512]{2,3,1,0:T(8,128)} %get-tuple-element.29, f32[4,8,128]{2,1,0:T(8,128)S(1)} %get-tuple-element.28), kind=kOutput, calls=%fused_computation.45 | convolution fusion | flops 552079872 | bytes 18366464 | tf_op jit(solution)/shard_map/hgqk,khd->qhgd/dot_general | solution.py:56
  238.0 1.3 copy.80
  239.4 1.0 copy.102
  240.4 6.8 %reduce-scatter.10.cloned.1.call-done = bf16[128,512]{1,0:T(8,128)(2,1)} async-done(((bf16[512,512]{1,0:T(8,128)(2,1)}), bf16[128,512]{1,0:T(8,128)(2,1)}) %reduce-scatter.10.cloned.1.call-update) | async-done | bytes 131088
  247.2 1.0 copy.100
  248.3 14.5 %multiply_reduce_fusion = (f32[128]{0:T(128)S(1)}, f32[128,8192]{1,0:T(8,128)}) fusion(f32[128,8192]{1,0:T(8,128)} %get-tuple-element.27, f32[8192]{0:T(1024)S(1)} %copy-done.3, bf16[8192,1024]{1,0:T(8,128)(2,1)} %all-gather.3.cloned.1.call-done, bf16[128,512]{0,1:T(8,128)(2,1)S(1)} %copy.102, bf16[128,512]{0,1:T(8,128)(2,1)S(1)} %copy.100), kind=kOutput, calls=%fused_computation.23 | convolution fusion | flops 2151153664 | bytes 25461248 | tf_op jit(solution)/shard_map/dot_general | solution.py:154
  262.8 4.4 %fusion.5 = bf16[32,1,8192]{2,0,1:T(8,128)(2,1)S(1)} fusion(s32[32]{0:T(128)S(1)} %reduce, f32[128,8192]{1,0:T(8,128)} %get-tuple-element.27, f32[128,8192]{1,0:T(8,128)} %get-tuple-element.31, f32[128]{0:T(128)S(1)} %multiply_multiply_fusion.5, f32[128]{0:T(128)S(1)} %fusion.104), kind=kOutput, calls=%fused_computation.12 | convolution fusion | flops 72617984 | bytes 8914048 | tf_op jit(solution)/shard_map/dot_general | solution.py:163
  267.2 0.9 reduce.6
  268.1 1.2 reshape.162
  269.3 4.6 %all-to-all-start.2 = ((bf16[32,2,4096]{2,1,0:T(2,128)(2,1)}), bf16[32,2,4096]{2,1,0:T(2,128)(2,1)S(1)}, u32[]{:S(2)}, u32[]{:S(2)}) async-start(bf16[32,2,4096]{2,1,0:T(2,128)(2,1)} %reshape.162), calls=%async_computation.3 | async-start | bytes 1048576 | tf_op jit(solution)/shard_map/all_to_all | solution.py:168
  273.9 5.8 %fusion.17 = bf16[1,128,8192]{2,1,0:T(8,128)(2,1)} fusion(pred[128]{0:T(512)(128)(4,1)S(1)} %fusion.91, f32[128,8192]{1,0:T(8,128)} %get-tuple-element.27, f32[128]{0:T(128)S(1)} %multiply_multiply_fusion.5, f32[128,8192]{1,0:T(8,128)} %get-tuple-element.31, f32[128]{0:T(128)S(1)} %fusion.104), kind=kLoop, calls=%fused_computation.36 | loop fusion | flops 6291456 | bytes 10486912 | tf_op jit(solution)/shard_map/broadcast_in_dim | solution.py:172
  279.7 9.7 %all-to-all-done.2 = bf16[32,2,4096]{2,1,0:T(2,128)(2,1)S(1)} async-done(((bf16[32,2,4096]{2,1,0:T(2,128)(2,1)}), bf16[32,2,4096]{2,1,0:T(2,128)(2,1)S(1)}, u32[]{:S(2)}, u32[]{:S(2)}) %all-to-all-start.2) | async-done | bytes 524320 | tf_op jit(solution)/shard_map/all_to_all | solution.py:168
  289.4 0.5 reshape.163
  290.0 1.6 convolution_convert_fusion.2
  (37 shorter events, 0.6 us)
Async XLA Ops:
  8.0 56.1 %reduce-scatter.8.cloned.1.call-start = ((), (), s32[]{:S(2)}) async-start(), calls=%async_computation.6 | async-start | bytes 2621440 | tf_op jit(solution)/shard_map/reduce_scatter | solution.py:97
  16.1 14.2 %copy-start.5 = (s32[32]{0:T(128)S(1)}, s32[32]{0:T(128)}, u32[]{:S(2)}) copy-start(s32[32]{0:T(128)} %param.16) | copy-start | bytes 388
  29.8 130.9 %all-gather.3.cloned.1.call-start = ((), (), s32[]{:S(2)}) async-start(), calls=%async_computation.7 | async-start | bytes 17301504 | tf_op jit(solution)/shard_map/all_gather | solution.py:127
  31.4 36.7 %all-to-all-start = ((s32[32,1,1]{2,1,0:T(1,128)}), s32[32,1,1]{2,1,0:T(1,128)S(1)}, u32[]{:S(2)}, u32[]{:S(2)}) async-start(s32[32,1,1]{2,1,0:T(1,128)} %copy.64), calls=%async_computation | async-start | bytes 32768 | tf_op jit(solution)/shard_map/all_to_all | solution.py:115
  68.1 33.0 %all-to-all-start.1 = ((bf16[32,2,4096]{2,1,0:T(2,128)(2,1)}), bf16[32,2,4096]{2,1,0:T(2,128)(2,1)S(1)}, u32[]{:S(2)}, u32[]{:S(2)}) async-start(bf16[32,2,4096]{2,1,0:T(2,128)(2,1)} %reshape.160), calls=%async_computation.2 | async-start | bytes 1048576 | tf_op jit(solution)/shard_map/all_to_all | solution.py:114
  72.7 113.4 %all-gather.5.cloned.1.call-start = ((), (), s32[]{:S(2)}) async-start(), calls=%async_computation.8 | async-start | bytes 1310720 | tf_op jit(solution)/shard_map/all_gather | solution.py:131
  73.7 87.1 %copy-start.3 = (f32[8192]{0:T(1024)S(1)}, f32[8192]{0:T(1024)}, u32[]{:S(2)}) copy-start(f32[8192]{0:T(1024)} %param.18) | copy-start | bytes 98308
  160.7 10.9 %copy-start.4 = (s32[1,512]{1,0:T(1,128)S(1)}, s32[1,512]{1,0:T(1,128)}, u32[]{:S(2)}) copy-start(s32[1,512]{1,0:T(1,128)} %param.23) | copy-start | bytes 6148
  160.7 11.6 %copy-start.6 = (s32[8]{0:T(128)S(1)}, s32[8]{0:T(128)}, u32[]{:S(2)}) copy-start(s32[8]{0:T(128)} %param.22) | copy-start | bytes 100
  160.7 12.6 %copy-start = (bf16[1,128,4096]{2,1,0:T(8,128)(2,1)S(1)}, bf16[1,128,4096]{2,1,0:T(8,128)(2,1)}, u32[]{:S(2)}) copy-start(bf16[1,128,4096]{2,1,0:T(8,128)(2,1)} %param.20) | copy-start | bytes 3145732
  160.7 13.9 %copy-start.1 = (bf16[1,128,4096]{2,1,0:T(8,128)(2,1)S(1)}, bf16[1,128,4096]{2,1,0:T(8,128)(2,1)}, u32[]{:S(2)}) copy-start(bf16[1,128,4096]{2,1,0:T(8,128)(2,1)} %param.21) | copy-start | bytes 3145732
  171.0 68.3 %reduce-scatter.12.cloned.1.call-start = ((), (), s32[]{:S(2)}) async-start(), calls=%async_computation.10 | async-start | bytes 655360
  200.8 46.4 %reduce-scatter.10.cloned.1.call-start = ((), (), s32[]{:S(2)}) async-start(), calls=%async_computation.9 | async-start | bytes 655360
  201.0 4.5 %copy-start.2 = (bf16[1,128,4096]{1,2,0:T(8,128)(2,1)S(1)}, bf16[1,128,4096]{1,2,0:T(8,128)(2,1)}, u32[]{:S(2)}) copy-start(bf16[1,128,4096]{1,2,0:T(8,128)(2,1)} %copy.105) | copy-start | bytes 3145732
  269.3 20.2 %all-to-all-start.2 = ((bf16[32,2,4096]{2,1,0:T(2,128)(2,1)}), bf16[32,2,4096]{2,1,0:T(2,128)(2,1)S(1)}, u32[]{:S(2)}, u32[]{:S(2)}) async-start(bf16[32,2,4096]{2,1,0:T(2,128)(2,1)} %reshape.162), calls=%async_computation.3 | async-start | bytes 1048576 | tf_op jit(solution)/shard_map/all_to_all | solution.py:168
Sparse Core Ops, SparseCore 0:
  29.9 34.1 reduce-scatter.7
  171.2 14.8 all-gather.4
  201.0 21.6 reduce-scatter.11
  225.6 21.6 reduce-scatter.9
Sparse Core Ops, SparseCore 1:
  33.6 127.1 all-gather.2
where the time goes:
time: 299 us
  waiting for transfers between devices  135 us (45%)
  matrix products  97.2 us (33%)
  local copies, waits for them, and re-layouts  23.3 us (8%)
  starting transfers between devices  16.9 us (6%)
  between operations  15.5 us (5%)
  other arithmetic  11 us (4%)
    all_gather x1, waiting for transfers between devices, local(): lax.all_gather(kv_weight, ('dp', 'ctx'), axis=0, tiled=True)  54.1 us
    all_to_all x1, waiting for transfers between devices, local(): lax.all_to_all(outgoing, ('dp', 'ctx'), split_axis=0, concat_axis=0, tile...  27.4 us
    reduce_scatter x1, waiting for transfers between devices, local(): lax.psum_scatter(jnp.dot(inner_hidden, merge_down, preferred_element_type...  25.4 us
    dot_general x1, matrix products, local(): lax.dot_general(pair_grad, lax.all_gather(kv_weight, ('dp', 'ctx'), axis=...  14.5 us
    dot_general x1, matrix products, local(): jnp.dot(inner_hidden, merge_down, preferred_element_type=jnp.float32)  13.6 us
    dot_general x1, matrix products, attend(): jnp.einsum('hgqk,khd->qhgd', score_grad, key_heads, preferred_element_typ...  13.5 us
    unnamed x27, local copies, waits for them, and re-layouts  13 us
    dot_general x1, matrix products, attend(): jnp.einsum('hgqk,qhgd->khd', score_grad, query_heads, preferred_element_t...  12.4 us
  transfers between devices with their start and end apart: 8, of which 6 were waited for; matrix products, arithmetic and copies ran while one was open for 20% of the time, Pallas kernels for 0%

commit v1 on v0

--- a/solution.py
+++ b/solution.py
@@ -1,6 +1,9 @@
 import jax
 import jax.numpy as jnp
 from jax import lax
+from jax.experimental import pallas as pl
+from jax.experimental.pallas import tpu as pltpu
+from jax.sharding import Mesh
 from jax.sharding import PartitionSpec as P
 
 HEADS = 32
@@ -172,30 +175,571 @@
     return (attention[None], query_grad[None], hidden_grad[None], visual_grad)
 
 
+def neighbor(values, axis, offset):
+    count = lax.axis_size(axis)
+    return lax.ppermute(values, axis, [(d, d ^ offset) for d in range(count)])
+
+
+def swap(values):
+    return neighbor(values, "core", 1)
+
+
+def vmem_params():
+    return pltpu.CompilerParams(vmem_limit_bytes=56 * 1024 * 1024)
+
+
+def smem():
+    return pl.BlockSpec(memory_space=pltpu.SMEM)
+
+
+def store_halves(core, values, own_ref, other_ref, block):
+    def put(own_parity):
+        for j in range(values.shape[1] // (2 * block)):
+            even = values[:, 2 * j * block : (2 * j + 1) * block]
+            odd = values[:, (2 * j + 1) * block : (2 * j + 2) * block]
+            own_ref[:, j * block : (j + 1) * block] = odd if own_parity else even
+            other_ref[:, j * block : (j + 1) * block] = even if own_parity else odd
+
+    @pl.when(core == 0)
+    def _():
+        put(0)
+
+    @pl.when(core != 0)
+    def _():
+        put(1)
+
+
+def split_halves(values, core, block):
+    rows, width = values.shape
+    step = 8 * block
+
+    def kernel(core_ref, value_ref, own_ref, other_ref):
+        store_halves(core_ref[0], value_ref[...], own_ref, other_ref, block)
+
+    half = jax.ShapeDtypeStruct((rows, width // 2), values.dtype)
+    out = pl.BlockSpec((rows, step // 2), lambda j: (0, j))
+    return pl.pallas_call(
+        kernel,
+        grid=(width // step,),
+        in_specs=[smem(), pl.BlockSpec((rows, step), lambda j: (0, j))],
+        out_specs=[out, out],
+        out_shape=[half, half],
+        compiler_params=vmem_params(),
+        name="split_halves",
+    )(core, values)
+
+
+def down_halves(inner_hidden, merge_down, core, block):
+    rows, depth = inner_hidden.shape
+    width = merge_down.shape[1]
+    step = 4 * block
+
+    def kernel(core_ref, hidden_ref, weight_ref, own_ref, other_ref):
+        product = jnp.dot(hidden_ref[...], weight_ref[...], preferred_element_type=jnp.float32)
+        store_halves(core_ref[0], product.astype(jnp.bfloat16), own_ref, other_ref, block)
+
+    half = jax.ShapeDtypeStruct((rows, width // 2), jnp.bfloat16)
+    out = pl.BlockSpec((rows, step // 2), lambda j: (0, j))
+    return pl.pallas_call(
+        kernel,
+        grid=(width // step,),
+        in_specs=[
+            smem(),
+            pl.BlockSpec((rows, depth), lambda j: (0, 0)),
+            pl.BlockSpec((depth, step), lambda j: (0, j)),
+        ],
+        out_specs=[out, out],
+        out_shape=[half, half],
+        compiler_params=vmem_params(),
+        cost_estimate=pl.CostEstimate(
+            flops=2 * rows * depth * width, bytes_accessed=2 * depth * width, transcendentals=0
+        ),
+        name="merge_down",
+    )(core, inner_hidden, merge_down)
+
+
+def project(table, own_rows, sibling_rows, visual, gain, blocks):
+    rows = own_rows.shape[0]
+    total = 2 * rows + visual.shape[0]
+    block, width = blocks[0].shape
+    quarter = width // 4
+    count = len(blocks)
+
+    def kernel(table_ref, own_ref, sibling_ref, visual_ref, gain_ref, *rest):
+        block_refs = rest[:count]
+        mine_ref, theirs_ref, buffers, total_ref, sems = rest[count:]
+        copies = [
+            pltpu.make_async_copy(block_refs[r], buffers.at[r], sems.at[r]) for r in range(count)
+        ]
+        for copy in copies:
+            copy.start()
+        for r in range(count):
+            columns = pl.ds(pl.multiple_of(table_ref[r] * block, block), block)
+            gains = gain_ref[:, columns]
+            part = jnp.concatenate(
+                [
+                    (ref[:, columns].astype(jnp.float32) * gains).astype(jnp.bfloat16)
+                    for ref in (own_ref, sibling_ref, visual_ref)
+                ],
+                axis=0,
+            )
+            copies[r].wait()
+            product = jnp.dot(part, buffers[r], preferred_element_type=jnp.float32)
+            if r == 0:
+                total_ref[...] = product
+            else:
+                total_ref[...] += product
+
+        def put(parity):
+            for piece in range(2):
+                start = 2 * piece * quarter
+                mine = slice(start + parity * quarter, start + (parity + 1) * quarter)
+                theirs = slice(start + (1 - parity) * quarter, start + (2 - parity) * quarter)
+                place = slice(piece * quarter, (piece + 1) * quarter)
+                mine_ref[:, place] = total_ref[:, mine]
+                theirs_ref[:rows, place] = total_ref[rows : 2 * rows, theirs].astype(jnp.bfloat16)
+                theirs_ref[rows : 2 * rows, place] = total_ref[:rows, theirs].astype(jnp.bfloat16)
+                theirs_ref[2 * rows :, place] = total_ref[2 * rows :, theirs].astype(jnp.bfloat16)
+
+        @pl.when(table_ref[count] == 0)
+        def _():
+            put(0)
+
+        @pl.when(table_ref[count] != 0)
+        def _():
+            put(1)
+
+    vmem = pl.BlockSpec(memory_space=pltpu.VMEM)
+    return pl.pallas_call(
+        kernel,
+        in_specs=[smem()] + [vmem] * 4 + [pl.BlockSpec(memory_space=pl.ANY)] * count,
+        out_specs=[vmem, vmem],
+        out_shape=[
+            jax.ShapeDtypeStruct((total, width // 2), jnp.float32),
+            jax.ShapeDtypeStruct((total, width // 2), jnp.bfloat16),
+        ],
+        scratch_shapes=[
+            pltpu.VMEM((count, block, width), jnp.bfloat16),
+            pltpu.VMEM((total, width), jnp.float32),
+            pltpu.SemaphoreType.DMA((count,)),
+        ],
+        compiler_params=vmem_params(),
+        cost_estimate=pl.CostEstimate(
+            flops=2 * total * count * block * width,
+            bytes_accessed=2 * count * block * (width + total),
+            transcendentals=0,
+        ),
+        name="project_pairs",
+    )(table, own_rows, sibling_rows, visual, gain, *blocks)
+
+
+def project_back(table, grads, sibling_grads, own_rows, sibling_rows, visual, gain, scale, back, keep, blocks):
+    rows = own_rows.shape[0]
+    tokens = visual.shape[0] // 2
+    total = 2 * rows + 2 * tokens
+    block, width = blocks[0].shape
+    quarter = width // 4
+    count = len(blocks)
+
+    def kernel(
+        table_ref, grad_ref, other_ref, own_ref, sibling_ref, visual_ref, gain_ref, scale_ref, back_ref, keep_ref, *rest
+    ):
+        block_refs = rest[:count]
+        held_ref, sent_ref, buffers, pair_ref, sems = rest[count:]
+        copies = [
+            pltpu.make_async_copy(block_refs[r], buffers.at[r], sems.at[r]) for r in range(count)
+        ]
+        for copy in copies:
+            copy.start()
+
+        def gather(parity):
+            for piece in range(2):
+                place = slice(piece * quarter, (piece + 1) * quarter)
+                start = (2 * piece + parity) * quarter
+                pair_ref[:, start : start + quarter] = grad_ref[:, place]
+                start = (2 * piece + 1 - parity) * quarter
+                pair_ref[:, start : start + quarter] = other_ref[:, place]
+
+        @pl.when(table_ref[count] == 0)
+        def _():
+            gather(0)
+
+        @pl.when(table_ref[count] != 0)
+        def _():
+            gather(1)
+
+        for r in range(count):
+            columns = pl.ds(pl.multiple_of(table_ref[r] * block, block), block)
+            copies[r].wait()
+            normed_grad = lax.dot_general(
+                pair_ref[...], buffers[r], (((1,), (1,)), ((), ())), preferred_element_type=jnp.float32
+            )
+            value = jnp.concatenate(
+                [ref[:, columns].astype(jnp.float32) for ref in (own_ref, sibling_ref, visual_ref)],
+                axis=0,
+            )
+            full = normed_grad * (scale_ref[...] * gain_ref[:, columns]) - value * back_ref[...]
+            full = jnp.where(keep_ref[...] > 0, full, 0.0).astype(jnp.bfloat16)
+            held_ref[:rows, columns] = full[:rows]
+            sent_ref[:rows, columns] = full[rows : 2 * rows]
+            first, second = full[2 * rows : 2 * rows + tokens], full[2 * rows + tokens :]
+
+            @pl.when(table_ref[count] == 0)
+            def _():
+                held_ref[rows:, columns] = first
+                sent_ref[rows:, columns] = second
+
+            @pl.when(table_ref[count] != 0)
+            def _():
+                held_ref[rows:, columns] = second
+                sent_ref[rows:, columns] = first
+
+    vmem = pl.BlockSpec(memory_space=pltpu.VMEM)
+    half = jax.ShapeDtypeStruct((rows + tokens, count * block), jnp.bfloat16)
+    return pl.pallas_call(
+        kernel,
+        in_specs=[smem()] + [vmem] * 9 + [pl.BlockSpec(memory_space=pl.ANY)] * count,
+        out_specs=[vmem, vmem],
+        out_shape=[half, half],
+        scratch_shapes=[
+            pltpu.VMEM((count, block, width), jnp.bfloat16),
+            pltpu.VMEM((total, width), jnp.bfloat16),
+            pltpu.SemaphoreType.DMA((count,)),
+        ],
+        compiler_params=vmem_params(),
+        cost_estimate=pl.CostEstimate(
+            flops=2 * total * count * block * width,
+            bytes_accessed=2 * count * block * (width + 2 * total),
+            transcendentals=0,
+        ),
+        name="project_back",
+    )(table, grads, sibling_grads, own_rows, sibling_rows, visual, gain, scale, back, keep, *blocks)
+
+
+def join_halves(core, held, received, rows, block):
+    total, half = held.shape
+    step = 4 * block
+
+    def kernel(core_ref, held_ref, received_ref, hidden_ref, visual_ref):
+        def put(parity):
+            for j in range(step // block):
+                source = slice(j * block, (j + 1) * block)
+                for ref, side in ((held_ref, parity), (received_ref, 1 - parity)):
+                    place = slice((2 * j + side) * block, (2 * j + side + 1) * block)
+                    hidden_ref[:, place] = ref[:rows, source]
+                    visual_ref[:, place] = ref[rows:, source]
+
+        @pl.when(core_ref[0] == 0)
+        def _():
+            put(0)
+
+        @pl.when(core_ref[0] != 0)
+        def _():
+            put(1)
+
+    part = pl.BlockSpec((total, step), lambda j: (0, j))
+    return pl.pallas_call(
+        kernel,
+        grid=(half // step,),
+        in_specs=[smem(), part, part],
+        out_specs=[
+            pl.BlockSpec((rows, 2 * step), lambda j: (0, j)),
+            pl.BlockSpec((total - rows, 2 * step), lambda j: (0, j)),
+        ],
+        out_shape=[
+            jax.ShapeDtypeStruct((rows, 2 * half), jnp.bfloat16),
+            jax.ShapeDtypeStruct((total - rows, 2 * half), jnp.bfloat16),
+        ],
+        compiler_params=vmem_params(),
+        name="join_halves",
+    )(core, held, received)
+
+
+def attend_pair(queries, upstream, pair_text, pair_visual, key_row, key_pos, key_doc, visual_row, query_pos, query_doc):
+    rows, width = queries[0].shape
+    length, pair_width = pair_text.shape
+    slots = pair_visual.shape[0]
+    own_kv = pair_width // (2 * HD)
+    heads = width // HD
+    group = heads // own_kv
+    step_heads = max(1, group // 2)
+    steps = heads // step_heads
+    score_scale = HD ** (-0.5)
+    f32, bf16 = jnp.float32, jnp.bfloat16
+
+    def kernel(
+        qa, qb, ua, ub, text_ref, visual_ref, row_s, row_l, pos_ref, doc_ref, slot_s, slot_l, qpos_ref, qdoc_ref,
+        oa, ob, ga, gb, grad_ref, grad_visual_ref, keep_ref, heads_ref, turned_ref, bias_ref, total_ref,
+    ):
+        step = pl.program_id(0)
+
+        @pl.when(step == 0)
+        def _():
+            hit = row_s[...] == slot_l[...]
+            placing = jnp.where(hit, 1.0, 0.0).astype(f32)
+            placed = jnp.dot(placing.astype(bf16), visual_ref[...], preferred_element_type=f32)
+            marked = jnp.max(placing, axis=1, keepdims=True)
+            keep_ref[...] = 1.0 - marked
+            pairs = jnp.where(marked > 0, placed, text_ref[...].astype(f32))
+            for j in range(2 * own_kv):
+                piece = pairs[:, j * HD : (j + 1) * HD]
+                heads_ref[j] = piece.astype(bf16)
+                turned_ref[j] = piece.T.astype(bf16)
+            allowed = (pos_ref[...] <= qpos_ref[...]) & (doc_ref[...] == qdoc_ref[...])
+            bias_ref[...] = jnp.where(allowed, 0.0, -jnp.inf).astype(f32)
+            total_ref[...] = jnp.zeros_like(total_ref)
+
+        head = (step * step_heads) // group
+        keys, values = heads_ref[head], heads_ref[own_kv + head]
+        keys_turned, values_turned = turned_ref[head], turned_ref[own_kv + head]
+        contract = (((1,), (1,)), ((), ()))
+        for h in range(step_heads):
+            lanes = slice(h * HD, (h + 1) * HD)
+            query = jnp.concatenate([qa[:, lanes], qb[:, lanes]], axis=0)
+            up = jnp.concatenate([ua[:, lanes], ub[:, lanes]], axis=0)
+            scores = lax.dot_general(keys, query, contract, preferred_element_type=f32)
+            scores = scores * score_scale + bias_ref[...]
+            weights = jnp.exp(scores - jnp.max(scores, axis=0, keepdims=True))
+            weights = weights * (1.0 / jnp.sum(weights, axis=0, keepdims=True))
+            light = weights.astype(bf16)
+            output = jnp.dot(values_turned, light, preferred_element_type=f32).T.astype(bf16)
+            oa[:, lanes] = output[:rows]
+            ob[:, lanes] = output[rows:]
+            total_ref[own_kv + head] += jnp.dot(light, up, preferred_element_type=f32)
+            weight_grad = lax.dot_general(values, up, contract, preferred_element_type=f32)
+            inner = jnp.sum(weights * weight_grad, axis=0, keepdims=True)
+            score_grad = (weights * (weight_grad - inner) * score_scale).astype(bf16)
+            query_grad = jnp.dot(keys_turned, score_grad, preferred_element_type=f32).T.astype(bf16)
+            ga[:, lanes] = query_grad[:rows]
+            gb[:, lanes] = query_grad[rows:]
+            total_ref[head] += jnp.dot(score_grad, query, preferred_element_type=f32)
+
+        @pl.when(step == steps - 1)
+        def _():
+            lifting = jnp.where(slot_s[...] == row_l[...], 1.0, 0.0).astype(bf16)
+            for j in range(2 * own_kv):
+                piece = total_ref[j].astype(bf16)
+                place = slice(j * HD, (j + 1) * HD)
+                grad_ref[:, place] = piece
+                grad_visual_ref[:, place] = jnp.dot(lifting, piece, preferred_element_type=f32).astype(bf16)
+
+    part = pl.BlockSpec((rows, step_heads * HD), lambda j: (0, j))
+    vmem = pl.BlockSpec(memory_space=pltpu.VMEM)
+    shape = jax.ShapeDtypeStruct
+    return pl.pallas_call(
+        kernel,
+        grid=(steps,),
+        in_specs=[part] * 4 + [vmem] * 10,
+        out_specs=[part] * 4 + [vmem] * 3,
+        out_shape=[shape((rows, width), bf16)] * 4
+        + [shape((length, pair_width), bf16), shape((slots, pair_width), bf16), shape((length, 1), f32)],
+        scratch_shapes=[
+            pltpu.VMEM((2 * own_kv, length, HD), bf16),
+            pltpu.VMEM((2 * own_kv, HD, length), bf16),
+            pltpu.VMEM((length, 2 * rows), f32),
+            pltpu.VMEM((2 * own_kv, length, HD), f32),
+        ],
+        compiler_params=vmem_params(),
+        cost_estimate=pl.CostEstimate(
+            flops=20 * rows * length * width,
+            bytes_accessed=16 * rows * width,
+            transcendentals=2 * heads * rows * length,
+        ),
+        name="attend",
+    )(
+        *queries,
+        *upstream,
+        pair_text,
+        pair_visual,
+        key_row[:, None],
+        key_row[None, :],
+        key_pos[:, None],
+        key_doc[:, None],
+        visual_row[:, None],
+        visual_row[None, :],
+        query_pos[None, :],
+        query_doc[None, :],
+    )
+
+
+def local_fast(
+    patches, vit_gain, merge_up, merge_down, dest, text, norm_gain, kv_weight, queries, out_grad, assign, docs
+):
+    f32, bf16 = jnp.float32, jnp.bfloat16
+    data_count, column_count = lax.axis_size("dp"), lax.axis_size("y")
+    ctx_count = 2 * column_count
+    data, column, core = lax.axis_index("dp"), lax.axis_index("y"), lax.axis_index("core")
+    rows, width = text.shape[1], text.shape[2]
+    tokens = dest.shape[0]
+    block = kv_weight.shape[0]
+    length = rows * ctx_count
+    core_word = core[None].astype(jnp.int32)
+
+    far = [kv_weight] + [neighbor(kv_weight, "dp", 2 * i) for i in range(1, data_count // 2)]
+    blocks, owners = [], []
+    for i, held in enumerate(far):
+        beside = neighbor(held, "dp", 1)
+        below = neighbor(held, "y", 1)
+        corner = neighbor(beside, "y", 1) if i % 2 == 0 else neighbor(below, "dp", 1)
+        for piece, along, down in ((held, 0, 0), (beside, 1, 0), (below, 0, 1), (corner, 1, 1)):
+            blocks.append(piece)
+            owners.append((data ^ (2 * i + along)) * column_count + (column ^ down))
+    table = jnp.stack(owners + [core]).astype(jnp.int32)
+
+    own_rows, other_part = split_halves(text[0], core_word, block)
+    sibling_rows = swap(other_part)
+    query_width = queries.shape[2] // 2
+
+    def heads_of(values):
+        mine = lax.dynamic_slice_in_dim(values, core * query_width, query_width, 1)
+        theirs = lax.dynamic_slice_in_dim(values, (1 - core) * query_width, query_width, 1)
+        return mine, swap(theirs)
+
+    query_parts, upstream_parts = heads_of(queries[0]), heads_of(out_grad[0])
+
+    normed = merger_norm(patches, vit_gain)
+    inner_hidden = jax.nn.gelu(
+        jnp.dot(normed, merge_up, preferred_element_type=f32), approximate=False
+    ).astype(bf16)
+    merged, merged_other = down_halves(inner_hidden, merge_down, core_word, block)
+    merged = (merged.astype(f32) + swap(merged_other).astype(f32)).astype(bf16)
+    chip_tokens = 2 * tokens
+    visual32 = lax.dynamic_slice_in_dim(merged, column * chip_tokens, chip_tokens, 0).astype(f32)
+    for offset in range(1, column_count):
+        leaving = lax.dynamic_slice_in_dim(merged, (column ^ offset) * chip_tokens, chip_tokens, 0)
+        visual32 = visual32 + neighbor(leaving, "y", offset).astype(f32)
+    visual = visual32.astype(bf16)
+
+    dest_other = swap(dest)
+    chip_dest = jnp.where(
+        core == 0, jnp.concatenate([dest, dest_other]), jnp.concatenate([dest_other, dest])
+    )
+    token_core = jnp.arange(chip_tokens, dtype=jnp.int32) // tokens
+    sequence, row_of = chip_dest // length, chip_dest % length
+    slot = sequence * (2 * ctx_count) + token_core * ctx_count + row_of // rows
+    slot_total = data_count * 2 * ctx_count
+    picking = jnp.arange(slot_total, dtype=jnp.int32)[:, None] == slot[None, :]
+    leaving_rows = jnp.sum(jnp.where(picking, row_of[None, :] + 1, 0), axis=1) - 1
+
+    def to_sequences(values):
+        shaped = values.reshape((data_count, 1, 2 * ctx_count) + values.shape[1:])
+        shaped = jnp.broadcast_to(shaped, (data_count, column_count) + shaped.shape[2:])
+        shaped = shaped.reshape((data_count * column_count,) + shaped.shape[2:])
+        return lax.all_to_all(shaped, ("dp", "y"), split_axis=0, concat_axis=0, tiled=True)
+
+    visual_row = to_sequences(leaving_rows).reshape(-1)
+
+    halves = rows // 2
+    positions = (assign[:, None] * halves + jnp.arange(halves, dtype=jnp.int32)[None, :]).reshape(length)
+    labels = docs[0].reshape(-1, halves)[assign].reshape(length)
+    order = jnp.stack(
+        [2 * (column ^ down) + (core ^ side) for down in range(column_count) for side in range(2)]
+    )
+    key_row = (order[:, None] * rows + jnp.arange(rows, dtype=jnp.int32)[None, :]).reshape(length)
+    key_pos = positions.reshape(ctx_count, rows)[order].reshape(length)
+    key_doc = labels.reshape(ctx_count, rows)[order].reshape(length)
+
+    def squares(values):
+        values = values.astype(f32)
+        return jnp.sum(values * values, axis=1)
+
+    own_squares, sibling_squares, visual_squares = squares(own_rows), squares(sibling_rows), squares(visual)
+    arrived = swap(jnp.concatenate([sibling_squares, own_squares, visual_squares]))
+    square = jnp.concatenate([own_squares, sibling_squares, visual_squares]) + arrived
+    scale = lax.rsqrt(square / width + epsilon)[:, None]
+    gain = lax.dynamic_index_in_dim(
+        norm_gain.reshape(-1, 2, block), core, axis=1, keepdims=False
+    ).reshape(1, width // 2)
+
+    mine, theirs = project(table, own_rows, sibling_rows, visual, gain, blocks)
+    pairs = ((mine + swap(theirs).astype(f32)) * scale).astype(bf16)
+    pair_chip, pair_tokens = pairs[: 2 * rows], pairs[2 * rows :]
+    pair_text = jnp.concatenate(
+        [pair_chip] + [neighbor(pair_chip, "y", down) for down in range(1, column_count)], axis=0
+    )
+    leaving = jnp.dot(picking.astype(bf16), pair_tokens, preferred_element_type=f32).astype(bf16)
+    pair_visual = to_sequences(leaving).reshape(-1, pairs.shape[1])
+    out_a, out_b, grad_a, grad_b, pair_grad, visual_pair_grad, keep = attend_pair(
+        query_parts, upstream_parts, pair_text, pair_visual, key_row, key_pos, key_doc, visual_row,
+        key_pos[: 2 * rows], key_doc[: 2 * rows],
+    )
+
+    def heads_back(held, leaving):
+        arrived = swap(leaving)
+        return jnp.where(
+            core == 0, jnp.concatenate([held, arrived], axis=1), jnp.concatenate([arrived, held], axis=1)
+        )
+
+    attention, query_grad = heads_back(out_a, out_b), heads_back(grad_a, grad_b)
+    text_grad = pair_grad[: 2 * rows].astype(f32)
+    for down in range(1, column_count):
+        part = pair_grad[2 * rows * down : 2 * rows * (down + 1)]
+        text_grad = text_grad + neighbor(part, "y", down).astype(f32)
+    returned = lax.all_to_all(
+        visual_pair_grad.reshape(data_count * column_count, 2 * ctx_count, -1),
+        ("dp", "y"), split_axis=0, concat_axis=0, tiled=True,
+    )
+    returned = jnp.sum(returned.reshape(data_count, column_count, 2 * ctx_count, -1).astype(f32), axis=1)
+    token_grad = jnp.dot(
+        picking.T.astype(bf16), returned.reshape(slot_total, -1).astype(bf16), preferred_element_type=f32
+    )
+    grads = jnp.concatenate([text_grad, token_grad], axis=0).astype(bf16)
+
+    def turned(values):
+        return jnp.concatenate([values[rows : 2 * rows], values[:rows], values[2 * rows :]], axis=0)
+
+    inner = jnp.sum(grads.astype(f32) * pairs.astype(f32), axis=1)
+    inner = inner + swap(turned(inner))
+    back = inner[:, None] * scale * scale / width
+    sibling_grads = swap(turned(grads))
+    keep_rows = jnp.concatenate([keep[: 2 * rows], jnp.ones((chip_tokens, 1), f32)], axis=0)
+    held, leaving = project_back(
+        table, grads, sibling_grads, own_rows, sibling_rows, visual, gain, scale, back, keep_rows, blocks
+    )
+    hidden_grad, visual_grad = join_halves(core_word, held, swap(leaving), rows, block)
+    return (attention[None], query_grad[None], hidden_grad[None], visual_grad)
+
+
 def solution(mesh):
-    placed = (
-        P("dp", None),
-        P(),
-        P(None, "ctx"),
-        P("ctx", None),
-        P(("dp", "ctx")),
-        P("dp", "ctx", None),
-        P(),
-        P(("dp", "ctx"), None),
-        P("dp", "ctx", None),
-        P("dp", "ctx", None),
-        P(),
-        P("dp", None),
-    )
-    return jax.shard_map(
-        local,
-        mesh=mesh,
-        in_specs=placed,
-        out_specs=(
-            P("dp", "ctx", None),
-            P("dp", "ctx", None),
-            P("dp", "ctx", None),
-            P(("dp", "ctx"), None),
-        ),
-        check_vma=False,
-    )
+    data_count, ctx_count = mesh.shape["dp"], mesh.shape["ctx"]
+    split = Mesh(mesh.devices.reshape(data_count, -1, 2), ("dp", "y", "core"))
+
+    def call(*arrays):
+        text, kv_weight, dest = arrays[5], arrays[7], arrays[4]
+        devices = data_count * ctx_count
+        rows = text.shape[1] // ctx_count
+        fits = (
+            ctx_count == 4
+            and data_count % 4 == 0
+            and data_count & (data_count - 1) == 0
+            and (kv_weight.shape[0] // devices) % 128 == 0
+            and dest.shape[0] // devices <= devices
+            and rows % 128 == 0
+        )
+        if fits:
+            whole, ctx, body, used = ("dp", "y", "core"), ("y", "core"), local_fast, split
+        else:
+            whole, ctx, body, used = ("dp", "ctx"), "ctx", local, mesh
+        placed = (
+            P("dp", None),
+            P(),
+            P(None, ctx),
+            P(ctx, None),
+            P(whole),
+            P("dp", ctx, None),
+            P(),
+            P(whole, None),
+            P("dp", ctx, None),
+            P("dp", ctx, None),
+            P(),
+            P("dp", None),
+        )
+        return jax.shard_map(
+            body,
+            mesh=used,
+            in_specs=placed,
+            out_specs=(P("dp", ctx, None), P("dp", ctx, None), P("dp", ctx, None), P(whole, None)),
+            check_vma=False,
+        )(*arrays)
+
+    return call

time: 299 us -> 228 us (0.76)
  matrix products: 97.2 us -> 7.61 us
  Pallas kernels: 0 us -> 57.1 us
  waiting for transfers between devices: 135 us -> 82.7 us
  starting transfers between devices: 16.9 us -> 37.5 us
  between operations: 15.5 us -> 1.18 us
  local copies, waits for them, and re-layouts: 23.3 us -> 27.3 us
    dot_general x12 -> x3, matrix products: 90.1 us -> 7.61 us  [the longest x1 7.26 us: local_fast(): jnp.dot(normed, merge_up, preferred_element_type=f32)]
    ppermute x0 -> x30, waiting for transfers between devices: none -> 70.6 us  [neighbor(): return lax.ppermute(values, axis, [(d, d ^ offset) for d in range(count)])]
    all_gather x2 -> x0, waiting for transfers between devices: 64.7 us -> none  [the longest x1 54.1 us: local(): lax.all_gather(kv_weight, ('dp', 'ctx'), axis=0, tiled=True)]
    pallas_call x0 -> x6, Pallas kernels: none -> 57.1 us  [the longest x1 18.5 us: attend_pair(): pl.pallas_call(kernel, grid=(steps,), in_specs=[part] * 4 + [vmem] * 10,...]
    reduce_scatter x1 -> x0, waiting for transfers between devices: 25.4 us -> none  [local(): lax.psum_scatter(jnp.dot(inner_hidden, merge_down, preferred_element_type...]
    all_to_all x3, waiting for transfers between devices: 37.2 us -> 12.1 us  [the longest x2 7.86 us: to_sequences(): lax.all_to_all(shaped, ('dp', 'y'), split_axis=0, concat_axis=0, tiled=True)]
    ppermute x0 -> x30, starting transfers between devices: none -> 24.3 us  [neighbor(): return lax.ppermute(values, axis, [(d, d ^ offset) for d in range(count)])]
    unnamed x7 -> x0, waiting for transfers between devices: 7.43 us -> none
  transfers between devices with their start and end apart: 8 -> 33, of which waited for: 6 -> 11; matrix products, arithmetic and copies ran while one was open for 20% -> 20% of each run, Pallas kernels for 0% -> 15%
where the time goes in v1:
time: 228 us; the launch traced here: 227 us
  waiting for transfers between devices  82.7 us (36%)
  Pallas kernels  57.1 us (25%)
  starting transfers between devices  37.5 us (16%)
  local copies, waits for them, and re-layouts  27.3 us (12%)
  other arithmetic  13.3 us (6%)
  matrix products  7.61 us (3%)
    ppermute x30, waiting for transfers between devices, neighbor(): return lax.ppermute(values, axis, [(d, d ^ offset) for d in range(count)])  70.6 us
    ppermute x30, starting transfers between devices, neighbor(): return lax.ppermute(values, axis, [(d, d ^ offset) for d in range(count)])  24.3 us
    pallas_call x1, Pallas kernels, attend_pair(): pl.pallas_call(kernel, grid=(steps,), in_specs=[part] * 4 + [vmem] * 10,...  18.5 us
    pallas_call x1, Pallas kernels, project_back(): pl.pallas_call(kernel, in_specs=[smem()] + [vmem] * 9 + [pl.BlockSpec(mem...  13.3 us
    all_to_all x2, starting transfers between devices, to_sequences(): lax.all_to_all(shaped, ('dp', 'y'), split_axis=0, concat_axis=0, tiled=True)  9.46 us
    pallas_call x1, Pallas kernels, down_halves(): pl.pallas_call(kernel, grid=(width // step,), in_specs=[smem(), pl.BlockS...  9.39 us
    pallas_call x1, Pallas kernels, project(): pl.pallas_call(kernel, in_specs=[smem()] + [vmem] * 4 + [pl.BlockSpec(mem...  7.98 us
    all_to_all x2, waiting for transfers between devices, to_sequences(): lax.all_to_all(shaped, ('dp', 'y'), split_axis=0, concat_axis=0, tiled=True)  7.86 us
  transfers between devices with their start and end apart: 33, of which 11 were waited for; matrix products, arithmetic and copies ran while one was open for 20% of the time, Pallas kernels for 15%

profile of v1, /device:TPU:0, one launch (start us, length us, event | category | flops | bytes accessed | tf_op | source)
XLA Modules:
  0.0 226.7 jit_solution(3689028860350490225)
XLA Ops:
  0.6 3.1 %collective-permute-start.8 = (bf16[256,1024]{1,0:T(8,128)(2,1)}, bf16[256,1024]{1,0:T(8,128)(2,1)S(1)}, u32[]{:S(2)}, u32[]{:S(2)}) collective-permute-start(bf16[256,1024]{1,0:T(8,128)(2,1)} %rest_0_.3), channel_id=1, source_target_pairs={{0,8},{4,12},{8,0},{12,4},{16,24},{20,28},{24,16},{28,20},{1,9},{5... | collective-permute-start | bytes 1572872 | tf_op jit(solution)/shard_map/ppermute | solution.py:180
  3.7 2.6 %collective-permute-start.12 = (bf16[256,1024]{1,0:T(8,128)(2,1)}, bf16[256,1024]{1,0:T(8,128)(2,1)}, u32[]{:S(2)}, u32[]{:S(2)}) collective-permute-start(bf16[256,1024]{1,0:T(8,128)(2,1)} %rest_0_.3), channel_id=1, source_target_pairs={{0,16},{4,20},{8,24},{12,28},{16,0},{20,4},{24,8},{28,12},{1,17},{... | collective-permute-start | bytes 1572872 | tf_op jit(solution)/shard_map/ppermute | solution.py:180
  6.3 2.8 %reshape.540 = f32[128,4,1280]{2,1,0:T(4,128)S(1)} reshape(bf16[128,5120]{1,0:T(8,128)(2,1)} %param.12) | data formatting | bytes 3932160 | tf_op jit(solution)/shard_map/reshape | solution.py:18
  9.6 0.8 multiply_reduce_fusion
  11.7 1.9 copy.37
  13.7 7.3 %fusion.6.hidden_ref = bf16[128,768]{1,0:T(8,128)(2,1)} fusion(bf16[5120,768]{1,0:T(8,128)(2,1)} %param.14, f32[128,5120]{1,0:T(8,128)S(1)} %bitcast.69, f32[128,5120]{1,0:T(8,128)} %bitcast.70, f32[5120]{0:T(1024)S(1)} %mul.171, bf16[128,5120]{1,0:T(8,128)(2,1)} %param.12), kind=kOutput, calls=%fused_computation.31 | convolution fusion | flops 1016299520 | bytes 14635008 | tf_op jit(solution)/shard_map/dot_general | solution.py:602
  21.0 9.4 %merge_down.1 = (bf16[128,4096]{1,0:T(8,128)(2,1)}, bf16[128,4096]{1,0:T(8,128)(2,1)}) custom-call(s32[1]{0:T(128)} %bitcast.20.core_ref, bf16[128,768]{1,0:T(8,128)(2,1)} %fusion.6.hidden_ref, bf16[768,8192]{1,0:T(8,128)(2,1)} %weight_ref.1), custom_call_target="tpu_custom_call" | custom-call | flops 1610612736 | bytes 12582912 | tf_op jit(solution)/shard_map/merge_down/pallas_call | solution.py:243
  30.9 0.6 constant_dynamic-slice_fusion
  31.6 3.9 %split_halves.1 = (bf16[128,4096]{1,0:T(8,128)(2,1)}, bf16[128,4096]{1,0:T(8,128)(2,1)}) custom-call(s32[1]{0:T(128)} %bitcast.20.core_ref, bf16[128,8192]{1,0:T(8,128)(2,1)} %bitcast.71), custom_call_target="tpu_custom_call" | custom-call | tf_op jit(solution)/shard_map/split_halves/pallas_call | solution.py:221
  35.9 1.5 multiply_reduce_fusion.2
  38.0 0.7 reduce.10
  40.5 0.8 copy.33.doc_ref
  42.5 0.9 copy.32.pos_ref
  43.3 2.4 %dynamic-slice_bitcast_fusion = (bf16[128,2048]{1,0:T(8,128)(2,1)}, bf16[128,2048]{1,0:T(8,128)(2,1)}) fusion(bf16[1,128,4096]{2,1,0:T(8,128)(2,1)} %param.21, s32[]{:T(128)S(6)} %select_n.116, s32[]{:T(128)S(6)} %select_n.115), kind=kLoop, calls=%fused_computation.23 | loop fusion | bytes 2097160 | tf_op jit(solution)/shard_map/dynamic_slice | solution.py:595
  45.8 2.3 %dynamic-slice_bitcast_fusion.2 = (bf16[128,2048]{1,0:T(8,128)(2,1)}, bf16[128,2048]{1,0:T(8,128)(2,1)}) fusion(bf16[1,128,4096]{2,1,0:T(8,128)(2,1)} %param.20, s32[]{:T(128)S(6)} %select_n.116, s32[]{:T(128)S(6)} %select_n.115), kind=kLoop, calls=%fused_computation.25 | loop fusion | bytes 2097160 | tf_op jit(solution)/shard_map/dynamic_slice | solution.py:595
  48.1 0.7 stack.96.table_ref
  48.8 1.7 collective-permute-start.5
  50.5 1.5 collective-permute-start.6
  53.3 10.2 %collective-permute-done.5.rest_1_ = bf16[256,1024]{1,0:T(8,128)(2,1)S(1)} collective-permute-done((bf16[256,1024]{1,0:T(8,128)(2,1)S(1)}, bf16[256,1024]{1,0:T(8,128)(2,1)S(1)}, u32[]{:S(2)}, u32[]{:S(2)}) %collective-permute-start.5) | collective-permute-done | bytes 524320 | tf_op jit(solution)/shard_map/ppermute | solution.py:180
  63.6 1.7 collective-permute-start.14
  65.3 1.5 collective-permute-start.18
  67.4 9.2 %collective-permute-done.10.rest_6_ = bf16[256,1024]{1,0:T(8,128)(2,1)S(1)} collective-permute-done((bf16[256,1024]{1,0:T(8,128)(2,1)S(1)}, bf16[256,1024]{1,0:T(8,128)(2,1)S(1)}, u32[]{:S(2)}, u32[]{:S(2)}) %collective-permute-start.10) | collective-permute-done | bytes 524320 | tf_op jit(solution)/shard_map/ppermute | solution.py:180
  76.5 1.5 collective-permute-start.4
  78.4 0.6 collective-permute-start.9
  79.0 20.0 %collective-permute-done.18.rest_14_ = bf16[256,1024]{1,0:T(8,128)(2,1)S(1)} collective-permute-done((bf16[256,1024]{1,0:T(8,128)(2,1)}, bf16[256,1024]{1,0:T(8,128)(2,1)S(1)}, u32[]{:S(2)}, u32[]{:S(2)}) %collective-permute-start.18) | collective-permute-done | bytes 524320 | tf_op jit(solution)/shard_map/ppermute | solution.py:180
  99.0 1.5 collective-permute-start.7
  101.4 8.9 %collective-permute-done.4 = bf16[64,4096]{1,0:T(8,128)(2,1)S(1)} collective-permute-done((bf16[64,4096]{1,0:T(8,128)(2,1)S(1)}, bf16[64,4096]{1,0:T(8,128)(2,1)S(1)}, u32[]{:S(2)}, u32[]{:S(2)}) %collective-permute-start.4) | collective-permute-done | bytes 524320 | tf_op jit(solution)/shard_map/ppermute | solution.py:180
  110.8 1.1 multiply_reduce_fusion.3
  112.1 9.4 %collective-permute-done.7.rest_3_ = bf16[256,1024]{1,0:T(8,128)(2,1)S(1)} collective-permute-done((bf16[256,1024]{1,0:T(8,128)(2,1)S(1)}, bf16[256,1024]{1,0:T(8,128)(2,1)S(1)}, u32[]{:S(2)}, u32[]{:S(2)}) %collective-permute-start.7) | collective-permute-done | bytes 524320 | tf_op jit(solution)/shard_map/ppermute | solution.py:180
  122.0 9.5 %collective-permute-done.15.rest_11_ = bf16[256,1024]{1,0:T(8,128)(2,1)S(1)} collective-permute-done((bf16[256,1024]{1,0:T(8,128)(2,1)S(1)}, bf16[256,1024]{1,0:T(8,128)(2,1)S(1)}, u32[]{:S(2)}, u32[]{:S(2)}) %collective-permute-start.15) | collective-permute-done | bytes 524320 | tf_op jit(solution)/shard_map/ppermute | solution.py:180
  131.5 0.8 copy-done.14
  132.5 8.0 %project_pairs.1 = (f32[320,512]{1,0:T(8,128)}, bf16[320,512]{1,0:T(8,128)(2,1)}) custom-call(s32[17]{0:T(128)} %stack.96.table_ref, bf16[128,4096]{1,0:T(8,128)(2,1)} %get-tuple-element.21.own_ref, bf16[128,4096]{1,0:T(8,128)(2,1)} %copy-done, bf16[64,4096]{1,0:T(8,128)(2,1)} %get-tuple-element.41.visual_ref, f32[1,4096]{1,0:T(1,128)} %bitcast.76, ...), custom_call_target="tpu_custom_call" | custom-call | flops 2684354560 | bytes 11010048 | tf_op jit(solution)/shard_map/project_pairs/pallas_call | solution.py:313
  140.7 0.6 broadcast_in_dim.33
  141.3 5.9 %all-to-all-start.1 = ((s32[16,1,8]{2,1,0:T(1,128)}), s32[16,1,8]{2,1,0:T(1,128)S(1)}, u32[]{:S(2)}, u32[]{:S(2)}) async-start(s32[16,1,8]{2,1,0:T(1,128)} %bitcast.40), calls=%async_computation.1 | async-start | bytes 16384 | tf_op jit(solution)/shard_map/all_to_all | solution.py:628
  147.3 1.2 multiply_convert_fusion.2
  148.5 2.0 collective-permute-start.22
  150.6 3.9 %all-to-all-done.1 = s32[16,1,8]{2,1,0:T(1,128)S(1)} async-done(((s32[16,1,8]{2,1,0:T(1,128)}), s32[16,1,8]{2,1,0:T(1,128)S(1)}, u32[]{:S(2)}, u32[]{:S(2)}) %all-to-all-start.1) | async-done | bytes 544 | tf_op jit(solution)/shard_map/all_to_all | solution.py:628
  154.5 0.7 broadcast_in_dim.29
  155.2 3.5 %all-to-all-start = ((bf16[16,8,512]{2,1,0:T(8,128)(2,1)}), bf16[16,8,512]{2,1,0:T(8,128)(2,1)S(1)}, u32[]{:S(2)}, u32[]{:S(2)}) async-start(bf16[16,8,512]{2,1,0:T(8,128)(2,1)} %bitcast.24), calls=%async_computation | async-start | bytes 262144 | tf_op jit(solution)/shard_map/all_to_all | solution.py:628
  158.8 0.8 copy.31.row_s
  159.6 0.7 reduce.11
  160.3 0.7 broadcast_in_dim_reshape.18.slot_s
  161.0 0.7 broadcast_in_dim_reshape.17.slot_l
  161.6 0.8 pad_maximum_fusion.text_ref
  162.5 4.0 %all-to-all-done = bf16[16,8,512]{2,1,0:T(8,128)(2,1)S(1)} async-done(((bf16[16,8,512]{2,1,0:T(8,128)(2,1)}), bf16[16,8,512]{2,1,0:T(8,128)(2,1)S(1)}, u32[]{:S(2)}, u32[]{:S(2)}) %all-to-all-start) | async-done | bytes 131104 | tf_op jit(solution)/shard_map/all_to_all | solution.py:628
  166.4 0.6 copy-done.21
  167.1 18.5 %attend.1 = (bf16[128,2048]{1,0:T(8,128)(2,1)}, bf16[128,2048]{1,0:T(8,128)(2,1)}, bf16[128,2048]{1,0:T(8,128)(2,1)}, bf16[128,2048]{1,0:T(8,128)(2,1)}, bf16[51...) custom-call(bf16[128,2048]{1,0:T(8,128)(2,1)} %get-tuple-element.45.qa, ...), custom_call_target="tpu_custom_call" | custom-call | flops 2684354560 | bytes 4194304 | tf_op jit(solution)/shard_map/attend/pallas_call | solution.py:529
  185.6 3.7 %all-to-all-start.2 = ((bf16[16,8,512]{2,1,0:T(8,128)(2,1)}), bf16[16,8,512]{2,1,0:T(8,128)(2,1)S(1)}, u32[]{:S(2)}, u32[]{:S(2)}) async-start(bf16[16,8,512]{2,1,0:T(8,128)(2,1)} %bitcast.79), calls=%async_computation.2 | async-start | bytes 262144 | tf_op jit(solution)/shard_map/all_to_all | solution.py:678
  189.4 0.8 broadcast_in_dim.66.scale_ref
  190.2 1.0 slice.49
  191.1 1.6 collective-permute-start.26
  192.8 4.2 %all-to-all-done.2 = bf16[16,8,512]{2,1,0:T(8,128)(2,1)S(1)} async-done(((bf16[16,8,512]{2,1,0:T(8,128)(2,1)}), bf16[16,8,512]{2,1,0:T(8,128)(2,1)S(1)}, u32[]{:S(2)}, u32[]{:S(2)}) %all-to-all-start.2) | async-done | bytes 131104 | tf_op jit(solution)/shard_map/all_to_all | solution.py:678
  197.3 1.2 collective-permute-done.26
  198.5 1.0 add_convert_fusion.2
  199.8 0.8 pad_maximum_fusion.1
  201.1 0.7 slice_select_fusion.keep_ref
  201.8 0.8 div.62.back_ref
  202.6 0.7 copy-done.20
  203.3 13.3 %project_back.1 = (bf16[160,4096]{1,0:T(8,128)(2,1)}, bf16[160,4096]{1,0:T(8,128)(2,1)}) custom-call(s32[17]{0:T(128)} %stack.96.table_ref, bf16[320,512]{1,0:T(8,128)(2,1)} %get-tuple-element.49.grad_ref, bf16[320,512]{1,0:T(8,128)(2,1)} %copy-done.20, bf16[128,4096]{1,0:T(8,128)(2,1)} %get-tuple-element.21.own_ref, bf16[128,4096]{1,0:T(8,128)(2,1)} %copy-done, ...), custom_call_target="tpu_custom_call" | custom-call | flops 2684354560 | bytes 13631488 | tf_op jit(solution)/shard_map/project_back/pallas_call | solution.py:399
  217.2 1.2 maximum_select_fusion.1
  218.4 2.1 collective-permute-done.24
  220.5 1.2 maximum_select_fusion
  221.7 1.1 copy-done.15
  222.7 4.0 %join_halves.1 = (bf16[128,8192]{1,0:T(8,128)(2,1)}, bf16[32,8192]{1,0:T(8,128)(2,1)}) custom-call(s32[1]{0:T(128)} %bitcast.20.core_ref, bf16[160,4096]{1,0:T(8,128)(2,1)} %get-tuple-element.34.held_ref, bf16[160,4096]{1,0:T(8,128)(2,1)} %copy-done.15), custom_call_target="tpu_custom_call" | custom-call | tf_op jit(solution)/shard_map/join_halves/pallas_call | solution.py:441
  (148 shorter events, 12.5 us)
Async XLA Ops:
  0.6 49.9 %collective-permute-start.8 = (bf16[256,1024]{1,0:T(8,128)(2,1)}, bf16[256,1024]{1,0:T(8,128)(2,1)S(1)}, u32[]{:S(2)}, u32[]{:S(2)}) collective-permute-start(bf16[256,1024]{1,0:T(8,128)(2,1)} %rest_0_.3), channel_id=1, source_target_pairs={{0,8},{4,12},{8,0},{12,4},{16,24},{20,28},{24,16},{28,20},{1,9},{5... | collective-permute-start | bytes 1572872 | tf_op jit(solution)/shard_map/ppermute | solution.py:180
  3.7 48.3 %collective-permute-start.12 = (bf16[256,1024]{1,0:T(8,128)(2,1)}, bf16[256,1024]{1,0:T(8,128)(2,1)}, u32[]{:S(2)}, u32[]{:S(2)}) collective-permute-start(bf16[256,1024]{1,0:T(8,128)(2,1)} %rest_0_.3), channel_id=1, source_target_pairs={{0,16},{4,20},{8,24},{12,28},{16,0},{20,4},{24,8},{28,12},{1,17},{... | collective-permute-start | bytes 1572872 | tf_op jit(solution)/shard_map/ppermute | solution.py:180
  6.3 46.6 %collective-permute-start.16 = (bf16[256,1024]{1,0:T(8,128)(2,1)}, bf16[256,1024]{1,0:T(8,128)(2,1)}, u32[]{:S(2)}, u32[]{:S(2)}) collective-permute-start(bf16[256,1024]{1,0:T(8,128)(2,1)} %rest_0_.3), channel_id=1, source_target_pairs={{0,24},{4,28},{8,16},{12,20},{16,8},{20,12},{24,0},{28,4},{1,25},{... | collective-permute-start | bytes 1572872 | tf_op jit(solution)/shard_map/ppermute | solution.py:180
  11.7 2.0 copy-start.26
  21.0 9.4 %copy-start.28 = (s32[32]{0:T(128)S(1)}, s32[32]{0:T(128)}, u32[]{:S(2)}) copy-start(s32[32]{0:T(128)} %param.16) | copy-start | bytes 388
  21.0 9.9 %copy-start.24 = (f32[8192]{0:T(1024)S(1)}, f32[8192]{0:T(1024)}, u32[]{:S(2)}) copy-start(f32[8192]{0:T(1024)} %param.18) | copy-start | bytes 98308
  21.0 9.9 %copy-start.30 = (s32[8]{0:T(128)S(1)}, s32[8]{0:T(128)}, u32[]{:S(2)}) copy-start(s32[8]{0:T(128)} %param.22) | copy-start | bytes 100
  30.4 7.6 %copy-start.27 = (s32[1,512]{1,0:T(1,128)S(1)}, s32[1,512]{1,0:T(1,128)}, u32[]{:S(2)}) copy-start(s32[1,512]{1,0:T(1,128)} %param.23) | copy-start | bytes 6148
  30.4 21.7 %collective-permute-start.3 = (bf16[128,4096]{1,0:T(8,128)(2,1)}, bf16[128,4096]{1,0:T(8,128)(2,1)S(1)}, u32[]{:S(2)}, u32[]{:S(2)}) collective-permute-start(bf16[128,4096]{1,0:T(8,128)(2,1)} %get-tuple-element.24), channel_id=1, source_target_pairs={{0,1},{1,0},{2,3},{3,2},{4,5},{5,4},{6,7},{7,6},{8,9},{9,8},{10,11... | collective-permute-start | bytes 3145736 | tf_op jit(solution)/shard_map/ppermute | solution.py:180
  30.4 18.4 %collective-permute-start.23 = (s32[32]{0:T(128)S(1)}, s32[32]{0:T(128)S(1)}, u32[]{:S(2)}, u32[]{:S(2)}) collective-permute-start(s32[32]{0:T(128)S(1)} %copy-done.28), channel_id=1, source_target_pairs={{0,1},{1,0},{2,3},{3,2},{4,5},{5,4},{6,7},{7,6},{8,9},{9,8},{10,11... | collective-permute-start | bytes 392 | tf_op jit(solution)/shard_map/ppermute | solution.py:180
  43.3 5.5 %copy-start.1 = (bf16[256,1024]{1,0:T(8,128)(2,1)S(1)}, bf16[256,1024]{1,0:T(8,128)(2,1)}, u32[]{:S(2)}) copy-start(bf16[256,1024]{1,0:T(8,128)(2,1)} %rest_0_.3) | copy-start | bytes 1572868
  43.3 9.3 %copy-start.16 = (bf16[128,4096]{1,0:T(8,128)(2,1)S(1)}, bf16[128,4096]{1,0:T(8,128)(2,1)}, u32[]{:S(2)}) copy-start(bf16[128,4096]{1,0:T(8,128)(2,1)} %get-tuple-element.23) | copy-start | bytes 3145732
  48.8 14.8 %collective-permute-start.5 = (bf16[256,1024]{1,0:T(8,128)(2,1)S(1)}, bf16[256,1024]{1,0:T(8,128)(2,1)S(1)}, u32[]{:S(2)}, u32[]{:S(2)}) collective-permute-start(bf16[256,1024]{1,0:T(8,128)(2,1)S(1)} %copy-done.1), channel_id=1, source_target_pairs={{0,4},{4,0},{8,12},{12,8},{16,20},{20,16},{24,28},{28,24},{1,5},{5... | collective-permute-start | bytes 1572872 | tf_op jit(solution)/shard_map/ppermute | solution.py:180
  50.5 27.9 %copy-start.2 = (bf16[256,1024]{1,0:T(8,128)(2,1)}, bf16[256,1024]{1,0:T(8,128)(2,1)S(1)}, u32[]{:S(2)}) copy-start(bf16[256,1024]{1,0:T(8,128)(2,1)S(1)} %collective-permute-done.8.rest_4_) | copy-start | bytes 1572868
  50.5 14.8 %collective-permute-start.6 = (bf16[256,1024]{1,0:T(8,128)(2,1)S(1)}, bf16[256,1024]{1,0:T(8,128)(2,1)S(1)}, u32[]{:S(2)}, u32[]{:S(2)}) collective-permute-start(bf16[256,1024]{1,0:T(8,128)(2,1)S(1)} %copy-done.1), channel_id=1, source_target_pairs={{0,2},{2,0},{1,3},{3,1},{4,6},{6,4},{5,7},{7,5},{8,10},{10,8},{9,1... | collective-permute-start | bytes 1572872 | tf_op jit(solution)/shard_map/ppermute | solution.py:180
  52.0 14.8 %collective-permute-start.2 = (bf16[128,4096]{1,0:T(8,128)(2,1)}, bf16[128,4096]{1,0:T(8,128)(2,1)S(1)}, u32[]{:S(2)}, u32[]{:S(2)}) collective-permute-start(bf16[128,4096]{1,0:T(8,128)(2,1)} %get-tuple-element.22), channel_id=1, source_target_pairs={{0,1},{1,0},{2,3},{3,2},{4,5},{5,4},{6,7},{7,6},{8,9},{9,8},{10,11... | collective-permute-start | bytes 3145736 | tf_op jit(solution)/shard_map/ppermute | solution.py:180
  52.0 24.5 %collective-permute-start.10 = (bf16[256,1024]{1,0:T(8,128)(2,1)S(1)}, bf16[256,1024]{1,0:T(8,128)(2,1)S(1)}, u32[]{:S(2)}, u32[]{:S(2)}) collective-permute-start(bf16[256,1024]{1,0:T(8,128)(2,1)S(1)} %collective-permute-done.8.rest_4_), channel_id=1, source_target_pairs={{0,2},{2,0},{1,3},{3,1},{4,6},{6,4},{5,7},{7,5},{8,10},{10,8},{9,1... | collective-permute-start | bytes 1572872 | tf_op jit(solution)/shard_map/ppermute | solution.py:180
  52.9 68.6 %copy-start.19 = (bf16[128,2048]{1,0:T(8,128)(2,1)S(1)}, bf16[128,2048]{1,0:T(8,128)(2,1)}, u32[]{:S(2)}) copy-start(bf16[128,2048]{1,0:T(8,128)(2,1)} %get-tuple-element.44) | copy-start | bytes 1572868
  52.9 25.4 %collective-permute-start.13 = (bf16[256,1024]{1,0:T(8,128)(2,1)}, bf16[256,1024]{1,0:T(8,128)(2,1)S(1)}, u32[]{:S(2)}, u32[]{:S(2)}) collective-permute-start(bf16[256,1024]{1,0:T(8,128)(2,1)} %collective-permute-done.12.rest_8_), channel_id=1, source_target_pairs={{0,4},{4,0},{8,12},{12,8},{16,20},{20,16},{24,28},{28,24},{1,5},{5... | collective-permute-start | bytes 1572872 | tf_op jit(solution)/shard_map/ppermute | solution.py:180
  63.6 68.8 %copy-start.3 = (bf16[256,1024]{1,0:T(8,128)(2,1)}, bf16[256,1024]{1,0:T(8,128)(2,1)S(1)}, u32[]{:S(2)}) copy-start(bf16[256,1024]{1,0:T(8,128)(2,1)S(1)} %collective-permute-done.5.rest_1_) | copy-start | bytes 1572868
  63.6 37.0 %collective-permute-start.14 = (bf16[256,1024]{1,0:T(8,128)(2,1)}, bf16[256,1024]{1,0:T(8,128)(2,1)S(1)}, u32[]{:S(2)}, u32[]{:S(2)}) collective-permute-start(bf16[256,1024]{1,0:T(8,128)(2,1)} %collective-permute-done.12.rest_8_), channel_id=1, source_target_pairs={{0,2},{2,0},{1,3},{3,1},{4,6},{6,4},{5,7},{7,5},{8,10},{10,8},{9,1... | collective-permute-start | bytes 1572872 | tf_op jit(solution)/shard_map/ppermute | solution.py:180
  65.3 67.1 %copy-start.4 = (bf16[256,1024]{1,0:T(8,128)(2,1)}, bf16[256,1024]{1,0:T(8,128)(2,1)S(1)}, u32[]{:S(2)}) copy-start(bf16[256,1024]{1,0:T(8,128)(2,1)S(1)} %collective-permute-done.6.rest_2_) | copy-start | bytes 1572868
  65.3 33.7 %collective-permute-start.18 = (bf16[256,1024]{1,0:T(8,128)(2,1)}, bf16[256,1024]{1,0:T(8,128)(2,1)S(1)}, u32[]{:S(2)}, u32[]{:S(2)}) collective-permute-start(bf16[256,1024]{1,0:T(8,128)(2,1)} %collective-permute-done.16.rest_12_), channel_id=1, source_target_pairs={{0,2},{2,0},{1,3},{3,1},{4,6},{6,4},{5,7},{7,5},{8,10},{10,8},{9,1... | collective-permute-start | bytes 1572872 | tf_op jit(solution)/shard_map/ppermute | solution.py:180
  66.8 65.5 %copy-start = (bf16[128,4096]{1,0:T(8,128)(2,1)}, bf16[128,4096]{1,0:T(8,128)(2,1)S(1)}, u32[]{:S(2)}) copy-start(bf16[128,4096]{1,0:T(8,128)(2,1)S(1)} %collective-permute-done.2.sibling_ref) | copy-start | bytes 3145732
  66.8 34.2 %collective-permute-start.17 = (bf16[256,1024]{1,0:T(8,128)(2,1)}, bf16[256,1024]{1,0:T(8,128)(2,1)S(1)}, u32[]{:S(2)}, u32[]{:S(2)}) collective-permute-start(bf16[256,1024]{1,0:T(8,128)(2,1)} %collective-permute-done.16.rest_12_), channel_id=1, source_target_pairs={{0,4},{4,0},{8,12},{12,8},{16,20},{20,16},{24,28},{28,24},{1,5},{5... | collective-permute-start | bytes 1572872 | tf_op jit(solution)/shard_map/ppermute | solution.py:180
  76.5 55.8 %copy-start.5 = (bf16[256,1024]{1,0:T(8,128)(2,1)}, bf16[256,1024]{1,0:T(8,128)(2,1)S(1)}, u32[]{:S(2)}) copy-start(bf16[256,1024]{1,0:T(8,128)(2,1)S(1)} %collective-permute-done.10.rest_6_) | copy-start | bytes 1572868
  76.5 33.7 %collective-permute-start.4 = (bf16[64,4096]{1,0:T(8,128)(2,1)S(1)}, bf16[64,4096]{1,0:T(8,128)(2,1)S(1)}, u32[]{:S(2)}, u32[]{:S(2)}) collective-permute-start(bf16[64,4096]{1,0:T(8,128)(2,1)S(1)} %constant_dynamic-slice_fusion.1), channel_id=1, source_target_pairs={{0,2},{2,0},{1,3},{3,1},{4,6},{6,4},{5,7},{7,5},{8,10},{10,8},{9,1... | collective-permute-start | bytes 1572872 | tf_op jit(solution)/shard_map/ppermute | solution.py:180
  78.4 54.0 %copy-start.6 = (bf16[256,1024]{1,0:T(8,128)(2,1)}, bf16[256,1024]{1,0:T(8,128)(2,1)S(1)}, u32[]{:S(2)}) copy-start(bf16[256,1024]{1,0:T(8,128)(2,1)S(1)} %collective-permute-done.13.rest_9_) | copy-start | bytes 1572868
  78.4 33.6 %collective-permute-start.9 = (bf16[256,1024]{1,0:T(8,128)(2,1)S(1)}, bf16[256,1024]{1,0:T(8,128)(2,1)S(1)}, u32[]{:S(2)}, u32[]{:S(2)}) collective-permute-start(bf16[256,1024]{1,0:T(8,128)(2,1)S(1)} %collective-permute-done.8.rest_4_), channel_id=1, source_target_pairs={{0,4},{4,0},{8,12},{12,8},{16,20},{20,16},{24,28},{28,24},{1,5},{5... | collective-permute-start | bytes 1572872 | tf_op jit(solution)/shard_map/ppermute | solution.py:180
  99.0 33.4 %copy-start.8 = (bf16[256,1024]{1,0:T(8,128)(2,1)}, bf16[256,1024]{1,0:T(8,128)(2,1)S(1)}, u32[]{:S(2)}) copy-start(bf16[256,1024]{1,0:T(8,128)(2,1)S(1)} %collective-permute-done.18.rest_14_) | copy-start | bytes 1572868
  99.0 22.5 %collective-permute-start.7 = (bf16[256,1024]{1,0:T(8,128)(2,1)S(1)}, bf16[256,1024]{1,0:T(8,128)(2,1)S(1)}, u32[]{:S(2)}, u32[]{:S(2)}) collective-permute-start(bf16[256,1024]{1,0:T(8,128)(2,1)S(1)} %collective-permute-done.5.rest_1_), channel_id=1, source_target_pairs={{0,2},{2,0},{1,3},{3,1},{4,6},{6,4},{5,7},{7,5},{8,10},{10,8},{9,1... | collective-permute-start | bytes 1572872 | tf_op jit(solution)/shard_map/ppermute | solution.py:180
  100.5 31.9 %copy-start.7 = (bf16[256,1024]{1,0:T(8,128)(2,1)}, bf16[256,1024]{1,0:T(8,128)(2,1)S(1)}, u32[]{:S(2)}) copy-start(bf16[256,1024]{1,0:T(8,128)(2,1)S(1)} %collective-permute-done.14.rest_10_) | copy-start | bytes 1572868
  100.5 21.0 %collective-permute-start.11 = (bf16[256,1024]{1,0:T(8,128)(2,1)S(1)}, bf16[256,1024]{1,0:T(8,128)(2,1)S(1)}, u32[]{:S(2)}, u32[]{:S(2)}) collective-permute-start(bf16[256,1024]{1,0:T(8,128)(2,1)S(1)} %collective-permute-done.10.rest_6_), channel_id=1, source_target_pairs={{0,4},{4,0},{8,12},{12,8},{16,20},{20,16},{24,28},{28,24},{1,5},{5... | collective-permute-start | bytes 1572872 | tf_op jit(solution)/shard_map/ppermute | solution.py:180
  101.1 31.3 %copy-start.9 = (bf16[256,1024]{1,0:T(8,128)(2,1)}, bf16[256,1024]{1,0:T(8,128)(2,1)S(1)}, u32[]{:S(2)}) copy-start(bf16[256,1024]{1,0:T(8,128)(2,1)S(1)} %collective-permute-done.17.rest_13_) | copy-start | bytes 1572868
  101.1 30.4 %collective-permute-start.15 = (bf16[256,1024]{1,0:T(8,128)(2,1)S(1)}, bf16[256,1024]{1,0:T(8,128)(2,1)S(1)}, u32[]{:S(2)}, u32[]{:S(2)}) collective-permute-start(bf16[256,1024]{1,0:T(8,128)(2,1)S(1)} %collective-permute-done.13.rest_9_), channel_id=1, source_target_pairs={{0,2},{2,0},{1,3},{3,1},{4,6},{6,4},{5,7},{7,5},{8,10},{10,8},{9,1... | collective-permute-start | bytes 1572872 | tf_op jit(solution)/shard_map/ppermute | solution.py:180
  110.2 21.3 %collective-permute-start.19 = (bf16[256,1024]{1,0:T(8,128)(2,1)S(1)}, bf16[256,1024]{1,0:T(8,128)(2,1)S(1)}, u32[]{:S(2)}, u32[]{:S(2)}) collective-permute-start(bf16[256,1024]{1,0:T(8,128)(2,1)S(1)} %collective-permute-done.18.rest_14_), channel_id=1, source_target_pairs={{0,4},{4,0},{8,12},{12,8},{16,20},{20,16},{24,28},{28,24},{1,5},{5... | collective-permute-start | bytes 1572872 | tf_op jit(solution)/shard_map/ppermute | solution.py:180
  112.0 20.4 %copy-start.10 = (bf16[256,1024]{1,0:T(8,128)(2,1)}, bf16[256,1024]{1,0:T(8,128)(2,1)S(1)}, u32[]{:S(2)}) copy-start(bf16[256,1024]{1,0:T(8,128)(2,1)S(1)} %collective-permute-done.9.rest_5_) | copy-start | bytes 1572868
  112.0 50.5 %collective-permute-start.1 = (bf16[128,2048]{1,0:T(8,128)(2,1)}, bf16[128,2048]{1,0:T(8,128)(2,1)}, u32[]{:S(2)}, u32[]{:S(2)}) collective-permute-start(bf16[128,2048]{1,0:T(8,128)(2,1)} %get-tuple-element.42), channel_id=1, source_target_pairs={{0,1},{1,0},{2,3},{3,2},{4,5},{5,4},{6,7},{7,6},{8,9},{9,8},{10,11... | collective-permute-start | bytes 1572872 | tf_op jit(solution)/shard_map/ppermute | solution.py:180
  121.5 10.9 %copy-start.11 = (bf16[256,1024]{1,0:T(8,128)(2,1)}, bf16[256,1024]{1,0:T(8,128)(2,1)S(1)}, u32[]{:S(2)}) copy-start(bf16[256,1024]{1,0:T(8,128)(2,1)S(1)} %collective-permute-done.7.rest_3_) | copy-start | bytes 1572868
  121.5 41.0 %collective-permute-start = (bf16[128,2048]{1,0:T(8,128)(2,1)S(1)}, bf16[128,2048]{1,0:T(8,128)(2,1)}, u32[]{:S(2)}, u32[]{:S(2)}) collective-permute-start(bf16[128,2048]{1,0:T(8,128)(2,1)S(1)} %copy-done.19), channel_id=1, source_target_pairs={{0,1},{1,0},{2,3},{3,2},{4,5},{5,4},{6,7},{7,6},{8,9},{9,8},{10,11... | collective-permute-start | bytes 1572872 | tf_op jit(solution)/shard_map/ppermute | solution.py:180
  121.5 10.9 %copy-start.12 = (bf16[256,1024]{1,0:T(8,128)(2,1)}, bf16[256,1024]{1,0:T(8,128)(2,1)S(1)}, u32[]{:S(2)}) copy-start(bf16[256,1024]{1,0:T(8,128)(2,1)S(1)} %collective-permute-done.11.rest_7_) | copy-start | bytes 1572868
  121.5 25.7 %collective-permute-start.21 = (f32[320]{0:T(512)S(1)}, f32[320]{0:T(512)S(1)}, u32[]{:S(2)}, u32[]{:S(2)}) collective-permute-start(f32[320]{0:T(512)S(1)} %pad_maximum_fusion.3), channel_id=1, source_target_pairs={{0,1},{1,0},{2,3},{3,2},{4,5},{5,4},{6,7},{7,6},{8,9},{9,8},{10,11... | collective-permute-start | bytes 3848 | tf_op jit(solution)/shard_map/ppermute | solution.py:180
  131.5 1.0 copy-start.13
  131.5 0.8 copy-start.14
  140.5 6.8 %collective-permute-start.20 = (bf16[320,512]{1,0:T(8,128)(2,1)}, bf16[320,512]{1,0:T(8,128)(2,1)S(1)}, u32[]{:S(2)}, u32[]{:S(2)}) collective-permute-start(bf16[320,512]{1,0:T(8,128)(2,1)} %get-tuple-element.26), channel_id=1, source_target_pairs={{0,1},{1,0},{2,3},{3,2},{4,5},{5,4},{6,7},{7,6},{8,9},{9,8},{10,11... | collective-permute-start | bytes 983048 | tf_op jit(solution)/shard_map/ppermute | solution.py:180
  141.3 13.2 %all-to-all-start.1 = ((s32[16,1,8]{2,1,0:T(1,128)}), s32[16,1,8]{2,1,0:T(1,128)S(1)}, u32[]{:S(2)}, u32[]{:S(2)}) async-start(s32[16,1,8]{2,1,0:T(1,128)} %bitcast.40), calls=%async_computation.1 | async-start | bytes 16384 | tf_op jit(solution)/shard_map/all_to_all | solution.py:628
  148.5 13.1 %collective-permute-start.22 = (bf16[256,512]{1,0:T(8,128)(2,1)S(1)}, bf16[256,512]{1,0:T(8,128)(2,1)S(1)}, u32[]{:S(2)}, u32[]{:S(2)}) collective-permute-start(bf16[256,512]{1,0:T(8,128)(2,1)S(1)} %slice.63), channel_id=1, source_target_pairs={{0,2},{2,0},{1,3},{3,1},{4,6},{6,4},{5,7},{7,5},{8,10},{10,8},{9,1... | collective-permute-start | bytes 786440 | tf_op jit(solution)/shard_map/ppermute | solution.py:180
  155.2 11.3 %all-to-all-start = ((bf16[16,8,512]{2,1,0:T(8,128)(2,1)}), bf16[16,8,512]{2,1,0:T(8,128)(2,1)S(1)}, u32[]{:S(2)}, u32[]{:S(2)}) async-start(bf16[16,8,512]{2,1,0:T(8,128)(2,1)} %bitcast.24), calls=%async_computation | async-start | bytes 262144 | tf_op jit(solution)/shard_map/all_to_all | solution.py:628
  158.7 7.7 %copy-start.25 = (s32[4,128]{1,0:T(4,128)}, s32[4,128]{1,0:T(4,128)S(1)}, u32[]{:S(2)}) copy-start(s32[4,128]{1,0:T(4,128)S(1)} %iota_add_fusion) | copy-start | bytes 6148
  166.4 0.6 copy-start.21
  185.6 11.4 %all-to-all-start.2 = ((bf16[16,8,512]{2,1,0:T(8,128)(2,1)}), bf16[16,8,512]{2,1,0:T(8,128)(2,1)S(1)}, u32[]{:S(2)}, u32[]{:S(2)}) async-start(bf16[16,8,512]{2,1,0:T(8,128)(2,1)} %bitcast.79), calls=%async_computation.2 | async-start | bytes 262144 | tf_op jit(solution)/shard_map/all_to_all | solution.py:678
  189.4 11.7 %copy-start.22 = (f32[512,1]{1,0:T(8,128)S(1)}, f32[512,1]{1,0:T(8,128)}, u32[]{:S(2)}) copy-start(f32[512,1]{1,0:T(8,128)} %get-tuple-element.33) | copy-start | bytes 6148
  189.4 11.7 %copy-start.23 = (pred[320,1]{1,0:T(32,128)(4,1)S(1)}, pred[320,1]{1,0:T(32,128)(4,1)}, u32[]{:S(2)}) copy-start(pred[320,1]{1,0:T(32,128)(4,1)} %constant.179.clone.1) | copy-start | bytes 964
  191.1 7.4 %collective-permute-start.26 = (bf16[256,512]{1,0:T(8,128)(2,1)S(1)}, bf16[256,512]{1,0:T(8,128)(2,1)S(1)}, u32[]{:S(2)}, u32[]{:S(2)}) collective-permute-start(bf16[256,512]{1,0:T(8,128)(2,1)S(1)} %slice.49), channel_id=1, source_target_pairs={{0,2},{2,0},{1,3},{3,1},{4,6},{6,4},{5,7},{7,5},{8,10},{10,8},{9,1... | collective-permute-start | bytes 786440 | tf_op jit(solution)/shard_map/ppermute | solution.py:180
  192.8 24.4 %collective-permute-start.25 = (bf16[128,2048]{1,0:T(8,128)(2,1)}, bf16[128,2048]{1,0:T(8,128)(2,1)S(1)}, u32[]{:S(2)}, u32[]{:S(2)}) collective-permute-start(bf16[128,2048]{1,0:T(8,128)(2,1)} %get-tuple-element.30), channel_id=1, source_target_pairs={{0,1},{1,0},{2,3},{3,2},{4,5},{5,4},{6,7},{7,6},{8,9},{9,8},{10,11... | collective-permute-start | bytes 1572872 | tf_op jit(solution)/shard_map/ppermute | solution.py:180
  199.8 2.0 collective-permute-start.28
  200.6 2.0 collective-permute-start.27
  202.6 0.7 copy-start.20
  203.3 13.5 %copy-start.29 = (bf16[128,2048]{1,0:T(8,128)(2,1)S(1)}, bf16[128,2048]{1,0:T(8,128)(2,1)}, u32[]{:S(2)}) copy-start(bf16[128,2048]{1,0:T(8,128)(2,1)} %get-tuple-element.28) | copy-start | bytes 1572868
  203.3 13.9 %copy-start.18 = (bf16[128,2048]{1,0:T(8,128)(2,1)S(1)}, bf16[128,2048]{1,0:T(8,128)(2,1)}, u32[]{:S(2)}) copy-start(bf16[128,2048]{1,0:T(8,128)(2,1)} %get-tuple-element.29) | copy-start | bytes 1572868
  216.6 3.9 %copy-start.17 = (bf16[128,2048]{1,0:T(8,128)(2,1)S(1)}, bf16[128,2048]{1,0:T(8,128)(2,1)}, u32[]{:S(2)}) copy-start(bf16[128,2048]{1,0:T(8,128)(2,1)} %get-tuple-element.27) | copy-start | bytes 1572868
  216.6 5.1 %collective-permute-start.29 = (bf16[160,4096]{1,0:T(8,128)(2,1)}, bf16[160,4096]{1,0:T(8,128)(2,1)S(1)}, u32[]{:S(2)}, u32[]{:S(2)}) collective-permute-start(bf16[160,4096]{1,0:T(8,128)(2,1)} %get-tuple-element.35), channel_id=1, source_target_pairs={{0,1},{1,0},{2,3},{3,2},{4,5},{5,4},{6,7},{7,6},{8,9},{9,8},{10,11... | collective-permute-start | bytes 3932168 | tf_op jit(solution)/shard_map/ppermute | solution.py:180
  216.8 3.6 %collective-permute-start.24 = (bf16[128,2048]{1,0:T(8,128)(2,1)S(1)}, bf16[128,2048]{1,0:T(8,128)(2,1)S(1)}, u32[]{:S(2)}, u32[]{:S(2)}) collective-permute-start(bf16[128,2048]{1,0:T(8,128)(2,1)S(1)} %copy-done.29), channel_id=1, source_target_pairs={{0,1},{1,0},{2,3},{3,2},{4,5},{5,4},{6,7},{7,6},{8,9},{9,8},{10,11... | collective-permute-start | bytes 1572872 | tf_op jit(solution)/shard_map/ppermute | solution.py:180
  221.7 1.1 copy-start.15

commit v2 on v0

--- a/solution.py
+++ b/solution.py
@@ -1,6 +1,9 @@
 import jax
 import jax.numpy as jnp
 from jax import lax
+from jax.experimental import pallas as pl
+from jax.experimental.pallas import tpu as pltpu
+from jax.sharding import Mesh
 from jax.sharding import PartitionSpec as P
 
 HEADS = 32
@@ -172,30 +175,693 @@
     return (attention[None], query_grad[None], hidden_grad[None], visual_grad)
 
 
+def neighbor(values, axis, offset):
+    count = lax.axis_size(axis)
+    return lax.ppermute(values, axis, [(d, d ^ offset) for d in range(count)])
+
+
+def after(values, earlier):
+    return lax.optimization_barrier((values, *earlier))[0]
+
+
+def swap(values):
+    return neighbor(values, "core", 1)
+
+
+def vmem_params(size=16):
+    return pltpu.CompilerParams(vmem_limit_bytes=size * 1024 * 1024)
+
+
+def brief():
+    return pl.CostEstimate(flops=1, bytes_accessed=1, transcendentals=0)
+
+
+def smem():
+    return pl.BlockSpec(memory_space=pltpu.SMEM)
+
+
+def store_halves(core, values, own_ref, other_ref, block):
+    def put(own_parity):
+        for j in range(values.shape[1] // (2 * block)):
+            even = values[:, 2 * j * block : (2 * j + 1) * block]
+            odd = values[:, (2 * j + 1) * block : (2 * j + 2) * block]
+            own_ref[:, j * block : (j + 1) * block] = odd if own_parity else even
+            other_ref[:, j * block : (j + 1) * block] = even if own_parity else odd
+
+    @pl.when(core == 0)
+    def _():
+        put(0)
+
+    @pl.when(core != 0)
+    def _():
+        put(1)
+
+
+def split_halves(values, core, block):
+    rows, width = values.shape
+    step = 8 * block
+
+    def kernel(core_ref, value_ref, own_ref, other_ref):
+        store_halves(core_ref[0], value_ref[...], own_ref, other_ref, block)
+
+    half = jax.ShapeDtypeStruct((rows, width // 2), values.dtype)
+    out = pl.BlockSpec((rows, step // 2), lambda j: (0, j))
+    return pl.pallas_call(
+        kernel,
+        grid=(width // step,),
+        in_specs=[smem(), pl.BlockSpec((rows, step), lambda j: (0, j))],
+        out_specs=[out, out],
+        out_shape=[half, half],
+        compiler_params=vmem_params(56),
+        cost_estimate=brief(),
+        name="split_halves",
+    )(core, values)
+
+
+def down_halves(inner_hidden, merge_down, core, block):
+    rows, depth = inner_hidden.shape
+    width = merge_down.shape[1]
+    step = 4 * block
+    count = width // step
+
+    def kernel(core_ref, hidden_ref, weight_ref, own_ref, other_ref, buffers, sems):
+        copies = [
+            pltpu.make_async_copy(weight_ref.at[:, j * step : (j + 1) * step], buffers.at[j], sems.at[j])
+            for j in range(count)
+        ]
+        for copy in copies:
+            copy.start()
+        for j in range(count):
+            copies[j].wait()
+            product = jnp.dot(hidden_ref[...], buffers[j], preferred_element_type=jnp.float32)
+            place = slice(j * step // 2, (j + 1) * step // 2)
+            store_halves(
+                core_ref[0], product.astype(jnp.bfloat16), own_ref.at[:, place], other_ref.at[:, place], block
+            )
+
+    vmem = pl.BlockSpec(memory_space=pltpu.VMEM)
+    half = jax.ShapeDtypeStruct((rows, width // 2), jnp.bfloat16)
+    return pl.pallas_call(
+        kernel,
+        in_specs=[smem(), vmem, pl.BlockSpec(memory_space=pl.ANY)],
+        out_specs=[vmem, vmem],
+        out_shape=[half, half],
+        scratch_shapes=[
+            pltpu.VMEM((count, depth, step), jnp.bfloat16),
+            pltpu.SemaphoreType.DMA((count,)),
+        ],
+        compiler_params=vmem_params(56),
+        cost_estimate=brief(),
+        name="merge_down",
+    )(core, inner_hidden, merge_down)
+
+
+def project(table, own_rows, sibling_rows, visual, gain, blocks, first, count, earlier):
+    rows = own_rows.shape[0]
+    total = 2 * rows + visual.shape[0]
+    block, width = blocks[0].shape
+    quarter = width // 4
+    size = len(blocks)
+    last = first + size == count
+    flag = table.shape[0] - 1
+
+    def kernel(table_ref, own_ref, sibling_ref, visual_ref, gain_ref, *rest):
+        block_refs = rest[:size]
+        before_refs = rest[size : size + len(earlier)]
+        turned_ref, *outs, turning, sems = rest[size + len(earlier) :]
+        total_ref = outs[-1]
+        turns = []
+        for r in range(size):
+            columns = pl.ds(pl.multiple_of(table_ref[first + r] * block, block), block)
+            gains = gain_ref[:, columns]
+            part = jnp.concatenate(
+                [
+                    (ref[:, columns].astype(jnp.float32) * gains).astype(jnp.bfloat16)
+                    for ref in (own_ref, sibling_ref, visual_ref)
+                ],
+                axis=0,
+            )
+            values = block_refs[r][...]
+            product = jnp.dot(part, values, preferred_element_type=jnp.float32)
+            if r > 0:
+                total_ref[...] += product
+            elif earlier:
+                total_ref[...] = before_refs[0][...] + product
+            else:
+                total_ref[...] = product
+            turning[r] = values.T
+            turn = pltpu.make_async_copy(turning.at[r], turned_ref.at[r], sems.at[r])
+            turn.start()
+            turns.append(turn)
+        if last:
+            mine_ref, theirs_ref = outs[:2]
+
+            def put(parity):
+                for piece in range(2):
+                    start = 2 * piece * quarter
+                    mine = slice(start + parity * quarter, start + (parity + 1) * quarter)
+                    theirs = slice(start + (1 - parity) * quarter, start + (2 - parity) * quarter)
+                    place = slice(piece * quarter, (piece + 1) * quarter)
+                    mine_ref[:, place] = total_ref[:, mine]
+                    theirs_ref[:rows, place] = total_ref[rows : 2 * rows, theirs].astype(jnp.bfloat16)
+                    theirs_ref[rows : 2 * rows, place] = total_ref[:rows, theirs].astype(jnp.bfloat16)
+                    theirs_ref[2 * rows :, place] = total_ref[2 * rows :, theirs].astype(jnp.bfloat16)
+
+            @pl.when(table_ref[flag] == 0)
+            def _():
+                put(0)
+
+            @pl.when(table_ref[flag] != 0)
+            def _():
+                put(1)
+
+        for turn in turns:
+            turn.wait()
+
+    vmem = pl.BlockSpec(memory_space=pltpu.VMEM)
+    shape = jax.ShapeDtypeStruct
+    sums, scratch = [shape((total, width), jnp.float32)], []
+    if last:
+        sums = [shape((total, width // 2), jnp.float32), shape((total, width // 2), jnp.bfloat16)]
+        scratch = [pltpu.VMEM((total, width), jnp.float32)]
+    return pl.pallas_call(
+        kernel,
+        in_specs=[smem()] + [vmem] * (4 + size + len(earlier)),
+        out_specs=[pl.BlockSpec(memory_space=pl.ANY)] + [vmem] * len(sums),
+        out_shape=[shape((size, width, block), jnp.bfloat16)] + sums,
+        scratch_shapes=scratch + [pltpu.VMEM((size, width, block), jnp.bfloat16), pltpu.SemaphoreType.DMA((size,))],
+        compiler_params=vmem_params(24 if last else 56),
+        cost_estimate=brief(),
+        name="project_pairs",
+    )(table, own_rows, sibling_rows, visual, gain, *blocks, *earlier)
+
+
+def finish_pairs(mine, received, scale, codes, picking, rows):
+    total, width = mine.shape
+    slots, tokens = picking.shape
+
+    def kernel(mine_ref, received_ref, scale_ref, codes_ref, picking_ref, chip_ref, token_ref, slot_ref):
+        pairs = (mine_ref[...] + received_ref[...].astype(jnp.float32)) * scale_ref[...]
+        pairs = pairs.astype(jnp.bfloat16)
+        chip_ref[...] = pairs[: 2 * rows]
+        token_ref[...] = pairs[2 * rows :]
+        placing = picking_ref[...]
+        slot_ref[:, :width] = jnp.dot(
+            placing, pairs[2 * rows :], preferred_element_type=jnp.float32
+        ).astype(jnp.bfloat16)
+        slot_ref[:, width:] = jnp.dot(
+            placing, codes_ref[...], preferred_element_type=jnp.float32
+        ).astype(jnp.bfloat16)
+
+    shape = jax.ShapeDtypeStruct
+    return pl.pallas_call(
+        kernel,
+        out_shape=[
+            shape((2 * rows, width), jnp.bfloat16),
+            shape((tokens, width), jnp.bfloat16),
+            shape((slots, width + codes.shape[1]), jnp.bfloat16),
+        ],
+        compiler_params=vmem_params(56),
+        cost_estimate=brief(),
+        name="finish_pairs",
+    )(mine, received, scale, codes, picking)
+
+
+def sum_grads(core, pair_grad, received, returned, picking, rows):
+    width = pair_grad.shape[1]
+    tokens = picking.shape[1] // 2
+
+    def kernel(core_ref, grad_ref, returned_ref, picking_ref, *rest):
+        held_ref, sent_ref = rest[-2:]
+        text = grad_ref[...].astype(jnp.float32)
+        for ref in rest[:-2]:
+            text = text + ref[...].astype(jnp.float32)
+        text = text.astype(jnp.bfloat16)
+        held_ref[:rows] = text[:rows]
+        sent_ref[:rows] = text[rows:]
+        token = lax.dot_general(
+            picking_ref[...], returned_ref[...], (((0,), (0,)), ((), ())), preferred_element_type=jnp.float32
+        ).astype(jnp.bfloat16)
+
+        @pl.when(core_ref[0] == 0)
+        def _():
+            held_ref[rows:] = token[:tokens]
+            sent_ref[rows:] = token[tokens:]
+
+        @pl.when(core_ref[0] != 0)
+        def _():
+            held_ref[rows:] = token[tokens:]
+            sent_ref[rows:] = token[:tokens]
+
+    def whole(values):
+        return pl.BlockSpec(values.shape, lambda j: (0, 0))
+
+    half = jax.ShapeDtypeStruct((rows + tokens, width), jnp.bfloat16)
+    return pl.pallas_call(
+        kernel,
+        grid=(1,),
+        in_specs=[smem(), pl.BlockSpec((2 * rows, width), lambda j: (0, 0)), whole(returned), whole(picking)]
+        + [whole(part) for part in received],
+        out_specs=[whole(jax.ShapeDtypeStruct((rows + tokens, width), jnp.bfloat16))] * 2,
+        out_shape=[half, half],
+        compiler_params=vmem_params(56),
+        cost_estimate=brief(),
+        name="sum_grads",
+    )(core, pair_grad, returned, picking, *received)
+
+
+def project_back(table, grads, pairs, turned, text, visual, gain, scale, keep):
+    rows, width = text.shape
+    tokens = visual[0].shape[0]
+    total = rows + tokens
+    pair_width, block = turned[0][0].shape[1:]
+    quarter = pair_width // 4
+    flag = table.shape[0] - 1
+    pieces = len(turned[0])
+    count = sum(part.shape[0] for part in turned[0])
+    groups, first = [], 0
+    for piece in range(pieces):
+        size = turned[0][piece].shape[0]
+        for low in range(0, size, 4):
+            high = min(size, low + 4)
+            groups.append((piece, low, high, first + low))
+        first += size
+
+    def kernel(
+        table_ref, grad_ref, grad_other_ref, pair_ref, pair_other_ref, text_ref, visual_ref, visual_other_ref,
+        gain_ref, scale_ref, keep_ref, *rest,
+    ):
+        turned_refs, (hidden_ref, token_ref, joined, buffers, sems) = rest[: 2 * pieces], rest[2 * pieces :]
+        core = table_ref[flag]
+        copies = []
+        for at, (piece, low, high, place) in enumerate(groups):
+            copies.append(
+                [
+                    pltpu.make_async_copy(
+                        turned_refs[side * pieces + piece].at[low:high],
+                        buffers.at[side, place : place + high - low],
+                        sems.at[at, side],
+                    )
+                    for side in range(2)
+                ]
+            )
+        for pair in copies[:2]:
+            for copy in pair:
+                copy.start()
+
+        def join(parity):
+            for piece in range(2):
+                place = slice(piece * quarter, (piece + 1) * quarter)
+                start = (2 * piece + parity) * quarter
+                joined[:, start : start + quarter] = grad_ref[:, place]
+                start = (2 * piece + 1 - parity) * quarter
+                joined[:, start : start + quarter] = grad_other_ref[:, place]
+
+        @pl.when(core == 0)
+        def _():
+            join(0)
+
+        @pl.when(core != 0)
+        def _():
+            join(1)
+
+        inner = jnp.zeros((total, 1), jnp.float32)
+        for left, right in ((grad_ref, pair_ref), (grad_other_ref, pair_other_ref)):
+            inner = inner + jnp.sum(
+                left[...].astype(jnp.float32) * right[...].astype(jnp.float32), axis=1, keepdims=True
+            )
+        scales = scale_ref[...]
+        backs = inner * scales * scales * (1.0 / width)
+        keeps = keep_ref[:rows] > 0
+        for at, (piece, low, high, first) in enumerate(groups):
+            for copy in copies[at]:
+                copy.wait()
+            if at + 2 < len(groups):
+                for copy in copies[at + 2]:
+                    copy.start()
+            for r in range(first, first + high - low):
+                spot = table_ref[r]
+                inside = pl.ds(pl.multiple_of(spot * block, block), block)
+                for half, (side, token_in) in enumerate(((core, visual_ref), (1 - core, visual_other_ref))):
+                    place = pl.ds(pl.multiple_of((2 * spot + side) * block, block), block)
+                    normed_grad = jnp.dot(joined[...], buffers[half, r], preferred_element_type=jnp.float32)
+                    full = normed_grad * scales * gain_ref[:, place]
+                    hidden = full[:rows] - text_ref[:, place].astype(jnp.float32) * backs[:rows]
+                    hidden_ref[:, place] = jnp.where(keeps, hidden, 0.0).astype(jnp.bfloat16)
+                    token = full[rows:] - token_in[:, inside].astype(jnp.float32) * backs[rows:]
+                    token_ref[:, place] = token.astype(jnp.bfloat16)
+
+    vmem = pl.BlockSpec(memory_space=pltpu.VMEM)
+    shape = jax.ShapeDtypeStruct
+    return pl.pallas_call(
+        kernel,
+        in_specs=[smem()] + [vmem] * 10 + [pl.BlockSpec(memory_space=pl.ANY)] * (2 * pieces),
+        out_specs=[vmem, vmem],
+        out_shape=[shape((rows, width), jnp.bfloat16), shape((tokens, width), jnp.bfloat16)],
+        scratch_shapes=[
+            pltpu.VMEM((total, pair_width), jnp.bfloat16),
+            pltpu.VMEM((2, count, pair_width, block), jnp.bfloat16),
+            pltpu.SemaphoreType.DMA((len(groups), 2)),
+        ],
+        compiler_params=vmem_params(56),
+        cost_estimate=brief(),
+        name="project_back",
+    )(table, *grads, *pairs, text, *visual, gain, scale, keep, *turned[0], *turned[1])
+
+
+def attend_pair(queries, upstream, pair_text, pair_visual, keyed):
+    rows, width = queries[0].shape
+    length, pair_width = pair_text[0].shape[0] * len(pair_text), pair_text[0].shape[1]
+    slots = pair_visual.shape[0]
+    own_kv = pair_width // (2 * HD)
+    heads = width // HD
+    group = heads // own_kv
+    step_heads = max(1, group // 2)
+    steps = heads // step_heads
+    score_scale = HD ** (-0.5)
+    f32, bf16 = jnp.float32, jnp.bfloat16
+
+    def kernel(
+        qa, qb, ua, ub, visual_ref, row_s, row_l, pos_ref, doc_ref, qpos_ref, qdoc_ref, *rest,
+    ):
+        text_refs = rest[: len(pair_text)]
+        oa, ob, ga, gb, *grad_refs, grad_visual_ref, keep_ref, heads_ref, turned_ref, bias_ref, total_ref = rest[
+            len(pair_text) :
+        ]
+        step = pl.program_id(0)
+
+        @pl.when(step == 0)
+        def _():
+            codes = visual_ref[:, pair_width:].astype(f32).T
+            placing = jnp.where(row_s[...] == codes[0:1] * 16.0 + codes[1:2], 1.0, 0.0).astype(f32)
+            placed = jnp.dot(placing.astype(bf16), visual_ref[:, :pair_width], preferred_element_type=f32)
+            marked = jnp.max(placing, axis=1, keepdims=True)
+            keep_ref[...] = 1.0 - marked
+            texts = jnp.concatenate([ref[...].astype(f32) for ref in text_refs], axis=0)
+            pairs = jnp.where(marked > 0, placed, texts)
+            for j in range(2 * own_kv):
+                piece = pairs[:, j * HD : (j + 1) * HD]
+                heads_ref[j] = piece.astype(bf16)
+                turned_ref[j] = piece.T.astype(bf16)
+            allowed = (pos_ref[...] <= qpos_ref[...]) & (doc_ref[...] == qdoc_ref[...])
+            bias_ref[...] = jnp.where(allowed, 0.0, -jnp.inf).astype(f32)
+            total_ref[...] = jnp.zeros_like(total_ref)
+
+        head = (step * step_heads) // group
+        keys, values = heads_ref[head], heads_ref[own_kv + head]
+        keys_turned, values_turned = turned_ref[head], turned_ref[own_kv + head]
+        contract = (((1,), (1,)), ((), ()))
+        for h in range(step_heads):
+            lanes = slice(h * HD, (h + 1) * HD)
+            query = jnp.concatenate([qa[:, lanes], qb[:, lanes]], axis=0)
+            up = jnp.concatenate([ua[:, lanes], ub[:, lanes]], axis=0)
+            scores = lax.dot_general(keys, query, contract, preferred_element_type=f32)
+            scores = scores * score_scale + bias_ref[...]
+            weights = jnp.exp(scores - jnp.max(scores, axis=0, keepdims=True))
+            weights = weights * (1.0 / jnp.sum(weights, axis=0, keepdims=True))
+            light = weights.astype(bf16)
+            output = jnp.dot(values_turned, light, preferred_element_type=f32).T.astype(bf16)
+            oa[:, lanes] = output[:rows]
+            ob[:, lanes] = output[rows:]
+            total_ref[own_kv + head] += jnp.dot(light, up, preferred_element_type=f32)
+            weight_grad = lax.dot_general(values, up, contract, preferred_element_type=f32)
+            inner = jnp.sum(weights * weight_grad, axis=0, keepdims=True)
+            score_grad = (weights * (weight_grad - inner) * score_scale).astype(bf16)
+            query_grad = jnp.dot(keys_turned, score_grad, preferred_element_type=f32).T.astype(bf16)
+            ga[:, lanes] = query_grad[:rows]
+            gb[:, lanes] = query_grad[rows:]
+            total_ref[head] += jnp.dot(score_grad, query, preferred_element_type=f32)
+
+        @pl.when(step == steps - 1)
+        def _():
+            codes = visual_ref[:, pair_width : pair_width + 2].astype(f32)
+            lifting = jnp.where(codes[:, 0:1] * 16.0 + codes[:, 1:2] == row_l[...], 1.0, 0.0).astype(bf16)
+            for j in range(2 * own_kv):
+                piece = total_ref[j].astype(bf16)
+                place = slice(j * HD, (j + 1) * HD)
+                for i, ref in enumerate(grad_refs):
+                    ref[:, place] = piece[i * ref.shape[0] : (i + 1) * ref.shape[0]]
+                grad_visual_ref[:, place] = jnp.dot(lifting, piece, preferred_element_type=f32).astype(bf16)
+
+    part = pl.BlockSpec((rows, step_heads * HD), lambda j: (0, j))
+    vmem = pl.BlockSpec(memory_space=pltpu.VMEM)
+    shape = jax.ShapeDtypeStruct
+    return pl.pallas_call(
+        kernel,
+        grid=(steps,),
+        in_specs=[part] * 4 + [vmem] * (7 + len(pair_text)),
+        out_specs=[part] * 4 + [vmem] * (2 + len(pair_text)),
+        out_shape=[shape((rows, width), bf16)] * 4
+        + [shape(x.shape, bf16) for x in pair_text]
+        + [shape((slots, pair_width), bf16), shape((length, 1), f32)],
+        scratch_shapes=[
+            pltpu.VMEM((2 * own_kv, length, HD), bf16),
+            pltpu.VMEM((2 * own_kv, HD, length), bf16),
+            pltpu.VMEM((length, 2 * rows), f32),
+            pltpu.VMEM((2 * own_kv, length, HD), f32),
+        ],
+        compiler_params=vmem_params(56),
+        cost_estimate=brief(),
+        name="attend",
+    )(
+        *queries,
+        *upstream,
+        pair_visual,
+        *keyed,
+        *pair_text,
+    )
+
+
+def local_fast(
+    patches, vit_gain, merge_up, merge_down, dest, text, norm_gain, kv_weight, queries, out_grad, assign, docs
+):
+    f32, bf16 = jnp.float32, jnp.bfloat16
+    data_count, column_count = lax.axis_size("dp"), lax.axis_size("y")
+    ctx_count = 2 * column_count
+    data, column, core = lax.axis_index("dp"), lax.axis_index("y"), lax.axis_index("core")
+    rows, width = text.shape[1], text.shape[2]
+    tokens = dest.shape[0]
+    block = kv_weight.shape[0]
+    length = rows * ctx_count
+    core_word = core[None].astype(jnp.int32)
+
+    def line(values, pairs):
+        return lax.ppermute(values, "dp", [(2 * p + low, 2 * q + low) for p, q in pairs for low in range(2)])
+
+    def both(values):
+        return neighbor(values, "dp", 1), neighbor(values, "y", 1)
+
+    close = lax.optimization_barrier
+    swapped = [(0, 1), (1, 0), (2, 3), (3, 2)]
+    middle, outward = [(1, 2), (2, 1)], [(1, 0), (2, 3)]
+    far_index = data // 2
+    is_middle = (far_index == 1) | (far_index == 2)
+    hops = [0, 1, jnp.where(is_middle, 3, 2), jnp.where(is_middle, 2, 3)]
+    owners = [
+        ((far_index ^ hops[i + j]) * 2 + ((data % 2) ^ along)) * column_count + (column ^ down)
+        for i in (0, 2)
+        for along, down in ((0, 0), (1, 0), (0, 1), (1, 1))
+        for j in range(2)
+    ]
+    table = jnp.stack(owners + [core]).astype(jnp.int32)
+    gain = lax.dynamic_index_in_dim(
+        norm_gain.reshape(-1, 2, block), core, axis=1, keepdims=False
+    ).reshape(1, width // 2)
+    query_width = queries.shape[2] // 2
+    chip_tokens = 2 * tokens
+
+    beside0, below0 = both(kv_weight)
+    far1, across = line(kv_weight, swapped), line(kv_weight, middle)
+    vectors = []
+    for j in range(patches.shape[1] // vit_gain.shape[0]):
+        piece = lax.slice_in_dim(patches, j * vit_gain.shape[0], (j + 1) * vit_gain.shape[0], axis=1)
+        center = piece.astype(f32)
+        center = center - jnp.mean(center, axis=-1, keepdims=True)
+        spread = jnp.mean(center * center, axis=-1, keepdims=True)
+        vectors.append((center * lax.rsqrt(spread + epsilon) * vit_gain).astype(bf16))
+    normed = jnp.concatenate(vectors, axis=1)
+    inner_hidden = jax.nn.gelu(
+        jnp.dot(normed, merge_up, preferred_element_type=f32), approximate=False
+    ).astype(bf16)
+    rows_in = text[0]
+    beside0, below0, far1, across, inner_hidden, rows_in, core_word, table, gain = close(
+        (beside0, below0, far1, across, inner_hidden, rows_in, core_word, table, gain)
+    )
+
+    beside1, below1 = both(far1)
+    across2, ends1 = line(far1, middle), line(across, outward)
+    merged, merged_other = down_halves(inner_hidden, merge_down, core_word, block)
+    beside1, below1, across2, ends1, merged, merged_other, rows_in, core_word = close(
+        (beside1, below1, across2, ends1, merged, merged_other, rows_in, core_word)
+    )
+
+    corner0, corner1 = neighbor(beside0, "y", 1), neighbor(below1, "dp", 1)
+    ends2 = line(across2, outward)
+    arriving = swap(merged_other)
+    own_rows, other_part = split_halves(rows_in, core_word, block)
+    sibling_rows = swap(other_part)
+    far2 = jnp.where(is_middle, across, ends1)
+    merged = (merged.astype(f32) + arriving.astype(f32)).astype(bf16)
+    visual32 = lax.dynamic_slice_in_dim(merged, column * chip_tokens, chip_tokens, 0)
+    leaving = lax.dynamic_slice_in_dim(merged, (column ^ 1) * chip_tokens, chip_tokens, 0)
+    summing = neighbor(leaving, "y", 1)
+    query_in, upstream_in = queries[0], out_grad[0]
+    corner0, corner1, ends2, own_rows, sibling_rows, far2, visual32, summing = close(
+        (corner0, corner1, ends2, own_rows, sibling_rows, far2, visual32, summing)
+    )
+    query_in, upstream_in, dest, assign, docs, ends2 = close((query_in, upstream_in, dest, assign, docs, ends2))
+
+    def heads_of(values):
+        mine = lax.dynamic_slice_in_dim(values, core * query_width, query_width, 1)
+        theirs = lax.dynamic_slice_in_dim(values, (1 - core) * query_width, query_width, 1)
+        return mine, theirs
+
+    beside2, below2 = both(far2)
+    far3 = jnp.where(is_middle, across2, ends2)
+    query_parts, upstream_parts = heads_of(query_in), heads_of(upstream_in)
+    query_parts = (query_parts[0], swap(query_parts[1]))
+    upstream_parts = (upstream_parts[0], swap(upstream_parts[1]))
+
+    def squares(values):
+        values = values.astype(f32)
+        return jnp.sum(values * values, axis=1)
+
+    own_squares, sibling_squares = squares(own_rows), squares(sibling_rows)
+
+    dest_other = swap(dest)
+    chip_dest = jnp.where(
+        core == 0, jnp.concatenate([dest, dest_other]), jnp.concatenate([dest_other, dest])
+    )
+    token_core = jnp.arange(chip_tokens, dtype=jnp.int32) // tokens
+    sequence, row_of = chip_dest // length, chip_dest % length
+    slot = token_core * ctx_count + row_of // rows
+    slot_total = data_count * column_count * 2 * ctx_count
+    slot_index = jnp.arange(slot_total, dtype=jnp.int32)[:, None]
+    picking = (slot_index // (column_count * 2 * ctx_count) == sequence[None, :]) & (
+        slot_index % (2 * ctx_count) == slot[None, :]
+    )
+    picking = picking.astype(bf16)
+    lane = jnp.arange(128, dtype=jnp.int32)[None, :]
+    code = row_of[:, None] + 1
+    codes = jnp.where(lane == 0, code // 16, jnp.where(lane == 1, code % 16, 0)).astype(bf16)
+
+    def between_chips(values):
+        shaped = values.reshape(data_count * column_count, 2 * ctx_count, -1)
+        moved = lax.all_to_all(shaped, ("dp", "y"), split_axis=0, concat_axis=0, tiled=True)
+        return moved.reshape(values.shape)
+
+    halves = rows // 2
+    positions = (assign[:, None] * halves + jnp.arange(halves, dtype=jnp.int32)[None, :]).reshape(length)
+    labels = docs[0].reshape(-1, halves)[assign].reshape(length)
+    order = jnp.stack(
+        [2 * (column ^ down) + (core ^ side) for down in range(column_count) for side in range(2)]
+    )
+    key_row = (order[:, None] * rows + jnp.arange(rows, dtype=jnp.int32)[None, :]).reshape(length)
+    key_pos = positions.reshape(ctx_count, rows)[order].reshape(length)
+    key_doc = labels.reshape(ctx_count, rows)[order].reshape(length)
+    key_row = key_row.astype(f32) + 1.0
+    keyed = (key_row[:, None], key_row[None, :], key_pos[:, None], key_doc[:, None])
+    keyed += (key_pos[None, : 2 * rows], key_doc[None, : 2 * rows])
+
+    def of_core(values, which):
+        return lax.dynamic_slice_in_dim(values, which * tokens, tokens, 0)
+
+    beside2, below2, far3, summing, query_parts, upstream_parts, keyed, picking, codes, own_squares, sibling_squares = close(
+        (beside2, below2, far3, summing, query_parts, upstream_parts, keyed, picking, codes, own_squares, sibling_squares)
+    )
+
+    beside3, below3 = both(far3)
+    visual = (visual32.astype(f32) + summing.astype(f32)).astype(bf16)
+    blocks = [kv_weight, far1, beside0, beside1, below0, below1, corner0, corner1]
+    part0, sums = project(table, own_rows, sibling_rows, visual, gain, blocks, 0, 16, ())
+    beside3, below3, part0, sums, visual = close((beside3, below3, part0, sums, visual))
+
+    corner2, corner3 = neighbor(beside2, "y", 1), neighbor(below3, "dp", 1)
+    other0 = swap(part0)
+    blocks = [far2, far3, beside2, beside3, below2, below3]
+    part1, sums = project(table, own_rows, sibling_rows, visual, gain, blocks, 8, 16, (sums,))
+    visual_squares = squares(visual)
+    arrived = swap(jnp.concatenate([sibling_squares, own_squares, visual_squares]))
+    square = jnp.concatenate([own_squares, sibling_squares, visual_squares]) + arrived
+    scale = lax.rsqrt(square / width + epsilon)[:, None]
+    own_visual, other_visual = of_core(visual, core), swap(of_core(visual, 1 - core))
+    own_scale = jnp.concatenate([scale[:rows], of_core(scale[2 * rows :], core)], axis=0)
+    corner2, corner3, part1, sums, other0, scale, own_visual, other_visual, own_scale = close(
+        (corner2, corner3, part1, sums, other0, scale, own_visual, other_visual, own_scale)
+    )
+    part2, *sums = project(table, own_rows, sibling_rows, visual, gain, [corner2, corner3], 14, 16, (sums,))
+    turned, turned_other = [part0, part1, part2], [other0]
+    mine, theirs = sums
+    received = swap(theirs)
+    pair_chip, pair_tokens, leaving = finish_pairs(mine, received, scale, codes, picking, rows)
+    pair_text = [pair_chip] + [neighbor(pair_chip, "y", down) for down in range(1, column_count)]
+    pair_visual = between_chips(leaving)
+    turned_other += [swap(after(part, (received,))) for part in turned[1:]]
+
+    own_pairs = jnp.concatenate([pair_chip[:rows], of_core(pair_tokens, core)], axis=0)
+    other_pairs = swap(jnp.concatenate([pair_chip[rows:], of_core(pair_tokens, 1 - core)], axis=0))
+
+    out_a, out_b, grad_a, grad_b, pair_grad, *far_grads, visual_pair_grad, keep = attend_pair(
+        query_parts, upstream_parts, pair_text, pair_visual, keyed
+    )
+
+    def heads_back(held, leaving):
+        arrived = swap(leaving)
+        return jnp.where(
+            core == 0, jnp.concatenate([held, arrived], axis=1), jnp.concatenate([arrived, held], axis=1)
+        )
+
+    received = [neighbor(part, "y", down) for down, part in enumerate(far_grads, 1)]
+    returned = between_chips(after(visual_pair_grad, turned_other))
+    attention, query_grad = heads_back(out_a, out_b), heads_back(grad_a, grad_b)
+    pair_grad, attention, query_grad = close((pair_grad, attention, query_grad))
+    held, leaving = sum_grads(core_word, pair_grad, received, returned, picking, rows)
+    hidden_grad, visual_grad = project_back(
+        table, (held, swap(leaving)), (own_pairs, other_pairs), (turned, turned_other), text[0],
+        (own_visual, other_visual), norm_gain[None, :], own_scale, keep,
+    )
+    return (attention[None], query_grad[None], hidden_grad[None], visual_grad)
+
+
 def solution(mesh):
-    placed = (
-        P("dp", None),
-        P(),
-        P(None, "ctx"),
-        P("ctx", None),
-        P(("dp", "ctx")),
-        P("dp", "ctx", None),
-        P(),
-        P(("dp", "ctx"), None),
-        P("dp", "ctx", None),
-        P("dp", "ctx", None),
-        P(),
-        P("dp", None),
-    )
-    return jax.shard_map(
-        local,
-        mesh=mesh,
-        in_specs=placed,
-        out_specs=(
-            P("dp", "ctx", None),
-            P("dp", "ctx", None),
-            P("dp", "ctx", None),
-            P(("dp", "ctx"), None),
-        ),
-        check_vma=False,
-    )
+    data_count, ctx_count = mesh.shape["dp"], mesh.shape["ctx"]
+    split = Mesh(mesh.devices.reshape(data_count, -1, 2), ("dp", "y", "core"))
+
+    def call(*arrays):
+        text, kv_weight, dest = arrays[5], arrays[7], arrays[4]
+        devices = data_count * ctx_count
+        rows = text.shape[1] // ctx_count
+        fits = (
+            ctx_count == 4
+            and data_count == 8
+            and (kv_weight.shape[0] // devices) % 128 == 0
+            and dest.shape[0] // devices <= devices
+            and rows % 128 == 0
+        )
+        if fits:
+            whole, ctx, body, used = ("dp", "y", "core"), ("y", "core"), local_fast, split
+        else:
+            whole, ctx, body, used = ("dp", "ctx"), "ctx", local, mesh
+        placed = (
+            P("dp", None),
+            P(),
+            P(None, ctx),
+            P(ctx, None),
+            P(whole),
+            P("dp", ctx, None),
+            P(),
+            P(whole, None),
+            P("dp", ctx, None),
+            P("dp", ctx, None),
+            P(),
+            P("dp", None),
+        )
+        return jax.shard_map(
+            body,
+            mesh=used,
+            in_specs=placed,
+            out_specs=(P("dp", ctx, None), P("dp", ctx, None), P("dp", ctx, None), P(whole, None)),
+            check_vma=False,
+        )(*arrays)
+
+    return call

time: 299 us -> 190 us (0.64)
  waiting for transfers between devices: 135 us -> 43.7 us
  matrix products: 97.2 us -> 6.2 us
  Pallas kernels: 0 us -> 59.5 us
  starting transfers between devices: 16.9 us -> 40.4 us
  between operations: 15.5 us -> 1.55 us
  other arithmetic: 11 us -> 18 us
  local copies, waits for them, and re-layouts: 23.3 us -> 19.7 us
    dot_general x12 -> x1, matrix products: 90.1 us -> 6.2 us  [local_fast(): jnp.dot(normed, merge_up, preferred_element_type=f32)]
    all_gather x2 -> x0, waiting for transfers between devices: 64.7 us -> none  [the longest x1 54.1 us: local(): lax.all_gather(kv_weight, ('dp', 'ctx'), axis=0, tiled=True)]
    pallas_call x0 -> x9, Pallas kernels: none -> 59.5 us  [the longest x1 18.9 us: attend_pair(): pl.pallas_call(kernel, grid=(steps,), in_specs=[part] * 4 + [vmem] * (7 +...]
    ppermute x0 -> x35, waiting for transfers between devices: none -> 37.1 us  [the longest x30 27.7 us: neighbor(): return lax.ppermute(values, axis, [(d, d ^ offset) for d in range(count)])]
    all_to_all x3 -> x2, waiting for transfers between devices: 37.2 us -> 6.56 us  [between_chips(): lax.all_to_all(shaped, ('dp', 'y'), split_axis=0, concat_axis=0, tiled=True)]
    ppermute x0 -> x35, starting transfers between devices: none -> 26.9 us  [the longest x30 19 us: neighbor(): return lax.ppermute(values, axis, [(d, d ^ offset) for d in range(count)])]
    reduce_scatter x1 -> x0, waiting for transfers between devices: 25.4 us -> none  [local(): lax.psum_scatter(jnp.dot(inner_hidden, merge_down, preferred_element_type...]
    unnamed x27 -> x88, local copies, waits for them, and re-layouts: 13 us -> 5.12 us
  transfers between devices with their start and end apart: 8 -> 37, of which waited for: 6 -> 16; matrix products, arithmetic and copies ran while one was open for 20% -> 21% of each run, Pallas kernels for 0% -> 25%
where the time goes in v2:
time: 190 us; the launch traced here: 189 us
  Pallas kernels  59.5 us (31%)
  waiting for transfers between devices  43.7 us (23%)
  starting transfers between devices  40.4 us (21%)
  local copies, waits for them, and re-layouts  19.7 us (10%)
  other arithmetic  18 us (9%)
  matrix products  6.2 us (3%)
    ppermute x30, waiting for transfers between devices, neighbor(): return lax.ppermute(values, axis, [(d, d ^ offset) for d in range(count)])  27.7 us
    ppermute x30, starting transfers between devices, neighbor(): return lax.ppermute(values, axis, [(d, d ^ offset) for d in range(count)])  19 us
    pallas_call x1, Pallas kernels, attend_pair(): pl.pallas_call(kernel, grid=(steps,), in_specs=[part] * 4 + [vmem] * (7 +...  18.9 us
    pallas_call x3, Pallas kernels, project(): pl.pallas_call(kernel, in_specs=[smem()] + [vmem] * (4 + size + len(earli...  14.2 us
    all_to_all x2, starting transfers between devices, between_chips(): lax.all_to_all(shaped, ('dp', 'y'), split_axis=0, concat_axis=0, tiled=True)  13.5 us
    pallas_call x1, Pallas kernels, project_back(): pl.pallas_call(kernel, in_specs=[smem()] + [vmem] * 10 + [pl.BlockSpec(me...  10.7 us
    ppermute x5, waiting for transfers between devices, line(): lax.ppermute(values, 'dp', [(2 * p + low, 2 * q + low) for p, q in pairs...  9.47 us
    ppermute x5, starting transfers between devices, line(): lax.ppermute(values, 'dp', [(2 * p + low, 2 * q + low) for p, q in pairs...  7.97 us
  transfers between devices with their start and end apart: 37, of which 16 were waited for; matrix products, arithmetic and copies ran while one was open for 21% of the time, Pallas kernels for 25%

profile of v2, /device:TPU:0, one launch (start us, length us, event | category | flops | bytes accessed | tf_op | source)
XLA Modules:
  0.0 189.0 jit_solution(6003578583126521567)
XLA Ops:
  0.7 3.1 %collective-permute-start.2 = (bf16[256,1024]{1,0:T(8,128)(2,1)}, bf16[256,1024]{1,0:T(8,128)(2,1)S(1)}, u32[]{:S(2)}, u32[]{:S(2)}) collective-permute-start(bf16[256,1024]{1,0:T(8,128)(2,1)} %rest_0_.1), channel_id=1, source_target_pairs={{0,8},{4,12},{8,0},{12,4},{16,24},{20,28},{24,16},{28,20},{1,9},{5... | collective-permute-start | bytes 1572872 | tf_op jit(solution)/shard_map/ppermute | solution.py:649
  3.8 1.5 collective-permute-start.1
  5.3 1.5 collective-permute-start
  7.5 1.5 convert_reduce_fusion.3
  10.3 1.3 fusion.27
  11.6 0.7 stack.93.table_ref
  12.3 6.2 %fusion.30.hidden_ref = bf16[128,768]{1,0:T(8,128)(2,1)} fusion(bf16[5120,768]{1,0:T(8,128)(2,1)} %param.14, bf16[128,1280]{1,0:T(8,128)(2,1)} %get-tuple-element.209, bf16[128,1280]{1,0:T(8,128)(2,1)} %get-tuple-element.208, bf16[128,1280]{1,0:T(8,128)(2,1)} %get-tuple-element.207, bf16[128,1280]{1,0:T(8,128)(2,1)S(1)} %get-tuple-element.206), kind=kOutput, calls=%fused_computation.51 | convolution fusion | flops 1018265600 | bytes 9371648 | tf_op jit(solution)/shard_map/dot_general | solution.py:684
  18.7 1.3 collective-permute-start.8
  20.0 1.5 collective-permute-start.7
  21.9 1.5 collective-permute-start.5
  23.4 7.5 %merge_down.1 = (bf16[128,4096]{1,0:T(8,128)(2,1)}, bf16[128,4096]{1,0:T(8,128)(2,1)}) custom-call(s32[1]{0:T(128)} %bitcast.1.core_ref, bf16[128,768]{1,0:T(8,128)(2,1)} %fusion.30.hidden_ref, bf16[768,8192]{1,0:T(8,128)(2,1)} %weight_ref.1), custom_call_target="tpu_custom_call" | custom-call | flops 1 | bytes 1 | tf_op jit(solution)/shard_map/merge_down/pallas_call | solution.py:264
  30.9 4.1 %collective-permute-done.8 = bf16[256,1024]{1,0:T(8,128)(2,1)S(1)} collective-permute-done((bf16[256,1024]{1,0:T(8,128)(2,1)S(1)}, bf16[256,1024]{1,0:T(8,128)(2,1)S(1)}, u32[]{:S(2)}, u32[]{:S(2)}) %collective-permute-start.8) | collective-permute-done | bytes 524320 | tf_op jit(solution)/shard_map/ppermute | solution.py:649
  35.2 0.8 collective-permute-start.4
  36.1 1.0 collective-permute-start.9
  37.0 1.5 collective-permute-start.10
  38.5 3.9 %split_halves.1 = (bf16[128,4096]{1,0:T(8,128)(2,1)}, bf16[128,4096]{1,0:T(8,128)(2,1)}) custom-call(s32[1]{0:T(128)} %bitcast.1.core_ref, bf16[128,8192]{1,0:T(8,128)(2,1)} %bitcast.53), custom_call_target="tpu_custom_call" | custom-call | flops 1 | bytes 1 | tf_op jit(solution)/shard_map/split_halves/pallas_call | solution.py:229
  42.5 1.5 add_convert_fusion
  44.0 0.9 constant_dynamic-slice_fusion.8
  44.9 0.8 collective-permute-start.13
  45.9 1.1 broadcast_select_fusion.1.rest_0_
  47.1 3.3 %collective-permute-done.4.rest_6_ = bf16[256,1024]{1,0:T(8,128)(2,1)} collective-permute-done((bf16[256,1024]{1,0:T(8,128)(2,1)}, bf16[256,1024]{1,0:T(8,128)(2,1)}, u32[]{:S(2)}, u32[]{:S(2)}) %collective-permute-start.4) | collective-permute-done | bytes 524320 | tf_op jit(solution)/shard_map/ppermute | solution.py:180
  50.4 5.4 %collective-permute-done.10 = bf16[256,1024]{1,0:T(8,128)(2,1)} collective-permute-done((bf16[256,1024]{1,0:T(8,128)(2,1)}, bf16[256,1024]{1,0:T(8,128)(2,1)}, u32[]{:S(2)}, u32[]{:S(2)}) %collective-permute-start.10) | collective-permute-done | bytes 524320 | tf_op jit(solution)/shard_map/ppermute | solution.py:649
  55.8 5.3 %collective-permute-done.13 = bf16[64,4096]{1,0:T(8,128)(2,1)} collective-permute-done((bf16[64,4096]{1,0:T(8,128)(2,1)}, bf16[64,4096]{1,0:T(8,128)(2,1)}, u32[]{:S(2)}, u32[]{:S(2)}) %collective-permute-start.13) | collective-permute-done | bytes 524320 | tf_op jit(solution)/shard_map/ppermute | solution.py:180
  61.2 0.8 collective-permute-start.15
  61.9 1.0 collective-permute-start.14
  62.9 1.9 %broadcast_select_fusion.rest_1_ = bf16[256,1024]{1,0:T(8,128)(2,1)} fusion(bf16[256,1024]{1,0:T(8,128)(2,1)} %collective-permute-done.7, bf16[256,1024]{1,0:T(8,128)(2,1)} %collective-permute-done.10, pred[]{:T(512)S(6)} %or.3), kind=kLoop, calls=%fused_computation.47 | loop fusion | flops 262144 | bytes 1572865 | tf_op jit(solution)/shard_map/jit(_where)/select_n | solution.py:720
  69.9 2.1 %constant_dynamic-slice_fusion.6 = (bf16[128,2048]{1,0:T(8,128)(2,1)S(1)}, bf16[128,2048]{1,0:T(8,128)(2,1)}) fusion(bf16[128,4096]{1,0:T(8,128)(2,1)} %bitcast.57, s32[]{:T(128)S(6)} %select_n.236, s32[]{:T(128)S(6)} %select_n.235), kind=kLoop, calls=%fused_computation.81 | loop fusion | bytes 2097160 | tf_op jit(solution)/shard_map/dynamic_slice | solution.py:716
  72.5 0.9 constant_dynamic-slice_fusion.4
  74.2 0.7 and_convert_fusion.picking_ref
  75.3 0.8 copy-done.24
  76.1 1.2 collective-permute-start.20
  77.3 0.7 collective-permute-start.19
  78.0 2.0 %add_convert_fusion.1.visual_ref = bf16[64,4096]{1,0:T(8,128)(2,1)} fusion(bf16[64,4096]{1,0:T(8,128)(2,1)} %collective-permute-done.13, bf16[64,4096]{1,0:T(8,128)(2,1)S(1)} %get-tuple-element.133), kind=kLoop, calls=%fused_computation.17 | loop fusion | flops 1048576 | bytes 1572864 | tf_op jit(solution)/shard_map/convert_element_type | solution.py:774
  80.0 6.6 %project_pairs.3 = (bf16[8,1024,256]{2,1,0:T(8,128)(2,1)}, f32[320,1024]{1,0:T(8,128)}) custom-call(s32[17]{0:T(128)} %stack.93.table_ref, bf16[128,4096]{1,0:T(8,128)(2,1)} %get-tuple-element.125.own_ref, bf16[128,4096]{1,0:T(8,128)(2,1)} %copy-done.4, bf16[64,4096]{1,0:T(8,128)(2,1)} %add_convert_fusion.1.visual_ref, f32[1,4096]{1,0:T(1,128)} %bitcast.50, ...), custom_call_target="tpu_custom_call" | custom-call | flops 1 | bytes 1 | tf_op jit(solution)/shard_map/project_pairs/pallas_call | solution.py:347
  86.6 3.7 %collective-permute-done.20.rest_5_ = bf16[256,1024]{1,0:T(8,128)(2,1)S(1)} collective-permute-done((bf16[256,1024]{1,0:T(8,128)(2,1)}, bf16[256,1024]{1,0:T(8,128)(2,1)S(1)}, u32[]{:S(2)}, u32[]{:S(2)}) %collective-permute-start.20) | collective-permute-done | bytes 524320 | tf_op jit(solution)/shard_map/ppermute | solution.py:180
  90.8 1.2 collective-permute-start.21
  92.5 0.7 constant_dynamic-slice_fusion.2
  93.6 1.1 collective-permute-start.22
  94.7 6.3 %project_pairs.4 = (bf16[6,1024,256]{2,1,0:T(8,128)(2,1)}, f32[320,1024]{1,0:T(8,128)}) custom-call(s32[17]{0:T(128)} %stack.93.table_ref, bf16[128,4096]{1,0:T(8,128)(2,1)} %get-tuple-element.125.own_ref, bf16[128,4096]{1,0:T(8,128)(2,1)} %copy-done.4, bf16[64,4096]{1,0:T(8,128)(2,1)} %add_convert_fusion.1.visual_ref, f32[1,4096]{1,0:T(1,128)} %bitcast.51, ...), custom_call_target="tpu_custom_call" | custom-call | flops 1 | bytes 1 | tf_op jit(solution)/shard_map/project_pairs/pallas_call | solution.py:347
  101.2 4.2 %collective-permute-done.21.rest_0_ = bf16[256,1024]{1,0:T(8,128)(2,1)S(1)} collective-permute-done((bf16[256,1024]{1,0:T(8,128)(2,1)}, bf16[256,1024]{1,0:T(8,128)(2,1)S(1)}, u32[]{:S(2)}, u32[]{:S(2)}) %collective-permute-start.21) | collective-permute-done | bytes 524320 | tf_op jit(solution)/shard_map/ppermute | solution.py:180
  105.3 2.4 %collective-permute-done.22.rest_1_ = bf16[256,1024]{1,0:T(8,128)(2,1)S(1)} collective-permute-done((bf16[256,1024]{1,0:T(8,128)(2,1)S(1)}, bf16[256,1024]{1,0:T(8,128)(2,1)S(1)}, u32[]{:S(2)}, u32[]{:S(2)}) %collective-permute-start.22) | collective-permute-done | bytes 524320 | tf_op jit(solution)/shard_map/ppermute | solution.py:180
  107.7 1.3 copy-done.6
  109.1 1.4 project_pairs.5
  110.5 0.8 copy-done.8
  111.3 1.6 collective-permute-done.26.received_ref
  113.1 0.8 copy.24.scale_ref
  113.9 2.2 %finish_pairs.1 = (bf16[256,512]{1,0:T(8,128)(2,1)}, bf16[64,512]{1,0:T(8,128)(2,1)}, bf16[128,640]{1,0:T(8,128)(2,1)}) custom-call(f32[320,512]{1,0:T(8,128)} %copy-done.8, bf16[320,512]{1,0:T(8,128)(2,1)} %copy-done.29, f32[320,1]{1,0:T(8,128)} %copy.24.scale_ref, bf16[64,128]{1,0:T(8,128)(2,1)} %select_convert_fusion.codes_ref, ...), custom_call_target="tpu_custom_call" | custom-call | flops 1 | bytes 1 | tf_op jit(solution)/shard_map/finish_pairs/pallas_call | solution.py:377
  116.1 7.7 %all-to-all-start = ((bf16[16,8,640]{2,1,0:T(8,128)(2,1)}), bf16[16,8,640]{2,1,0:T(8,128)(2,1)S(1)}, u32[]{:S(2)}, u32[]{:S(2)}) async-start(bf16[16,8,640]{2,1,0:T(8,128)(2,1)} %bitcast.61), calls=%async_computation | async-start | bytes 327680 | tf_op jit(solution)/shard_map/all_to_all | solution.py:750
  123.8 2.0 %collective-permute-start.27 = (bf16[256,512]{1,0:T(8,128)(2,1)}, bf16[256,512]{1,0:T(8,128)(2,1)S(1)}, u32[]{:S(2)}, u32[]{:S(2)}) collective-permute-start(bf16[256,512]{1,0:T(8,128)(2,1)} %get-tuple-element.168.rest_0_), channel_id=1, source_target_pairs={{0,2},{2,0},{1,3},{3,1},{4,6},{6,4},{5,7},{7,5},{8,10},{10,8},{9,1... | collective-permute-start | bytes 786440 | tf_op jit(solution)/shard_map/ppermute | solution.py:180
  125.8 0.8 copy.25.row_s
  126.6 0.8 copy.26.pos_ref
  127.5 0.9 copy.27.doc_ref
  128.3 5.7 %collective-permute-done.27.rest_1_ = bf16[256,512]{1,0:T(8,128)(2,1)S(1)} collective-permute-done((bf16[256,512]{1,0:T(8,128)(2,1)}, bf16[256,512]{1,0:T(8,128)(2,1)S(1)}, u32[]{:S(2)}, u32[]{:S(2)}) %collective-permute-start.27) | collective-permute-done | bytes 262176 | tf_op jit(solution)/shard_map/ppermute | solution.py:180
  134.0 0.7 copy-done.32
  134.7 18.9 %attend.1 = (bf16[128,2048]{1,0:T(8,128)(2,1)}, bf16[128,2048]{1,0:T(8,128)(2,1)}, bf16[128,2048]{1,0:T(8,128)(2,1)}, bf16[128,2048]{1,0:T(8,128)(2,1)}, bf16[25...) custom-call(bf16[128,2048]{1,0:T(8,128)(2,1)} %get-tuple-element.127.qa, ...), custom_call_target="tpu_custom_call" | custom-call | flops 1 | bytes 1 | tf_op jit(solution)/shard_map/attend/pallas_call | solution.py:609
  155.8 1.3 collective-permute-start.32
  157.2 2.4 %maximum_select_fusion = bf16[128,4096]{1,0:T(8,128)(2,1)} fusion(bf16[128,2048]{1,0:T(8,128)(2,1)S(1)} %collective-permute-done.28, bf16[128,2048]{1,0:T(8,128)(2,1)} %get-tuple-element.170, pred[]{:T(512)S(6)} %eq.81), kind=kLoop, calls=%fused_computation.14 | loop fusion | flops 4718592 | bytes 2097153 | tf_op jit(solution)/shard_map/jit(_where)/select_n | solution.py:810
  159.6 5.7 %all-to-all-start.1 = ((bf16[16,8,512]{2,1,0:T(8,128)(2,1)}), bf16[16,8,512]{2,1,0:T(8,128)(2,1)S(1)}, u32[]{:S(2)}, u32[]{:S(2)}) async-start(bf16[16,8,512]{2,1,0:T(8,128)(2,1)} %bitcast.63), calls=%async_computation.1 | async-start | bytes 262144 | tf_op jit(solution)/shard_map/all_to_all | solution.py:750
  165.4 1.2 maximum_select_fusion.1
  166.6 6.6 %all-to-all-done.1 = bf16[16,8,512]{2,1,0:T(8,128)(2,1)S(1)} async-done(((bf16[16,8,512]{2,1,0:T(8,128)(2,1)}), bf16[16,8,512]{2,1,0:T(8,128)(2,1)S(1)}, u32[]{:S(2)}, u32[]{:S(2)}) %all-to-all-start.1) | async-done | bytes 131104 | tf_op jit(solution)/shard_map/all_to_all | solution.py:750
  173.8 2.1 %sum_grads.1 = (bf16[160,512]{1,0:T(8,128)(2,1)}, bf16[160,512]{1,0:T(8,128)(2,1)}) custom-call(s32[1]{0:T(128)} %bitcast.1.core_ref, bf16[256,512]{1,0:T(8,128)(2,1)} %get-tuple-element.176.grad_ref, bf16[128,512]{1,0:T(8,128)(2,1)} %bitcast.60, bf16[128,64]{1,0:T(8,128)(2,1)} %and_convert_fusion.picking_ref, bf16[256,512]{1,0:T(8,128)(2,1)} %copy-done.31), custom_call_target="tpu_custom_call" | custom-call | flops 1 | bytes 1 | tf_op jit(solution)/shard_map/sum_grads/pallas_call | solution.py:420
  175.9 0.7 copy.28.scale_ref
  176.6 0.7 pad_maximum_fusion.pair_ref
  178.1 10.7 %project_back.1 = (bf16[128,8192]{1,0:T(8,128)(2,1)}, bf16[32,8192]{1,0:T(8,128)(2,1)}) custom-call(s32[17]{0:T(128)} %stack.93.table_ref, bf16[160,512]{1,0:T(8,128)(2,1)} %get-tuple-element.185.grad_ref, bf16[160,512]{1,0:T(8,128)(2,1)} %copy-done.33, bf16[160,512]{1,0:T(8,128)(2,1)} %pad_maximum_fusion.pair_ref, ...), custom_call_target="tpu_custom_call" | custom-call | flops 1 | bytes 1 | tf_op jit(solution)/shard_map/project_back/pallas_call | solution.py:516
  (178 shorter events, 15.3 us)
Async XLA Ops:
  0.6 8.4 %copy-start.11 = (bf16[128,5120]{1,0:T(8,128)(2,1)S(1)}, bf16[128,5120]{1,0:T(8,128)(2,1)}, u32[]{:S(2)}) copy-start(bf16[128,5120]{1,0:T(8,128)(2,1)} %param.12) | copy-start | bytes 3932164
  0.6 9.0 %copy-start.34 = (f32[8192]{0:T(1024)S(1)}, f32[8192]{0:T(1024)}, u32[]{:S(2)}) copy-start(f32[8192]{0:T(1024)} %param.18) | copy-start | bytes 98308
  0.7 9.6 %copy-start.38 = (f32[1280]{0:T(1024)S(1)}, f32[1280]{0:T(1024)}, u32[]{:S(2)}) copy-start(f32[1280]{0:T(1024)} %param.13) | copy-start | bytes 15364
  0.7 17.9 %collective-permute-start.2 = (bf16[256,1024]{1,0:T(8,128)(2,1)}, bf16[256,1024]{1,0:T(8,128)(2,1)S(1)}, u32[]{:S(2)}, u32[]{:S(2)}) collective-permute-start(bf16[256,1024]{1,0:T(8,128)(2,1)} %rest_0_.1), channel_id=1, source_target_pairs={{0,8},{4,12},{8,0},{12,4},{16,24},{20,28},{24,16},{28,20},{1,9},{5... | collective-permute-start | bytes 1572872 | tf_op jit(solution)/shard_map/ppermute | solution.py:649
  3.8 14.8 %collective-permute-start.1 = (bf16[256,1024]{1,0:T(8,128)(2,1)}, bf16[256,1024]{1,0:T(8,128)(2,1)S(1)}, u32[]{:S(2)}, u32[]{:S(2)}) collective-permute-start(bf16[256,1024]{1,0:T(8,128)(2,1)} %rest_0_.1), channel_id=1, source_target_pairs={{0,2},{2,0},{1,3},{3,1},{4,6},{6,4},{5,7},{7,5},{8,10},{10,8},{9,1... | collective-permute-start | bytes 1572872 | tf_op jit(solution)/shard_map/ppermute | solution.py:180
  5.3 13.4 %collective-permute-start = (bf16[256,1024]{1,0:T(8,128)(2,1)}, bf16[256,1024]{1,0:T(8,128)(2,1)}, u32[]{:S(2)}, u32[]{:S(2)}) collective-permute-start(bf16[256,1024]{1,0:T(8,128)(2,1)} %rest_0_.1), channel_id=1, source_target_pairs={{0,4},{4,0},{8,12},{12,8},{16,20},{20,16},{24,28},{28,24},{1,5},{5... | collective-permute-start | bytes 1572872 | tf_op jit(solution)/shard_map/ppermute | solution.py:180
  6.8 11.9 %collective-permute-start.3 = (bf16[256,1024]{1,0:T(8,128)(2,1)}, bf16[256,1024]{1,0:T(8,128)(2,1)S(1)}, u32[]{:S(2)}, u32[]{:S(2)}) collective-permute-start(bf16[256,1024]{1,0:T(8,128)(2,1)} %rest_0_.1), channel_id=1, source_target_pairs={{8,16},{12,20},{16,8},{20,12},{9,17},{13,21},{17,9},{21,13},{10,18... | collective-permute-start | bytes 1572872 | tf_op jit(solution)/shard_map/ppermute | solution.py:649
  18.5 12.4 %copy-start.26 = (bf16[256,1024]{1,0:T(8,128)(2,1)}, bf16[256,1024]{1,0:T(8,128)(2,1)S(1)}, u32[]{:S(2)}) copy-start(bf16[256,1024]{1,0:T(8,128)(2,1)S(1)} %collective-permute-done.2.rest_1_) | copy-start | bytes 1572868
  18.7 12.2 %copy-start.21 = (bf16[256,1024]{1,0:T(8,128)(2,1)}, bf16[256,1024]{1,0:T(8,128)(2,1)S(1)}, u32[]{:S(2)}) copy-start(bf16[256,1024]{1,0:T(8,128)(2,1)S(1)} %collective-permute-done.3) | copy-start | bytes 1572868
  18.7 16.3 %collective-permute-start.8 = (bf16[256,1024]{1,0:T(8,128)(2,1)S(1)}, bf16[256,1024]{1,0:T(8,128)(2,1)S(1)}, u32[]{:S(2)}, u32[]{:S(2)}) collective-permute-start(bf16[256,1024]{1,0:T(8,128)(2,1)S(1)} %collective-permute-done.3), channel_id=1, source_target_pairs={{8,0},{12,4},{16,24},{20,28},{9,1},{13,5},{17,25},{21,29},{10,2},{... | collective-permute-start | bytes 1572872 | tf_op jit(solution)/shard_map/ppermute | solution.py:649
  20.0 15.0 %collective-permute-start.7 = (bf16[256,1024]{1,0:T(8,128)(2,1)S(1)}, bf16[256,1024]{1,0:T(8,128)(2,1)}, u32[]{:S(2)}, u32[]{:S(2)}) collective-permute-start(bf16[256,1024]{1,0:T(8,128)(2,1)S(1)} %collective-permute-done.2.rest_1_), channel_id=1, source_target_pairs={{8,16},{12,20},{16,8},{20,12},{9,17},{13,21},{17,9},{21,13},{10,18... | collective-permute-start | bytes 1572872 | tf_op jit(solution)/shard_map/ppermute | solution.py:649
  21.4 13.6 %collective-permute-start.6 = (bf16[256,1024]{1,0:T(8,128)(2,1)S(1)}, bf16[256,1024]{1,0:T(8,128)(2,1)}, u32[]{:S(2)}, u32[]{:S(2)}) collective-permute-start(bf16[256,1024]{1,0:T(8,128)(2,1)S(1)} %collective-permute-done.2.rest_1_), channel_id=1, source_target_pairs={{0,2},{2,0},{1,3},{3,1},{4,6},{6,4},{5,7},{7,5},{8,10},{10,8},{9,1... | collective-permute-start | bytes 1572872 | tf_op jit(solution)/shard_map/ppermute | solution.py:180
  21.9 13.1 %collective-permute-start.5 = (bf16[256,1024]{1,0:T(8,128)(2,1)S(1)}, bf16[256,1024]{1,0:T(8,128)(2,1)S(1)}, u32[]{:S(2)}, u32[]{:S(2)}) collective-permute-start(bf16[256,1024]{1,0:T(8,128)(2,1)S(1)} %collective-permute-done.2.rest_1_), channel_id=1, source_target_pairs={{0,4},{4,0},{8,12},{12,8},{16,20},{20,16},{24,28},{28,24},{1,5},{5... | collective-permute-start | bytes 1572872 | tf_op jit(solution)/shard_map/ppermute | solution.py:180
  30.9 11.6 %copy-start.14 = (bf16[128,4096]{1,0:T(8,128)(2,1)S(1)}, bf16[128,4096]{1,0:T(8,128)(2,1)}, u32[]{:S(2)}) copy-start(bf16[128,4096]{1,0:T(8,128)(2,1)} %get-tuple-element.114) | copy-start | bytes 3145732
  35.0 7.4 %collective-permute-start.12 = (bf16[128,4096]{1,0:T(8,128)(2,1)}, bf16[128,4096]{1,0:T(8,128)(2,1)}, u32[]{:S(2)}, u32[]{:S(2)}) collective-permute-start(bf16[128,4096]{1,0:T(8,128)(2,1)} %get-tuple-element.115), channel_id=1, source_target_pairs={{0,1},{1,0},{2,3},{3,2},{4,5},{5,4},{6,7},{7,6},{8,9},{9,8},{10,11... | collective-permute-start | bytes 3145736 | tf_op jit(solution)/shard_map/ppermute | solution.py:180
  35.2 15.1 %collective-permute-start.4 = (bf16[256,1024]{1,0:T(8,128)(2,1)}, bf16[256,1024]{1,0:T(8,128)(2,1)}, u32[]{:S(2)}, u32[]{:S(2)}) collective-permute-start(bf16[256,1024]{1,0:T(8,128)(2,1)} %collective-permute-done.rest_2_), channel_id=1, source_target_pairs={{0,2},{2,0},{1,3},{3,1},{4,6},{6,4},{5,7},{7,5},{8,10},{10,8},{9,1... | collective-permute-start | bytes 1572872 | tf_op jit(solution)/shard_map/ppermute | solution.py:180
  36.1 14.4 %collective-permute-start.9 = (bf16[256,1024]{1,0:T(8,128)(2,1)}, bf16[256,1024]{1,0:T(8,128)(2,1)}, u32[]{:S(2)}, u32[]{:S(2)}) collective-permute-start(bf16[256,1024]{1,0:T(8,128)(2,1)} %collective-permute-done.6.rest_5_), channel_id=1, source_target_pairs={{0,4},{4,0},{8,12},{12,8},{16,20},{20,16},{24,28},{28,24},{1,5},{5... | collective-permute-start | bytes 1572872 | tf_op jit(solution)/shard_map/ppermute | solution.py:180
  37.0 18.8 %collective-permute-start.10 = (bf16[256,1024]{1,0:T(8,128)(2,1)}, bf16[256,1024]{1,0:T(8,128)(2,1)}, u32[]{:S(2)}, u32[]{:S(2)}) collective-permute-start(bf16[256,1024]{1,0:T(8,128)(2,1)} %collective-permute-done.7), channel_id=1, source_target_pairs={{8,0},{12,4},{16,24},{20,28},{9,1},{13,5},{17,25},{21,29},{10,2},{... | collective-permute-start | bytes 1572872 | tf_op jit(solution)/shard_map/ppermute | solution.py:649
  42.4 13.4 %collective-permute-start.11 = (bf16[128,4096]{1,0:T(8,128)(2,1)}, bf16[128,4096]{1,0:T(8,128)(2,1)S(1)}, u32[]{:S(2)}, u32[]{:S(2)}) collective-permute-start(bf16[128,4096]{1,0:T(8,128)(2,1)} %get-tuple-element.112), channel_id=1, source_target_pairs={{0,1},{1,0},{2,3},{3,2},{4,5},{5,4},{6,7},{7,6},{8,9},{9,8},{10,11... | collective-permute-start | bytes 3145736 | tf_op jit(solution)/shard_map/ppermute | solution.py:180
  44.9 20.0 %copy-start.2 = (bf16[128,4096]{1,0:T(8,128)(2,1)S(1)}, bf16[128,4096]{1,0:T(8,128)(2,1)}, u32[]{:S(2)}) copy-start(bf16[128,4096]{1,0:T(8,128)(2,1)} %get-tuple-element.125.own_ref) | copy-start | bytes 3145732
  44.9 16.3 %collective-permute-start.13 = (bf16[64,4096]{1,0:T(8,128)(2,1)}, bf16[64,4096]{1,0:T(8,128)(2,1)}, u32[]{:S(2)}, u32[]{:S(2)}) collective-permute-start(bf16[64,4096]{1,0:T(8,128)(2,1)} %get-tuple-element.214), channel_id=1, source_target_pairs={{0,2},{2,0},{1,3},{3,1},{4,6},{6,4},{5,7},{7,5},{8,10},{10,8},{9,1... | collective-permute-start | bytes 1572872 | tf_op jit(solution)/shard_map/ppermute | solution.py:180
  45.9 79.8 %copy-start.37 = (f32[4,128]{1,0:T(4,128)}, f32[4,128]{1,0:T(4,128)S(1)}, u32[]{:S(2)}) copy-start(f32[4,128]{1,0:T(4,128)S(1)} %convert_add_fusion) | copy-start | bytes 6148
  47.1 24.9 %copy-start.12 = (bf16[256,1024]{1,0:T(8,128)(2,1)}, bf16[256,1024]{1,0:T(8,128)(2,1)S(1)}, u32[]{:S(2)}) copy-start(bf16[256,1024]{1,0:T(8,128)(2,1)S(1)} %broadcast_select_fusion.1.rest_0_) | copy-start | bytes 1572868
  47.1 18.4 %copy-start.43 = (s32[8]{0:T(128)S(1)}, s32[8]{0:T(128)}, u32[]{:S(2)}) copy-start(s32[8]{0:T(128)} %param.22) | copy-start | bytes 100
  47.1 18.9 %copy-start.41 = (s32[1,512]{1,0:T(1,128)S(1)}, s32[1,512]{1,0:T(1,128)}, u32[]{:S(2)}) copy-start(s32[1,512]{1,0:T(1,128)} %param.23) | copy-start | bytes 6148
  47.1 22.8 %copy-start.42 = (s32[32]{0:T(128)S(1)}, s32[32]{0:T(128)}, u32[]{:S(2)}) copy-start(s32[32]{0:T(128)} %param.16) | copy-start | bytes 388
  55.8 16.1 %copy-start.4 = (bf16[128,4096]{1,0:T(8,128)(2,1)}, bf16[128,4096]{1,0:T(8,128)(2,1)S(1)}, u32[]{:S(2)}) copy-start(bf16[128,4096]{1,0:T(8,128)(2,1)S(1)} %collective-permute-done.11.sibling_ref) | copy-start | bytes 3145732
  61.2 13.8 %collective-permute-start.15 = (bf16[256,1024]{1,0:T(8,128)(2,1)S(1)}, bf16[256,1024]{1,0:T(8,128)(2,1)}, u32[]{:S(2)}, u32[]{:S(2)}) collective-permute-start(bf16[256,1024]{1,0:T(8,128)(2,1)S(1)} %broadcast_select_fusion.1.rest_0_), channel_id=1, source_target_pairs={{0,2},{2,0},{1,3},{3,1},{4,6},{6,4},{5,7},{7,5},{8,10},{10,8},{9,1... | collective-permute-start | bytes 1572872 | tf_op jit(solution)/shard_map/ppermute | solution.py:180
  61.9 13.4 %collective-permute-start.14 = (bf16[256,1024]{1,0:T(8,128)(2,1)S(1)}, bf16[256,1024]{1,0:T(8,128)(2,1)}, u32[]{:S(2)}, u32[]{:S(2)}) collective-permute-start(bf16[256,1024]{1,0:T(8,128)(2,1)S(1)} %broadcast_select_fusion.1.rest_0_), channel_id=1, source_target_pairs={{0,4},{4,0},{8,12},{12,8},{16,20},{20,16},{24,28},{28,24},{1,5},{5... | collective-permute-start | bytes 1572872 | tf_op jit(solution)/shard_map/ppermute | solution.py:180
  65.4 26.8 %copy-start.39 = (f32[128]{0:T(128)}, f32[128]{0:T(128)S(1)}, u32[]{:S(2)}) copy-start(f32[128]{0:T(128)S(1)} %multiply_reduce_fusion) | copy-start | bytes 1540
  69.9 3.5 %collective-permute-start.18 = (s32[32]{0:T(128)S(1)}, s32[32]{0:T(128)S(1)}, u32[]{:S(2)}, u32[]{:S(2)}) collective-permute-start(s32[32]{0:T(128)S(1)} %copy-done.42), channel_id=1, source_target_pairs={{0,1},{1,0},{2,3},{3,2},{4,5},{5,4},{6,7},{7,6},{8,9},{9,8},{10,11... | collective-permute-start | bytes 392 | tf_op jit(solution)/shard_map/ppermute | solution.py:180
  72.0 3.4 %collective-permute-start.16 = (bf16[128,2048]{1,0:T(8,128)(2,1)S(1)}, bf16[128,2048]{1,0:T(8,128)(2,1)S(1)}, u32[]{:S(2)}, u32[]{:S(2)}) collective-permute-start(bf16[128,2048]{1,0:T(8,128)(2,1)S(1)} %get-tuple-element.212), channel_id=1, source_target_pairs={{0,1},{1,0},{2,3},{3,2},{4,5},{5,4},{6,7},{7,6},{8,9},{9,8},{10,11... | collective-permute-start | bytes 1572872 | tf_op jit(solution)/shard_map/ppermute | solution.py:180
  73.4 2.0 %collective-permute-start.17 = (bf16[128,2048]{1,0:T(8,128)(2,1)S(1)}, bf16[128,2048]{1,0:T(8,128)(2,1)S(1)}, u32[]{:S(2)}, u32[]{:S(2)}) collective-permute-start(bf16[128,2048]{1,0:T(8,128)(2,1)S(1)} %get-tuple-element.210), channel_id=1, source_target_pairs={{0,1},{1,0},{2,3},{3,2},{4,5},{5,4},{6,7},{7,6},{8,9},{9,8},{10,11... | collective-permute-start | bytes 1572872 | tf_op jit(solution)/shard_map/ppermute | solution.py:180
  75.3 11.2 %copy-start.25 = (bf16[128,2048]{1,0:T(8,128)(2,1)}, bf16[128,2048]{1,0:T(8,128)(2,1)S(1)}, u32[]{:S(2)}) copy-start(bf16[128,2048]{1,0:T(8,128)(2,1)S(1)} %collective-permute-done.17.ub) | copy-start | bytes 1572868
  76.1 14.1 %collective-permute-start.20 = (bf16[256,1024]{1,0:T(8,128)(2,1)}, bf16[256,1024]{1,0:T(8,128)(2,1)S(1)}, u32[]{:S(2)}, u32[]{:S(2)}) collective-permute-start(bf16[256,1024]{1,0:T(8,128)(2,1)} %broadcast_select_fusion.rest_1_), channel_id=1, source_target_pairs={{0,2},{2,0},{1,3},{3,1},{4,6},{6,4},{5,7},{7,5},{8,10},{10,8},{9,1... | collective-permute-start | bytes 1572872 | tf_op jit(solution)/shard_map/ppermute | solution.py:180
  77.3 13.5 %collective-permute-start.19 = (bf16[256,1024]{1,0:T(8,128)(2,1)}, bf16[256,1024]{1,0:T(8,128)(2,1)S(1)}, u32[]{:S(2)}, u32[]{:S(2)}) collective-permute-start(bf16[256,1024]{1,0:T(8,128)(2,1)} %broadcast_select_fusion.rest_1_), channel_id=1, source_target_pairs={{0,4},{4,0},{8,12},{12,8},{16,20},{20,16},{24,28},{28,24},{1,5},{5... | collective-permute-start | bytes 1572872 | tf_op jit(solution)/shard_map/ppermute | solution.py:180
  80.0 12.0 %copy-start = (bf16[64,4096]{1,0:T(8,128)(2,1)S(1)}, bf16[64,4096]{1,0:T(8,128)(2,1)}, u32[]{:S(2)}) copy-start(bf16[64,4096]{1,0:T(8,128)(2,1)} %add_convert_fusion.1.visual_ref) | copy-start | bytes 1572868
  90.8 16.9 %collective-permute-start.23 = (bf16[8,1024,256]{2,1,0:T(8,128)(2,1)}, bf16[8,1024,256]{2,1,0:T(8,128)(2,1)}, u32[]{:S(2)}, u32[]{:S(2)}) collective-permute-start(bf16[8,1024,256]{2,1,0:T(8,128)(2,1)} %get-tuple-element.150.rest_0_), channel_id=1, source_target_pairs={{0,1},{1,0},{2,3},{3,2},{4,5},{5,4},{6,7},{7,6},{8,9},{9,8},{10,11... | collective-permute-start | bytes 12582920 | tf_op jit(solution)/shard_map/ppermute | solution.py:180
  90.8 14.5 %collective-permute-start.21 = (bf16[256,1024]{1,0:T(8,128)(2,1)}, bf16[256,1024]{1,0:T(8,128)(2,1)S(1)}, u32[]{:S(2)}, u32[]{:S(2)}) collective-permute-start(bf16[256,1024]{1,0:T(8,128)(2,1)} %collective-permute-done.14.rest_2_), channel_id=1, source_target_pairs={{0,2},{2,0},{1,3},{3,1},{4,6},{6,4},{5,7},{7,5},{8,10},{10,8},{9,1... | collective-permute-start | bytes 1572872 | tf_op jit(solution)/shard_map/ppermute | solution.py:180
  92.2 8.8 %collective-permute-start.24 = (f32[320]{0:T(512)S(1)}, f32[320]{0:T(512)S(1)}, u32[]{:S(2)}, u32[]{:S(2)}) collective-permute-start(f32[320]{0:T(512)S(1)} %pad_maximum_fusion.2), channel_id=1, source_target_pairs={{0,1},{1,0},{2,3},{3,2},{4,5},{5,4},{6,7},{7,6},{8,9},{9,8},{10,11... | collective-permute-start | bytes 3848 | tf_op jit(solution)/shard_map/ppermute | solution.py:180
  93.3 14.4 %copy-start.1 = (bf16[64,4096]{1,0:T(8,128)(2,1)S(1)}, bf16[64,4096]{1,0:T(8,128)(2,1)}, u32[]{:S(2)}) copy-start(bf16[64,4096]{1,0:T(8,128)(2,1)} %add_convert_fusion.1.visual_ref) | copy-start | bytes 1572868
  93.3 14.4 %copy-start.3 = (bf16[128,4096]{1,0:T(8,128)(2,1)S(1)}, bf16[128,4096]{1,0:T(8,128)(2,1)}, u32[]{:S(2)}) copy-start(bf16[128,4096]{1,0:T(8,128)(2,1)} %get-tuple-element.125.own_ref) | copy-start | bytes 3145732
  93.3 14.4 %copy-start.5 = (bf16[128,4096]{1,0:T(8,128)(2,1)S(1)}, bf16[128,4096]{1,0:T(8,128)(2,1)}, u32[]{:S(2)}) copy-start(bf16[128,4096]{1,0:T(8,128)(2,1)} %copy-done.4) | copy-start | bytes 3145732
  93.3 14.4 %copy-start.9 = (f32[16,1,256]{2,1,0:T(1,128)S(1)}, f32[16,1,256]{2,1,0:T(1,128)}, u32[]{:S(2)}) copy-start(f32[16,1,256]{2,1,0:T(1,128)} %constant_dynamic-slice_fusion.10) | copy-start | bytes 49156
  93.3 14.4 %copy-start.10 = (s32[17]{0:T(128)S(1)}, s32[17]{0:T(128)}, u32[]{:S(2)}) copy-start(s32[17]{0:T(128)} %stack.93.table_ref) | copy-start | bytes 208
  93.3 12.0 %collective-permute-start.25 = (bf16[32,4096]{1,0:T(8,128)(2,1)S(1)}, bf16[32,4096]{1,0:T(8,128)(2,1)S(1)}, u32[]{:S(2)}, u32[]{:S(2)}) collective-permute-start(bf16[32,4096]{1,0:T(8,128)(2,1)S(1)} %get-tuple-element.216), channel_id=1, source_target_pairs={{0,1},{1,0},{2,3},{3,2},{4,5},{5,4},{6,7},{7,6},{8,9},{9,8},{10,11... | collective-permute-start | bytes 786440 | tf_op jit(solution)/shard_map/ppermute | solution.py:180
  93.6 14.1 %collective-permute-start.22 = (bf16[256,1024]{1,0:T(8,128)(2,1)S(1)}, bf16[256,1024]{1,0:T(8,128)(2,1)S(1)}, u32[]{:S(2)}, u32[]{:S(2)}) collective-permute-start(bf16[256,1024]{1,0:T(8,128)(2,1)S(1)} %collective-permute-done.20.rest_5_), channel_id=1, source_target_pairs={{0,4},{4,0},{8,12},{12,8},{16,20},{20,16},{24,28},{28,24},{1,5},{5... | collective-permute-start | bytes 1572872 | tf_op jit(solution)/shard_map/ppermute | solution.py:180
  111.3 42.3 %copy-start.7 = (bf16[2,1024,256]{2,1,0:T(8,128)(2,1)}, bf16[2,1024,256]{2,1,0:T(8,128)(2,1)S(1)}, u32[]{:S(2)}) copy-start(bf16[2,1024,256]{2,1,0:T(8,128)(2,1)S(1)} %get-tuple-element.182.rest_2_) | copy-start | bytes 3145732
  111.3 1.6 collective-permute-start.26
  112.9 46.6 %collective-permute-start.30 = (bf16[6,1024,256]{2,1,0:T(8,128)(2,1)}, bf16[6,1024,256]{2,1,0:T(8,128)(2,1)}, u32[]{:S(2)}, u32[]{:S(2)}) collective-permute-start(bf16[6,1024,256]{2,1,0:T(8,128)(2,1)} %get-tuple-element.180.rest_1_), channel_id=1, source_target_pairs={{0,1},{1,0},{2,3},{3,2},{4,5},{5,4},{6,7},{7,6},{8,9},{9,8},{10,11... | collective-permute-start | bytes 9437192 | tf_op jit(solution)/shard_map/ppermute | solution.py:180
  116.1 17.9 %all-to-all-start = ((bf16[16,8,640]{2,1,0:T(8,128)(2,1)}), bf16[16,8,640]{2,1,0:T(8,128)(2,1)S(1)}, u32[]{:S(2)}, u32[]{:S(2)}) async-start(bf16[16,8,640]{2,1,0:T(8,128)(2,1)} %bitcast.61), calls=%async_computation | async-start | bytes 327680 | tf_op jit(solution)/shard_map/all_to_all | solution.py:750
  123.8 10.2 %collective-permute-start.27 = (bf16[256,512]{1,0:T(8,128)(2,1)}, bf16[256,512]{1,0:T(8,128)(2,1)S(1)}, u32[]{:S(2)}, u32[]{:S(2)}) collective-permute-start(bf16[256,512]{1,0:T(8,128)(2,1)} %get-tuple-element.168.rest_0_), channel_id=1, source_target_pairs={{0,2},{2,0},{1,3},{3,1},{4,6},{6,4},{5,7},{7,5},{8,10},{10,8},{9,1... | collective-permute-start | bytes 786440 | tf_op jit(solution)/shard_map/ppermute | solution.py:180
  125.8 33.8 %collective-permute-start.31 = (bf16[2,1024,256]{2,1,0:T(8,128)(2,1)S(1)}, bf16[2,1024,256]{2,1,0:T(8,128)(2,1)S(1)}, u32[]{:S(2)}, u32[]{:S(2)}) collective-permute-start(bf16[2,1024,256]{2,1,0:T(8,128)(2,1)S(1)} %get-tuple-element.182.rest_2_), channel_id=1, source_target_pairs={{0,1},{1,0},{2,3},{3,2},{4,5},{5,4},{6,7},{7,6},{8,9},{9,8},{10,11... | collective-permute-start | bytes 3145736 | tf_op jit(solution)/shard_map/ppermute | solution.py:180
  126.6 27.1 %copy-start.36 = (bf16[64,512]{1,0:T(8,128)(2,1)S(1)}, bf16[64,512]{1,0:T(8,128)(2,1)}, u32[]{:S(2)}) copy-start(bf16[64,512]{1,0:T(8,128)(2,1)} %get-tuple-element.187) | copy-start | bytes 196612
  126.6 27.8 %copy-start.16 = (bf16[256,512]{1,0:T(8,128)(2,1)S(1)}, bf16[256,512]{1,0:T(8,128)(2,1)}, u32[]{:S(2)}) copy-start(bf16[256,512]{1,0:T(8,128)(2,1)} %get-tuple-element.168.rest_0_) | copy-start | bytes 786436
  153.6 11.7 %copy-start.20 = (bf16[128,2048]{1,0:T(8,128)(2,1)S(1)}, bf16[128,2048]{1,0:T(8,128)(2,1)}, u32[]{:S(2)}) copy-start(bf16[128,2048]{1,0:T(8,128)(2,1)} %get-tuple-element.172) | copy-start | bytes 1572868
  153.7 2.2 %collective-permute-start.28 = (bf16[128,2048]{1,0:T(8,128)(2,1)}, bf16[128,2048]{1,0:T(8,128)(2,1)S(1)}, u32[]{:S(2)}, u32[]{:S(2)}) collective-permute-start(bf16[128,2048]{1,0:T(8,128)(2,1)} %get-tuple-element.171), channel_id=1, source_target_pairs={{0,1},{1,0},{2,3},{3,2},{4,5},{5,4},{6,7},{7,6},{8,9},{9,8},{10,11... | collective-permute-start | bytes 1572872 | tf_op jit(solution)/shard_map/ppermute | solution.py:180
  154.4 11.0 %collective-permute-start.29 = (bf16[128,2048]{1,0:T(8,128)(2,1)}, bf16[128,2048]{1,0:T(8,128)(2,1)S(1)}, u32[]{:S(2)}, u32[]{:S(2)}) collective-permute-start(bf16[128,2048]{1,0:T(8,128)(2,1)} %get-tuple-element.173), channel_id=1, source_target_pairs={{0,1},{1,0},{2,3},{3,2},{4,5},{5,4},{6,7},{7,6},{8,9},{9,8},{10,11... | collective-permute-start | bytes 1572872 | tf_op jit(solution)/shard_map/ppermute | solution.py:180
  155.6 21.7 %collective-permute-start.34 = (bf16[160,512]{1,0:T(8,128)(2,1)}, bf16[160,512]{1,0:T(8,128)(2,1)}, u32[]{:S(2)}, u32[]{:S(2)}) collective-permute-start(bf16[160,512]{1,0:T(8,128)(2,1)} %pad_maximum_fusion.1), channel_id=1, source_target_pairs={{0,1},{1,0},{2,3},{3,2},{4,5},{5,4},{6,7},{7,6},{8,9},{9,8},{10,11... | collective-permute-start | bytes 491528 | tf_op jit(solution)/shard_map/ppermute | solution.py:180
  155.8 10.7 %collective-permute-start.32 = (bf16[256,512]{1,0:T(8,128)(2,1)}, bf16[256,512]{1,0:T(8,128)(2,1)S(1)}, u32[]{:S(2)}, u32[]{:S(2)}) collective-permute-start(bf16[256,512]{1,0:T(8,128)(2,1)} %get-tuple-element.184), channel_id=1, source_target_pairs={{0,2},{2,0},{1,3},{3,1},{4,6},{6,4},{5,7},{7,5},{8,10},{10,8},{9,1... | collective-permute-start | bytes 786440 | tf_op jit(solution)/shard_map/ppermute | solution.py:180
  159.6 17.9 %copy-start.13 = (bf16[2,1024,256]{2,1,0:T(8,128)(2,1)}, bf16[2,1024,256]{2,1,0:T(8,128)(2,1)S(1)}, u32[]{:S(2)}) copy-start(bf16[2,1024,256]{2,1,0:T(8,128)(2,1)S(1)} %collective-permute-done.31.rest_5_) | copy-start | bytes 3145732
  159.6 17.1 %copy-start.35 = (bf16[32,512]{1,0:T(8,128)(2,1)S(1)}, bf16[32,512]{1,0:T(8,128)(2,1)}, u32[]{:S(2)}) copy-start(bf16[32,512]{1,0:T(8,128)(2,1)} %get-tuple-element.221) | copy-start | bytes 98308
  159.6 13.5 %all-to-all-start.1 = ((bf16[16,8,512]{2,1,0:T(8,128)(2,1)}), bf16[16,8,512]{2,1,0:T(8,128)(2,1)S(1)}, u32[]{:S(2)}, u32[]{:S(2)}) async-start(bf16[16,8,512]{2,1,0:T(8,128)(2,1)} %bitcast.63), calls=%async_computation.1 | async-start | bytes 262144 | tf_op jit(solution)/shard_map/all_to_all | solution.py:750
  175.9 1.6 collective-permute-start.33
  (17 other events, 61.5 us)

commit v3 on v2

--- a/solution.py
+++ b/solution.py
@@ -1,3 +1,5 @@
+import math
+
 import jax
 import jax.numpy as jnp
 from jax import lax
@@ -361,7 +363,7 @@
     slots, tokens = picking.shape
 
     def kernel(mine_ref, received_ref, scale_ref, codes_ref, picking_ref, chip_ref, token_ref, slot_ref):
-        pairs = (mine_ref[...] + received_ref[...].astype(jnp.float32)) * scale_ref[...]
+        pairs = (mine_ref[...] + received_ref[...].astype(jnp.float32)) * scale_ref[:, :1]
         pairs = pairs.astype(jnp.bfloat16)
         chip_ref[...] = pairs[: 2 * rows]
         token_ref[...] = pairs[2 * rows :]
@@ -536,7 +538,7 @@
     own_kv = pair_width // (2 * HD)
     heads = width // HD
     group = heads // own_kv
-    step_heads = max(1, group // 2)
+    step_heads = group
     steps = heads // step_heads
     score_scale = HD ** (-0.5)
     f32, bf16 = jnp.float32, jnp.bfloat16
@@ -564,40 +566,46 @@
                 heads_ref[j] = piece.astype(bf16)
                 turned_ref[j] = piece.T.astype(bf16)
             allowed = (pos_ref[...] <= qpos_ref[...]) & (doc_ref[...] == qdoc_ref[...])
-            bias_ref[...] = jnp.where(allowed, 0.0, -jnp.inf).astype(f32)
+            bias_ref[...] = jnp.where(allowed, 0.0, -jnp.inf).astype(f32).T
             total_ref[...] = jnp.zeros_like(total_ref)
 
         head = (step * step_heads) // group
         keys, values = heads_ref[head], heads_ref[own_kv + head]
         keys_turned, values_turned = turned_ref[head], turned_ref[own_kv + head]
-        contract = (((1,), (1,)), ((), ()))
+        lights, score_grads, query_list, ups = [], [], [], []
         for h in range(step_heads):
             lanes = slice(h * HD, (h + 1) * HD)
             query = jnp.concatenate([qa[:, lanes], qb[:, lanes]], axis=0)
             up = jnp.concatenate([ua[:, lanes], ub[:, lanes]], axis=0)
-            scores = lax.dot_general(keys, query, contract, preferred_element_type=f32)
-            scores = scores * score_scale + bias_ref[...]
-            weights = jnp.exp(scores - jnp.max(scores, axis=0, keepdims=True))
-            weights = weights * (1.0 / jnp.sum(weights, axis=0, keepdims=True))
+            scores = jnp.dot(query, keys_turned, preferred_element_type=f32)
+            weight_grad = jnp.dot(up, values_turned, preferred_element_type=f32)
+            scores = scores * (score_scale * math.log2(math.e)) + bias_ref[...]
+            weights = jnp.exp2(scores - jnp.max(scores, axis=1, keepdims=True))
+            weights = weights * (1.0 / jnp.sum(weights, axis=1, keepdims=True))
             light = weights.astype(bf16)
-            output = jnp.dot(values_turned, light, preferred_element_type=f32).T.astype(bf16)
+            inner = jnp.sum(weights * weight_grad, axis=1, keepdims=True)
+            score_grad = (weights * (weight_grad - inner)).astype(bf16)
+            output = jnp.dot(light, values, preferred_element_type=f32).astype(bf16)
             oa[:, lanes] = output[:rows]
             ob[:, lanes] = output[rows:]
-            total_ref[own_kv + head] += jnp.dot(light, up, preferred_element_type=f32)
-            weight_grad = lax.dot_general(values, up, contract, preferred_element_type=f32)
-            inner = jnp.sum(weights * weight_grad, axis=0, keepdims=True)
-            score_grad = (weights * (weight_grad - inner) * score_scale).astype(bf16)
-            query_grad = jnp.dot(keys_turned, score_grad, preferred_element_type=f32).T.astype(bf16)
+            query_grad = (jnp.dot(score_grad, keys, preferred_element_type=f32) * score_scale).astype(bf16)
             ga[:, lanes] = query_grad[:rows]
             gb[:, lanes] = query_grad[rows:]
-            total_ref[head] += jnp.dot(score_grad, query, preferred_element_type=f32)
+            lights.append(light)
+            score_grads.append(score_grad)
+            query_list.append(query)
+            ups.append(up)
+        up, light = jnp.concatenate(ups, axis=0).T, jnp.concatenate(lights, axis=0)
+        total_ref[own_kv + head] += jnp.dot(up, light, preferred_element_type=f32)
+        query, score_grad = jnp.concatenate(query_list, axis=0).T, jnp.concatenate(score_grads, axis=0)
+        total_ref[head] += jnp.dot(query, score_grad, preferred_element_type=f32) * score_scale
 
         @pl.when(step == steps - 1)
         def _():
             codes = visual_ref[:, pair_width : pair_width + 2].astype(f32)
             lifting = jnp.where(codes[:, 0:1] * 16.0 + codes[:, 1:2] == row_l[...], 1.0, 0.0).astype(bf16)
             for j in range(2 * own_kv):
-                piece = total_ref[j].astype(bf16)
+                piece = total_ref[j].T.astype(bf16)
                 place = slice(j * HD, (j + 1) * HD)
                 for i, ref in enumerate(grad_refs):
                     ref[:, place] = piece[i * ref.shape[0] : (i + 1) * ref.shape[0]]
@@ -617,8 +625,8 @@
         scratch_shapes=[
             pltpu.VMEM((2 * own_kv, length, HD), bf16),
             pltpu.VMEM((2 * own_kv, HD, length), bf16),
-            pltpu.VMEM((length, 2 * rows), f32),
-            pltpu.VMEM((2 * own_kv, length, HD), f32),
+            pltpu.VMEM((2 * rows, length), f32),
+            pltpu.VMEM((2 * own_kv, HD, length), f32),
         ],
         compiler_params=vmem_params(56),
         cost_estimate=brief(),
@@ -784,16 +792,17 @@
     arrived = swap(jnp.concatenate([sibling_squares, own_squares, visual_squares]))
     square = jnp.concatenate([own_squares, sibling_squares, visual_squares]) + arrived
     scale = lax.rsqrt(square / width + epsilon)[:, None]
+    wide_scale = jnp.broadcast_to(scale, (scale.shape[0], 128))
     own_visual, other_visual = of_core(visual, core), swap(of_core(visual, 1 - core))
     own_scale = jnp.concatenate([scale[:rows], of_core(scale[2 * rows :], core)], axis=0)
-    corner2, corner3, part1, sums, other0, scale, own_visual, other_visual, own_scale = close(
-        (corner2, corner3, part1, sums, other0, scale, own_visual, other_visual, own_scale)
+    corner2, corner3, part1, sums, other0, wide_scale, own_visual, other_visual, own_scale = close(
+        (corner2, corner3, part1, sums, other0, wide_scale, own_visual, other_visual, own_scale)
     )
     part2, *sums = project(table, own_rows, sibling_rows, visual, gain, [corner2, corner3], 14, 16, (sums,))
     turned, turned_other = [part0, part1, part2], [other0]
     mine, theirs = sums
     received = swap(theirs)
-    pair_chip, pair_tokens, leaving = finish_pairs(mine, received, scale, codes, picking, rows)
+    pair_chip, pair_tokens, leaving = finish_pairs(mine, received, wide_scale, codes, picking, rows)
     pair_text = [pair_chip] + [neighbor(pair_chip, "y", down) for down in range(1, column_count)]
     pair_visual = between_chips(leaving)
     turned_other += [swap(after(part, (received,))) for part in turned[1:]]
@@ -801,6 +810,7 @@
     own_pairs = jnp.concatenate([pair_chip[:rows], of_core(pair_tokens, core)], axis=0)
     other_pairs = swap(jnp.concatenate([pair_chip[rows:], of_core(pair_tokens, 1 - core)], axis=0))
 
+    pair_text[0] = after(pair_text[0], (own_pairs, other_pairs, turned_other))
     out_a, out_b, grad_a, grad_b, pair_grad, *far_grads, visual_pair_grad, keep = attend_pair(
         query_parts, upstream_parts, pair_text, pair_visual, keyed
     )
@@ -812,7 +822,7 @@
         )
 
     received = [neighbor(part, "y", down) for down, part in enumerate(far_grads, 1)]
-    returned = between_chips(after(visual_pair_grad, turned_other))
+    returned = between_chips(visual_pair_grad)
     attention, query_grad = heads_back(out_a, out_b), heads_back(grad_a, grad_b)
     pair_grad, attention, query_grad = close((pair_grad, attention, query_grad))
     held, leaving = sum_grads(core_word, pair_grad, received, returned, picking, rows)

time: 190 us -> 177 us (0.932)
  starting transfers between devices: 40.4 us -> 35.9 us
  Pallas kernels: 59.5 us -> 55.1 us
  waiting for transfers between devices: 43.7 us -> 41.2 us
    ppermute x30, waiting for transfers between devices: 27.7 us -> 20.7 us  [neighbor(): return lax.ppermute(values, axis, [(d, d ^ offset) for d in range(count)])]
    all_to_all x2, starting transfers between devices: 13.5 us -> 7.83 us  [between_chips(): lax.all_to_all(shaped, ('dp', 'y'), split_axis=0, concat_axis=0, tiled=True)]
    pallas_call x1, Pallas kernels: 18.9 us -> 14.6 us  [attend_pair(): pl.pallas_call(kernel, grid=(steps,), in_specs=[part] * 4 + [vmem] * (7 +...]
    ppermute x5, waiting for transfers between devices: 9.47 us -> 13.7 us  [line(): lax.ppermute(values, 'dp', [(2 * p + low, 2 * q + low) for p, q in pairs...]
    ppermute x30, starting transfers between devices: 19 us -> 21.6 us  [neighbor(): return lax.ppermute(values, axis, [(d, d ^ offset) for d in range(count)])]
    unnamed x88 -> x78, local copies, waits for them, and re-layouts: 5.12 us -> 4.56 us
  transfers between devices with their start and end apart: 37 -> 37, of which waited for: 16 -> 16; matrix products, arithmetic and copies ran while one was open for 21% -> 21% of each run, Pallas kernels for 25% -> 15%
where the time goes in v3:
time: 177 us
  Pallas kernels  55.1 us (31%)
  waiting for transfers between devices  41.2 us (23%)
  starting transfers between devices  35.9 us (20%)
  local copies, waits for them, and re-layouts  19.2 us (11%)
  other arithmetic  17.5 us (10%)
  matrix products  6.22 us (4%)
    ppermute x30, starting transfers between devices, neighbor(): return lax.ppermute(values, axis, [(d, d ^ offset) for d in range(count)])  21.6 us
    ppermute x30, waiting for transfers between devices, neighbor(): return lax.ppermute(values, axis, [(d, d ^ offset) for d in range(count)])  20.7 us
    pallas_call x1, Pallas kernels, attend_pair(): pl.pallas_call(kernel, grid=(steps,), in_specs=[part] * 4 + [vmem] * (7 +...  14.6 us
    pallas_call x3, Pallas kernels, project(): pl.pallas_call(kernel, in_specs=[smem()] + [vmem] * (4 + size + len(earli...  14.2 us
    ppermute x5, waiting for transfers between devices, line(): lax.ppermute(values, 'dp', [(2 * p + low, 2 * q + low) for p, q in pairs...  13.7 us
    pallas_call x1, Pallas kernels, project_back(): pl.pallas_call(kernel, in_specs=[smem()] + [vmem] * 10 + [pl.BlockSpec(me...  10.7 us
    all_to_all x2, starting transfers between devices, between_chips(): lax.all_to_all(shaped, ('dp', 'y'), split_axis=0, concat_axis=0, tiled=True)  7.83 us
    pallas_call x1, Pallas kernels, down_halves(): pl.pallas_call(kernel, in_specs=[smem(), vmem, pl.BlockSpec(memory_space=...  7.45 us
  transfers between devices with their start and end apart: 37, of which 16 were waited for; matrix products, arithmetic and copies ran while one was open for 21% of the time, Pallas kernels for 15%

profile of v3, /device:TPU:0, one launch (start us, length us, event | category | flops | bytes accessed | tf_op | source)
XLA Modules:
  0.0 176.6 jit_solution(14111944459978772153)
XLA Ops:
  0.7 3.0 %collective-permute-start = (bf16[256,1024]{1,0:T(8,128)(2,1)}, bf16[256,1024]{1,0:T(8,128)(2,1)}, u32[]{:S(2)}, u32[]{:S(2)}) collective-permute-start(bf16[256,1024]{1,0:T(8,128)(2,1)} %rest_0_.1), channel_id=1, source_target_pairs={{0,4},{4,0},{8,12},{12,8},{16,20},{20,16},{24,28},{28,24},{1,5},{5... | collective-permute-start | bytes 1572872 | tf_op jit(solution)/shard_map/ppermute | solution.py:182
  3.7 1.5 collective-permute-start.1
  5.2 1.6 collective-permute-start.2
  6.8 0.7 collective-permute-start.3
  7.5 1.5 convert_reduce_fusion.3
  10.3 1.3 fusion.27
  12.2 6.2 %fusion.30.hidden_ref = bf16[128,768]{1,0:T(8,128)(2,1)} fusion(bf16[5120,768]{1,0:T(8,128)(2,1)} %param.14, bf16[128,1280]{1,0:T(8,128)(2,1)} %get-tuple-element.209, bf16[128,1280]{1,0:T(8,128)(2,1)} %get-tuple-element.208, bf16[128,1280]{1,0:T(8,128)(2,1)} %get-tuple-element.207, bf16[128,1280]{1,0:T(8,128)(2,1)S(1)} %get-tuple-element.206), kind=kOutput, calls=%fused_computation.51 | convolution fusion | flops 1018265600 | bytes 9371648 | tf_op jit(solution)/shard_map/dot_general | solution.py:692
  19.6 1.4 collective-permute-start.7
  21.0 1.3 collective-permute-start.8
  22.3 7.5 %merge_down.1 = (bf16[128,4096]{1,0:T(8,128)(2,1)}, bf16[128,4096]{1,0:T(8,128)(2,1)}) custom-call(s32[1]{0:T(128)} %bitcast.1.core_ref, bf16[128,768]{1,0:T(8,128)(2,1)} %fusion.30.hidden_ref, bf16[768,8192]{1,0:T(8,128)(2,1)} %weight_ref.1), custom_call_target="tpu_custom_call" | custom-call | flops 1 | bytes 1 | tf_op jit(solution)/shard_map/merge_down/pallas_call | solution.py:266
  29.8 1.5 collective-permute-done.5.rest_3_
  31.7 6.6 %collective-permute-done.8 = bf16[256,1024]{1,0:T(8,128)(2,1)S(1)} collective-permute-done((bf16[256,1024]{1,0:T(8,128)(2,1)S(1)}, bf16[256,1024]{1,0:T(8,128)(2,1)S(1)}, u32[]{:S(2)}, u32[]{:S(2)}) %collective-permute-start.8) | collective-permute-done | bytes 524320 | tf_op jit(solution)/shard_map/ppermute | solution.py:657
  38.5 1.6 collective-permute-start.4
  40.1 3.9 %split_halves.1 = (bf16[128,4096]{1,0:T(8,128)(2,1)}, bf16[128,4096]{1,0:T(8,128)(2,1)}) custom-call(s32[1]{0:T(128)} %bitcast.1.core_ref, bf16[128,8192]{1,0:T(8,128)(2,1)} %bitcast.53), custom_call_target="tpu_custom_call" | custom-call | flops 1 | bytes 1 | tf_op jit(solution)/shard_map/split_halves/pallas_call | solution.py:231
  44.2 1.5 collective-permute-start.10
  45.7 1.6 collective-permute-start.9
  47.3 1.5 add_convert_fusion
  48.8 0.9 constant_dynamic-slice_fusion.8
  50.4 1.1 broadcast_select_fusion.1.rest_0_
  51.5 2.0 %collective-permute-done.4.rest_6_ = bf16[256,1024]{1,0:T(8,128)(2,1)} collective-permute-done((bf16[256,1024]{1,0:T(8,128)(2,1)}, bf16[256,1024]{1,0:T(8,128)(2,1)}, u32[]{:S(2)}, u32[]{:S(2)}) %collective-permute-start.4) | collective-permute-done | bytes 524320 | tf_op jit(solution)/shard_map/ppermute | solution.py:182
  53.6 7.0 %collective-permute-done.10 = bf16[256,1024]{1,0:T(8,128)(2,1)} collective-permute-done((bf16[256,1024]{1,0:T(8,128)(2,1)}, bf16[256,1024]{1,0:T(8,128)(2,1)}, u32[]{:S(2)}, u32[]{:S(2)}) %collective-permute-start.10) | collective-permute-done | bytes 524320 | tf_op jit(solution)/shard_map/ppermute | solution.py:657
  60.6 3.9 %collective-permute-done.13 = bf16[64,4096]{1,0:T(8,128)(2,1)} collective-permute-done((bf16[64,4096]{1,0:T(8,128)(2,1)}, bf16[64,4096]{1,0:T(8,128)(2,1)}, u32[]{:S(2)}, u32[]{:S(2)}) %collective-permute-start.13) | collective-permute-done | bytes 524320 | tf_op jit(solution)/shard_map/ppermute | solution.py:182
  64.4 1.5 collective-permute-start.14
  65.9 1.5 collective-permute-start.15
  70.5 1.0 constant_dynamic-slice_fusion.6
  72.0 1.0 constant_dynamic-slice_fusion.4
  73.1 1.9 %broadcast_select_fusion.rest_1_ = bf16[256,1024]{1,0:T(8,128)(2,1)} fusion(bf16[256,1024]{1,0:T(8,128)(2,1)} %collective-permute-done.7, bf16[256,1024]{1,0:T(8,128)(2,1)} %collective-permute-done.10, pred[]{:T(512)S(6)} %or.3), kind=kLoop, calls=%fused_computation.47 | loop fusion | flops 262144 | bytes 1572865 | tf_op jit(solution)/shard_map/jit(_where)/select_n | solution.py:728
  77.1 0.7 select_convert_fusion.codes_ref
  77.8 0.7 and_convert_fusion.picking_ref
  78.5 0.8 collective-permute-done.15.rest_4_
  79.8 1.5 collective-permute-start.20
  81.4 2.0 %add_convert_fusion.1.visual_ref = bf16[64,4096]{1,0:T(8,128)(2,1)} fusion(bf16[64,4096]{1,0:T(8,128)(2,1)} %collective-permute-done.13, bf16[64,4096]{1,0:T(8,128)(2,1)S(1)} %get-tuple-element.133), kind=kLoop, calls=%fused_computation.17 | loop fusion | flops 1048576 | bytes 1572864 | tf_op jit(solution)/shard_map/convert_element_type | solution.py:782
  83.3 6.6 %project_pairs.3 = (bf16[8,1024,256]{2,1,0:T(8,128)(2,1)}, f32[320,1024]{1,0:T(8,128)}) custom-call(s32[17]{0:T(128)} %stack.93.table_ref, bf16[128,4096]{1,0:T(8,128)(2,1)} %get-tuple-element.125.own_ref, bf16[128,4096]{1,0:T(8,128)(2,1)} %copy-done.4, bf16[64,4096]{1,0:T(8,128)(2,1)} %add_convert_fusion.1.visual_ref, f32[1,4096]{1,0:T(1,128)} %bitcast.50, ...), custom_call_target="tpu_custom_call" | custom-call | flops 1 | bytes 1 | tf_op jit(solution)/shard_map/project_pairs/pallas_call | solution.py:349
  89.9 3.2 %collective-permute-done.19.rest_3_ = bf16[256,1024]{1,0:T(8,128)(2,1)S(1)} collective-permute-done((bf16[256,1024]{1,0:T(8,128)(2,1)}, bf16[256,1024]{1,0:T(8,128)(2,1)S(1)}, u32[]{:S(2)}, u32[]{:S(2)}) %collective-permute-start.19) | collective-permute-done | bytes 524320 | tf_op jit(solution)/shard_map/ppermute | solution.py:182
  94.4 0.7 constant_dynamic-slice_fusion.2
  95.5 1.5 collective-permute-start.22
  97.0 6.3 %project_pairs.4 = (bf16[6,1024,256]{2,1,0:T(8,128)(2,1)}, f32[320,1024]{1,0:T(8,128)}) custom-call(s32[17]{0:T(128)} %stack.93.table_ref, bf16[128,4096]{1,0:T(8,128)(2,1)} %get-tuple-element.125.own_ref, bf16[128,4096]{1,0:T(8,128)(2,1)} %copy-done.4, bf16[64,4096]{1,0:T(8,128)(2,1)} %add_convert_fusion.1.visual_ref, f32[1,4096]{1,0:T(1,128)} %bitcast.51, ...), custom_call_target="tpu_custom_call" | custom-call | flops 1 | bytes 1 | tf_op jit(solution)/shard_map/project_pairs/pallas_call | solution.py:349
  103.4 4.5 %collective-permute-done.21.rest_0_ = bf16[256,1024]{1,0:T(8,128)(2,1)S(1)} collective-permute-done((bf16[256,1024]{1,0:T(8,128)(2,1)}, bf16[256,1024]{1,0:T(8,128)(2,1)S(1)}, u32[]{:S(2)}, u32[]{:S(2)}) %collective-permute-start.21) | collective-permute-done | bytes 524320 | tf_op jit(solution)/shard_map/ppermute | solution.py:182
  107.9 1.6 collective-permute-done.22.rest_1_
  109.6 0.8 broadcast_in_dim.100.scale_ref
  110.4 1.3 copy-done.6
  111.7 1.4 project_pairs.5
  113.1 0.8 copy-done.8
  113.9 1.6 collective-permute-done.26.received_ref
  116.3 2.2 %finish_pairs.1 = (bf16[256,512]{1,0:T(8,128)(2,1)}, bf16[64,512]{1,0:T(8,128)(2,1)}, bf16[128,640]{1,0:T(8,128)(2,1)}) custom-call(f32[320,512]{1,0:T(8,128)} %copy-done.8, bf16[320,512]{1,0:T(8,128)(2,1)} %copy-done.27, f32[320,128]{1,0:T(8,128)} %broadcast_in_dim.100.scale_ref, bf16[64,128]{1,0:T(8,128)(2,1)} %select_convert_fusion.codes_ref, ...), custom_call_target="tpu_custom_call" | custom-call | flops 1 | bytes 1 | tf_op jit(solution)/shard_map/finish_pairs/pallas_call | solution.py:379
  118.4 1.5 collective-permute-start.30
  120.0 4.0 %all-to-all-start = ((bf16[16,8,640]{2,1,0:T(8,128)(2,1)}), bf16[16,8,640]{2,1,0:T(8,128)(2,1)S(1)}, u32[]{:S(2)}, u32[]{:S(2)}) async-start(bf16[16,8,640]{2,1,0:T(8,128)(2,1)} %bitcast.61), calls=%async_computation | async-start | bytes 327680 | tf_op jit(solution)/shard_map/all_to_all | solution.py:758
  123.9 1.0 fusion.48
  124.9 0.8 constant_dynamic-slice_fusion
  125.8 0.9 copy.23.row_s
  126.7 0.9 copy.24.pos_ref
  127.5 0.9 copy.25.doc_ref
  128.4 0.7 pad_maximum_fusion.pair_ref
  129.1 2.7 %all-to-all-done = bf16[16,8,640]{2,1,0:T(8,128)(2,1)S(1)} async-done(((bf16[16,8,640]{2,1,0:T(8,128)(2,1)}), bf16[16,8,640]{2,1,0:T(8,128)(2,1)S(1)}, u32[]{:S(2)}, u32[]{:S(2)}) %all-to-all-start) | async-done | bytes 163872 | tf_op jit(solution)/shard_map/all_to_all | solution.py:758
  132.5 14.6 %attend.1 = (bf16[128,2048]{1,0:T(8,128)(2,1)}, bf16[128,2048]{1,0:T(8,128)(2,1)}, bf16[128,2048]{1,0:T(8,128)(2,1)}, bf16[128,2048]{1,0:T(8,128)(2,1)}, bf16[25...) custom-call(bf16[128,2048]{1,0:T(8,128)(2,1)} %get-tuple-element.127.qa, ...), custom_call_target="tpu_custom_call" | custom-call | flops 1 | bytes 1 | tf_op jit(solution)/shard_map/attend/pallas_call | solution.py:617
  147.7 1.2 collective-permute-start.33
  148.9 3.9 %all-to-all-start.1 = ((bf16[16,8,512]{2,1,0:T(8,128)(2,1)}), bf16[16,8,512]{2,1,0:T(8,128)(2,1)S(1)}, u32[]{:S(2)}, u32[]{:S(2)}) async-start(bf16[16,8,512]{2,1,0:T(8,128)(2,1)} %bitcast.63), calls=%async_computation.1 | async-start | bytes 262144 | tf_op jit(solution)/shard_map/all_to_all | solution.py:758
  152.8 2.5 %maximum_select_fusion.1 = bf16[128,4096]{1,0:T(8,128)(2,1)} fusion(bf16[128,2048]{1,0:T(8,128)(2,1)S(1)} %collective-permute-done.32, bf16[128,2048]{1,0:T(8,128)(2,1)} %get-tuple-element.179, pred[]{:T(512)S(6)} %eq.81), kind=kLoop, calls=%fused_computation.15 | loop fusion | flops 4718592 | bytes 2097153 | tf_op jit(solution)/shard_map/jit(_where)/select_n | solution.py:820
  155.3 1.2 maximum_select_fusion
  156.5 4.1 %all-to-all-done.1 = bf16[16,8,512]{2,1,0:T(8,128)(2,1)S(1)} async-done(((bf16[16,8,512]{2,1,0:T(8,128)(2,1)}), bf16[16,8,512]{2,1,0:T(8,128)(2,1)S(1)}, u32[]{:S(2)}, u32[]{:S(2)}) %all-to-all-start.1) | async-done | bytes 131104 | tf_op jit(solution)/shard_map/all_to_all | solution.py:758
  161.3 2.1 %sum_grads.1 = (bf16[160,512]{1,0:T(8,128)(2,1)}, bf16[160,512]{1,0:T(8,128)(2,1)}) custom-call(s32[1]{0:T(128)} %bitcast.1.core_ref, bf16[256,512]{1,0:T(8,128)(2,1)} %get-tuple-element.183.grad_ref, bf16[128,512]{1,0:T(8,128)(2,1)} %bitcast.60, bf16[128,64]{1,0:T(8,128)(2,1)} %and_convert_fusion.picking_ref, bf16[256,512]{1,0:T(8,128)(2,1)} %copy-done.29), custom_call_target="tpu_custom_call" | custom-call | flops 1 | bytes 1 | tf_op jit(solution)/shard_map/sum_grads/pallas_call | solution.py:422
  163.4 0.7 copy.26.scale_ref
  164.2 0.9 collective-permute-done.34.grad_other_ref
  165.7 10.7 %project_back.1 = (bf16[128,8192]{1,0:T(8,128)(2,1)}, bf16[32,8192]{1,0:T(8,128)(2,1)}) custom-call(s32[17]{0:T(128)} %stack.93.table_ref, bf16[160,512]{1,0:T(8,128)(2,1)} %get-tuple-element.186.grad_ref, bf16[160,512]{1,0:T(8,128)(2,1)} %copy-done.32, bf16[160,512]{1,0:T(8,128)(2,1)} %pad_maximum_fusion.pair_ref, bf16[160,512]{1,0:T(8,128)(2,1)} %copy-done.31, ...), custom_call_target="tpu_custom_call" | custom-call | flops 1 | bytes 1 | tf_op jit(solution)/shard_map/project_back/pallas_call | solution.py:518
  (167 shorter events, 15.8 us)
Async XLA Ops:
  0.6 8.4 %copy-start.11 = (bf16[128,5120]{1,0:T(8,128)(2,1)S(1)}, bf16[128,5120]{1,0:T(8,128)(2,1)}, u32[]{:S(2)}) copy-start(bf16[128,5120]{1,0:T(8,128)(2,1)} %param.12) | copy-start | bytes 3932164
  0.6 9.0 %copy-start.33 = (f32[8192]{0:T(1024)S(1)}, f32[8192]{0:T(1024)}, u32[]{:S(2)}) copy-start(f32[8192]{0:T(1024)} %param.18) | copy-start | bytes 98308
  0.7 9.6 %copy-start.35 = (f32[1280]{0:T(1024)S(1)}, f32[1280]{0:T(1024)}, u32[]{:S(2)}) copy-start(f32[1280]{0:T(1024)} %param.13) | copy-start | bytes 15364
  0.7 17.8 %collective-permute-start = (bf16[256,1024]{1,0:T(8,128)(2,1)}, bf16[256,1024]{1,0:T(8,128)(2,1)}, u32[]{:S(2)}, u32[]{:S(2)}) collective-permute-start(bf16[256,1024]{1,0:T(8,128)(2,1)} %rest_0_.1), channel_id=1, source_target_pairs={{0,4},{4,0},{8,12},{12,8},{16,20},{20,16},{24,28},{28,24},{1,5},{5... | collective-permute-start | bytes 1572872 | tf_op jit(solution)/shard_map/ppermute | solution.py:182
  3.7 14.8 %collective-permute-start.1 = (bf16[256,1024]{1,0:T(8,128)(2,1)}, bf16[256,1024]{1,0:T(8,128)(2,1)S(1)}, u32[]{:S(2)}, u32[]{:S(2)}) collective-permute-start(bf16[256,1024]{1,0:T(8,128)(2,1)} %rest_0_.1), channel_id=1, source_target_pairs={{0,2},{2,0},{1,3},{3,1},{4,6},{6,4},{5,7},{7,5},{8,10},{10,8},{9,1... | collective-permute-start | bytes 1572872 | tf_op jit(solution)/shard_map/ppermute | solution.py:182
  5.2 13.3 %collective-permute-start.2 = (bf16[256,1024]{1,0:T(8,128)(2,1)}, bf16[256,1024]{1,0:T(8,128)(2,1)S(1)}, u32[]{:S(2)}, u32[]{:S(2)}) collective-permute-start(bf16[256,1024]{1,0:T(8,128)(2,1)} %rest_0_.1), channel_id=1, source_target_pairs={{0,8},{4,12},{8,0},{12,4},{16,24},{20,28},{24,16},{28,20},{1,9},{5... | collective-permute-start | bytes 1572872 | tf_op jit(solution)/shard_map/ppermute | solution.py:657
  6.8 11.7 %collective-permute-start.3 = (bf16[256,1024]{1,0:T(8,128)(2,1)}, bf16[256,1024]{1,0:T(8,128)(2,1)S(1)}, u32[]{:S(2)}, u32[]{:S(2)}) collective-permute-start(bf16[256,1024]{1,0:T(8,128)(2,1)} %rest_0_.1), channel_id=1, source_target_pairs={{8,16},{12,20},{16,8},{20,12},{9,17},{13,21},{17,9},{21,13},{10,18... | collective-permute-start | bytes 1572872 | tf_op jit(solution)/shard_map/ppermute | solution.py:657
  18.5 11.3 %copy-start.25 = (bf16[256,1024]{1,0:T(8,128)(2,1)}, bf16[256,1024]{1,0:T(8,128)(2,1)S(1)}, u32[]{:S(2)}) copy-start(bf16[256,1024]{1,0:T(8,128)(2,1)S(1)} %collective-permute-done.2.rest_1_) | copy-start | bytes 1572868
  18.5 11.3 %copy-start.21 = (bf16[256,1024]{1,0:T(8,128)(2,1)}, bf16[256,1024]{1,0:T(8,128)(2,1)S(1)}, u32[]{:S(2)}) copy-start(bf16[256,1024]{1,0:T(8,128)(2,1)S(1)} %collective-permute-done.3) | copy-start | bytes 1572868
  18.5 12.9 %collective-permute-start.5 = (bf16[256,1024]{1,0:T(8,128)(2,1)S(1)}, bf16[256,1024]{1,0:T(8,128)(2,1)S(1)}, u32[]{:S(2)}, u32[]{:S(2)}) collective-permute-start(bf16[256,1024]{1,0:T(8,128)(2,1)S(1)} %collective-permute-done.2.rest_1_), channel_id=1, source_target_pairs={{0,4},{4,0},{8,12},{12,8},{16,20},{20,16},{24,28},{28,24},{1,5},{5... | collective-permute-start | bytes 1572872 | tf_op jit(solution)/shard_map/ppermute | solution.py:182
  19.1 12.6 %collective-permute-start.6 = (bf16[256,1024]{1,0:T(8,128)(2,1)S(1)}, bf16[256,1024]{1,0:T(8,128)(2,1)}, u32[]{:S(2)}, u32[]{:S(2)}) collective-permute-start(bf16[256,1024]{1,0:T(8,128)(2,1)S(1)} %collective-permute-done.2.rest_1_), channel_id=1, source_target_pairs={{0,2},{2,0},{1,3},{3,1},{4,6},{6,4},{5,7},{7,5},{8,10},{10,8},{9,1... | collective-permute-start | bytes 1572872 | tf_op jit(solution)/shard_map/ppermute | solution.py:182
  19.6 12.1 %collective-permute-start.7 = (bf16[256,1024]{1,0:T(8,128)(2,1)S(1)}, bf16[256,1024]{1,0:T(8,128)(2,1)}, u32[]{:S(2)}, u32[]{:S(2)}) collective-permute-start(bf16[256,1024]{1,0:T(8,128)(2,1)S(1)} %collective-permute-done.2.rest_1_), channel_id=1, source_target_pairs={{8,16},{12,20},{16,8},{20,12},{9,17},{13,21},{17,9},{21,13},{10,18... | collective-permute-start | bytes 1572872 | tf_op jit(solution)/shard_map/ppermute | solution.py:657
  21.0 17.3 %collective-permute-start.8 = (bf16[256,1024]{1,0:T(8,128)(2,1)S(1)}, bf16[256,1024]{1,0:T(8,128)(2,1)S(1)}, u32[]{:S(2)}, u32[]{:S(2)}) collective-permute-start(bf16[256,1024]{1,0:T(8,128)(2,1)S(1)} %collective-permute-done.3), channel_id=1, source_target_pairs={{8,0},{12,4},{16,24},{20,28},{9,1},{13,5},{17,25},{21,29},{10,2},{... | collective-permute-start | bytes 1572872 | tf_op jit(solution)/shard_map/ppermute | solution.py:657
  29.8 17.5 %copy-start.14 = (bf16[128,4096]{1,0:T(8,128)(2,1)S(1)}, bf16[128,4096]{1,0:T(8,128)(2,1)}, u32[]{:S(2)}) copy-start(bf16[128,4096]{1,0:T(8,128)(2,1)} %get-tuple-element.114) | copy-start | bytes 3145732
  31.4 12.6 %copy-start.26 = (bf16[256,1024]{1,0:T(8,128)(2,1)}, bf16[256,1024]{1,0:T(8,128)(2,1)S(1)}, u32[]{:S(2)}) copy-start(bf16[256,1024]{1,0:T(8,128)(2,1)S(1)} %collective-permute-done.5.rest_3_) | copy-start | bytes 1572868
  38.4 5.6 %copy-start.22 = (bf16[256,1024]{1,0:T(8,128)(2,1)}, bf16[256,1024]{1,0:T(8,128)(2,1)S(1)}, u32[]{:S(2)}) copy-start(bf16[256,1024]{1,0:T(8,128)(2,1)S(1)} %collective-permute-done.8) | copy-start | bytes 1572868
  38.4 8.9 %collective-permute-start.12 = (bf16[128,4096]{1,0:T(8,128)(2,1)}, bf16[128,4096]{1,0:T(8,128)(2,1)}, u32[]{:S(2)}, u32[]{:S(2)}) collective-permute-start(bf16[128,4096]{1,0:T(8,128)(2,1)} %get-tuple-element.115), channel_id=1, source_target_pairs={{0,1},{1,0},{2,3},{3,2},{4,5},{5,4},{6,7},{7,6},{8,9},{9,8},{10,11... | collective-permute-start | bytes 3145736 | tf_op jit(solution)/shard_map/ppermute | solution.py:182
  38.5 15.1 %collective-permute-start.4 = (bf16[256,1024]{1,0:T(8,128)(2,1)}, bf16[256,1024]{1,0:T(8,128)(2,1)}, u32[]{:S(2)}, u32[]{:S(2)}) collective-permute-start(bf16[256,1024]{1,0:T(8,128)(2,1)} %collective-permute-done.rest_2_), channel_id=1, source_target_pairs={{0,2},{2,0},{1,3},{3,1},{4,6},{6,4},{5,7},{7,5},{8,10},{10,8},{9,1... | collective-permute-start | bytes 1572872 | tf_op jit(solution)/shard_map/ppermute | solution.py:182
  44.0 16.6 %collective-permute-start.11 = (bf16[128,4096]{1,0:T(8,128)(2,1)}, bf16[128,4096]{1,0:T(8,128)(2,1)S(1)}, u32[]{:S(2)}, u32[]{:S(2)}) collective-permute-start(bf16[128,4096]{1,0:T(8,128)(2,1)} %get-tuple-element.112), channel_id=1, source_target_pairs={{0,1},{1,0},{2,3},{3,2},{4,5},{5,4},{6,7},{7,6},{8,9},{9,8},{10,11... | collective-permute-start | bytes 3145736 | tf_op jit(solution)/shard_map/ppermute | solution.py:182
  44.2 16.3 %collective-permute-start.10 = (bf16[256,1024]{1,0:T(8,128)(2,1)}, bf16[256,1024]{1,0:T(8,128)(2,1)}, u32[]{:S(2)}, u32[]{:S(2)}) collective-permute-start(bf16[256,1024]{1,0:T(8,128)(2,1)} %collective-permute-done.7), channel_id=1, source_target_pairs={{8,0},{12,4},{16,24},{20,28},{9,1},{13,5},{17,25},{21,29},{10,2},{... | collective-permute-start | bytes 1572872 | tf_op jit(solution)/shard_map/ppermute | solution.py:657
  45.7 14.8 %collective-permute-start.9 = (bf16[256,1024]{1,0:T(8,128)(2,1)}, bf16[256,1024]{1,0:T(8,128)(2,1)}, u32[]{:S(2)}, u32[]{:S(2)}) collective-permute-start(bf16[256,1024]{1,0:T(8,128)(2,1)} %collective-permute-done.6.rest_5_), channel_id=1, source_target_pairs={{0,4},{4,0},{8,12},{12,8},{16,20},{20,16},{24,28},{28,24},{1,5},{5... | collective-permute-start | bytes 1572872 | tf_op jit(solution)/shard_map/ppermute | solution.py:182
  48.8 18.7 %copy-start.37 = (s32[32]{0:T(128)S(1)}, s32[32]{0:T(128)}, u32[]{:S(2)}) copy-start(s32[32]{0:T(128)} %param.16) | copy-start | bytes 388
  48.8 19.2 %copy-start.36 = (s32[1,512]{1,0:T(1,128)S(1)}, s32[1,512]{1,0:T(1,128)}, u32[]{:S(2)}) copy-start(s32[1,512]{1,0:T(1,128)} %param.23) | copy-start | bytes 6148
  48.8 19.9 %copy-start.38 = (s32[8]{0:T(128)S(1)}, s32[8]{0:T(128)}, u32[]{:S(2)}) copy-start(s32[8]{0:T(128)} %param.22) | copy-start | bytes 100
  48.8 21.7 %copy-start.15 = (bf16[1,128,4096]{2,1,0:T(8,128)(2,1)S(1)}, bf16[1,128,4096]{2,1,0:T(8,128)(2,1)}, u32[]{:S(2)}) copy-start(bf16[1,128,4096]{2,1,0:T(8,128)(2,1)} %param.20) | copy-start | bytes 3145732
  49.7 14.7 %collective-permute-start.13 = (bf16[64,4096]{1,0:T(8,128)(2,1)}, bf16[64,4096]{1,0:T(8,128)(2,1)}, u32[]{:S(2)}, u32[]{:S(2)}) collective-permute-start(bf16[64,4096]{1,0:T(8,128)(2,1)} %get-tuple-element.214), channel_id=1, source_target_pairs={{0,2},{2,0},{1,3},{3,1},{4,6},{6,4},{5,7},{7,5},{8,10},{10,8},{9,1... | collective-permute-start | bytes 1572872 | tf_op jit(solution)/shard_map/ppermute | solution.py:182
  50.4 75.4 %copy-start.34 = (f32[4,128]{1,0:T(4,128)}, f32[4,128]{1,0:T(4,128)S(1)}, u32[]{:S(2)}) copy-start(f32[4,128]{1,0:T(4,128)S(1)} %convert_add_fusion) | copy-start | bytes 6148
  51.5 21.5 %copy-start.12 = (bf16[256,1024]{1,0:T(8,128)(2,1)}, bf16[256,1024]{1,0:T(8,128)(2,1)S(1)}, u32[]{:S(2)}) copy-start(bf16[256,1024]{1,0:T(8,128)(2,1)S(1)} %broadcast_select_fusion.1.rest_0_) | copy-start | bytes 1572868
  60.6 14.7 %copy-start.4 = (bf16[128,4096]{1,0:T(8,128)(2,1)}, bf16[128,4096]{1,0:T(8,128)(2,1)S(1)}, u32[]{:S(2)}) copy-start(bf16[128,4096]{1,0:T(8,128)(2,1)S(1)} %collective-permute-done.11.sibling_ref) | copy-start | bytes 3145732
  64.4 14.1 %collective-permute-start.14 = (bf16[256,1024]{1,0:T(8,128)(2,1)S(1)}, bf16[256,1024]{1,0:T(8,128)(2,1)}, u32[]{:S(2)}, u32[]{:S(2)}) collective-permute-start(bf16[256,1024]{1,0:T(8,128)(2,1)S(1)} %broadcast_select_fusion.1.rest_0_), channel_id=1, source_target_pairs={{0,4},{4,0},{8,12},{12,8},{16,20},{20,16},{24,28},{28,24},{1,5},{5... | collective-permute-start | bytes 1572872 | tf_op jit(solution)/shard_map/ppermute | solution.py:182
  65.9 13.4 %collective-permute-start.15 = (bf16[256,1024]{1,0:T(8,128)(2,1)S(1)}, bf16[256,1024]{1,0:T(8,128)(2,1)}, u32[]{:S(2)}, u32[]{:S(2)}) collective-permute-start(bf16[256,1024]{1,0:T(8,128)(2,1)S(1)} %broadcast_select_fusion.1.rest_0_), channel_id=1, source_target_pairs={{0,2},{2,0},{1,3},{3,1},{4,6},{6,4},{5,7},{7,5},{8,10},{10,8},{9,1... | collective-permute-start | bytes 1572872 | tf_op jit(solution)/shard_map/ppermute | solution.py:182
  67.4 9.5 %collective-permute-start.18 = (s32[32]{0:T(128)S(1)}, s32[32]{0:T(128)S(1)}, u32[]{:S(2)}, u32[]{:S(2)}) collective-permute-start(s32[32]{0:T(128)S(1)} %copy-done.37), channel_id=1, source_target_pairs={{0,1},{1,0},{2,3},{3,2},{4,5},{5,4},{6,7},{7,6},{8,9},{9,8},{10,11... | collective-permute-start | bytes 392 | tf_op jit(solution)/shard_map/ppermute | solution.py:182
  71.5 4.0 %copy-start.2 = (bf16[128,4096]{1,0:T(8,128)(2,1)S(1)}, bf16[128,4096]{1,0:T(8,128)(2,1)}, u32[]{:S(2)}) copy-start(bf16[128,4096]{1,0:T(8,128)(2,1)} %get-tuple-element.125.own_ref) | copy-start | bytes 3145732
  71.5 7.0 %collective-permute-start.16 = (bf16[128,2048]{1,0:T(8,128)(2,1)}, bf16[128,2048]{1,0:T(8,128)(2,1)}, u32[]{:S(2)}, u32[]{:S(2)}) collective-permute-start(bf16[128,2048]{1,0:T(8,128)(2,1)} %get-tuple-element.212), channel_id=1, source_target_pairs={{0,1},{1,0},{2,3},{3,2},{4,5},{5,4},{6,7},{7,6},{8,9},{9,8},{10,11... | collective-permute-start | bytes 1572872 | tf_op jit(solution)/shard_map/ppermute | solution.py:182
  73.1 5.4 %collective-permute-start.17 = (bf16[128,2048]{1,0:T(8,128)(2,1)}, bf16[128,2048]{1,0:T(8,128)(2,1)}, u32[]{:S(2)}, u32[]{:S(2)}) collective-permute-start(bf16[128,2048]{1,0:T(8,128)(2,1)} %get-tuple-element.210), channel_id=1, source_target_pairs={{0,1},{1,0},{2,3},{3,2},{4,5},{5,4},{6,7},{7,6},{8,9},{9,8},{10,11... | collective-permute-start | bytes 1572872 | tf_op jit(solution)/shard_map/ppermute | solution.py:182
  79.3 13.8 %collective-permute-start.19 = (bf16[256,1024]{1,0:T(8,128)(2,1)}, bf16[256,1024]{1,0:T(8,128)(2,1)S(1)}, u32[]{:S(2)}, u32[]{:S(2)}) collective-permute-start(bf16[256,1024]{1,0:T(8,128)(2,1)} %broadcast_select_fusion.rest_1_), channel_id=1, source_target_pairs={{0,4},{4,0},{8,12},{12,8},{16,20},{20,16},{24,28},{28,24},{1,5},{5... | collective-permute-start | bytes 1572872 | tf_op jit(solution)/shard_map/ppermute | solution.py:182
  79.8 13.5 %collective-permute-start.20 = (bf16[256,1024]{1,0:T(8,128)(2,1)}, bf16[256,1024]{1,0:T(8,128)(2,1)S(1)}, u32[]{:S(2)}, u32[]{:S(2)}) collective-permute-start(bf16[256,1024]{1,0:T(8,128)(2,1)} %broadcast_select_fusion.rest_1_), channel_id=1, source_target_pairs={{0,2},{2,0},{1,3},{3,1},{4,6},{6,4},{5,7},{7,5},{8,10},{10,8},{9,1... | collective-permute-start | bytes 1572872 | tf_op jit(solution)/shard_map/ppermute | solution.py:182
  83.3 10.6 %copy-start = (bf16[64,4096]{1,0:T(8,128)(2,1)S(1)}, bf16[64,4096]{1,0:T(8,128)(2,1)}, u32[]{:S(2)}) copy-start(bf16[64,4096]{1,0:T(8,128)(2,1)} %add_convert_fusion.1.visual_ref) | copy-start | bytes 1572868
  93.4 16.2 %collective-permute-start.23 = (bf16[8,1024,256]{2,1,0:T(8,128)(2,1)}, bf16[8,1024,256]{2,1,0:T(8,128)(2,1)}, u32[]{:S(2)}, u32[]{:S(2)}) collective-permute-start(bf16[8,1024,256]{2,1,0:T(8,128)(2,1)} %get-tuple-element.150.rest_0_), channel_id=1, source_target_pairs={{0,1},{1,0},{2,3},{3,2},{4,5},{5,4},{6,7},{7,6},{8,9},{9,8},{10,11... | collective-permute-start | bytes 12582920 | tf_op jit(solution)/shard_map/ppermute | solution.py:182
  93.4 14.5 %collective-permute-start.21 = (bf16[256,1024]{1,0:T(8,128)(2,1)}, bf16[256,1024]{1,0:T(8,128)(2,1)S(1)}, u32[]{:S(2)}, u32[]{:S(2)}) collective-permute-start(bf16[256,1024]{1,0:T(8,128)(2,1)} %collective-permute-done.14.rest_2_), channel_id=1, source_target_pairs={{0,2},{2,0},{1,3},{3,1},{4,6},{6,4},{5,7},{7,5},{8,10},{10,8},{9,1... | collective-permute-start | bytes 1572872 | tf_op jit(solution)/shard_map/ppermute | solution.py:182
  94.1 9.2 %collective-permute-start.24 = (f32[320]{0:T(512)S(1)}, f32[320]{0:T(512)S(1)}, u32[]{:S(2)}, u32[]{:S(2)}) collective-permute-start(f32[320]{0:T(512)S(1)} %pad_maximum_fusion.2), channel_id=1, source_target_pairs={{0,1},{1,0},{2,3},{3,2},{4,5},{5,4},{6,7},{7,6},{8,9},{9,8},{10,11... | collective-permute-start | bytes 3848 | tf_op jit(solution)/shard_map/ppermute | solution.py:182
  95.1 15.2 %copy-start.1 = (bf16[64,4096]{1,0:T(8,128)(2,1)S(1)}, bf16[64,4096]{1,0:T(8,128)(2,1)}, u32[]{:S(2)}) copy-start(bf16[64,4096]{1,0:T(8,128)(2,1)} %add_convert_fusion.1.visual_ref) | copy-start | bytes 1572868
  95.1 15.2 %copy-start.3 = (bf16[128,4096]{1,0:T(8,128)(2,1)S(1)}, bf16[128,4096]{1,0:T(8,128)(2,1)}, u32[]{:S(2)}) copy-start(bf16[128,4096]{1,0:T(8,128)(2,1)} %get-tuple-element.125.own_ref) | copy-start | bytes 3145732
  95.1 15.2 %copy-start.5 = (bf16[128,4096]{1,0:T(8,128)(2,1)S(1)}, bf16[128,4096]{1,0:T(8,128)(2,1)}, u32[]{:S(2)}) copy-start(bf16[128,4096]{1,0:T(8,128)(2,1)} %copy-done.4) | copy-start | bytes 3145732
  95.1 15.2 %copy-start.9 = (f32[16,1,256]{2,1,0:T(1,128)S(1)}, f32[16,1,256]{2,1,0:T(1,128)}, u32[]{:S(2)}) copy-start(f32[16,1,256]{2,1,0:T(1,128)} %constant_dynamic-slice_fusion.10) | copy-start | bytes 49156
  95.2 15.2 %copy-start.10 = (s32[17]{0:T(128)S(1)}, s32[17]{0:T(128)}, u32[]{:S(2)}) copy-start(s32[17]{0:T(128)} %stack.93.table_ref) | copy-start | bytes 208
  95.2 12.8 %collective-permute-start.25 = (bf16[32,4096]{1,0:T(8,128)(2,1)S(1)}, bf16[32,4096]{1,0:T(8,128)(2,1)S(1)}, u32[]{:S(2)}, u32[]{:S(2)}) collective-permute-start(bf16[32,4096]{1,0:T(8,128)(2,1)S(1)} %get-tuple-element.216), channel_id=1, source_target_pairs={{0,1},{1,0},{2,3},{3,2},{4,5},{5,4},{6,7},{7,6},{8,9},{9,8},{10,11... | collective-permute-start | bytes 786440 | tf_op jit(solution)/shard_map/ppermute | solution.py:182
  95.5 14.1 %collective-permute-start.22 = (bf16[256,1024]{1,0:T(8,128)(2,1)S(1)}, bf16[256,1024]{1,0:T(8,128)(2,1)S(1)}, u32[]{:S(2)}, u32[]{:S(2)}) collective-permute-start(bf16[256,1024]{1,0:T(8,128)(2,1)S(1)} %collective-permute-done.20.rest_5_), channel_id=1, source_target_pairs={{0,4},{4,0},{8,12},{12,8},{16,20},{20,16},{24,28},{28,24},{1,5},{5... | collective-permute-start | bytes 1572872 | tf_op jit(solution)/shard_map/ppermute | solution.py:182
  107.9 5.2 %copy-start.28 = (bf16[32,4096]{1,0:T(8,128)(2,1)}, bf16[32,4096]{1,0:T(8,128)(2,1)S(1)}, u32[]{:S(2)}) copy-start(bf16[32,4096]{1,0:T(8,128)(2,1)S(1)} %collective-permute-done.25.visual_other_ref) | copy-start | bytes 786436
  113.9 33.2 %copy-start.7 = (bf16[2,1024,256]{2,1,0:T(8,128)(2,1)}, bf16[2,1024,256]{2,1,0:T(8,128)(2,1)S(1)}, u32[]{:S(2)}) copy-start(bf16[2,1024,256]{2,1,0:T(8,128)(2,1)S(1)} %get-tuple-element.174.rest_2_) | copy-start | bytes 3145732
  113.9 1.6 collective-permute-start.26
  115.6 13.5 %collective-permute-start.28 = (bf16[6,1024,256]{2,1,0:T(8,128)(2,1)}, bf16[6,1024,256]{2,1,0:T(8,128)(2,1)}, u32[]{:S(2)}, u32[]{:S(2)}) collective-permute-start(bf16[6,1024,256]{2,1,0:T(8,128)(2,1)} %get-tuple-element.172.rest_1_), channel_id=1, source_target_pairs={{0,1},{1,0},{2,3},{3,2},{4,5},{5,4},{6,7},{7,6},{8,9},{9,8},{10,11... | collective-permute-start | bytes 9437192 | tf_op jit(solution)/shard_map/ppermute | solution.py:182
  115.7 13.4 %collective-permute-start.29 = (bf16[2,1024,256]{2,1,0:T(8,128)(2,1)S(1)}, bf16[2,1024,256]{2,1,0:T(8,128)(2,1)S(1)}, u32[]{:S(2)}, u32[]{:S(2)}) collective-permute-start(bf16[2,1024,256]{2,1,0:T(8,128)(2,1)S(1)} %get-tuple-element.174.rest_2_), channel_id=1, source_target_pairs={{0,1},{1,0},{2,3},{3,2},{4,5},{5,4},{6,7},{7,6},{8,9},{9,8},{10,11... | collective-permute-start | bytes 3145736 | tf_op jit(solution)/shard_map/ppermute | solution.py:182
  118.4 10.7 %collective-permute-start.30 = (bf16[256,512]{1,0:T(8,128)(2,1)}, bf16[256,512]{1,0:T(8,128)(2,1)S(1)}, u32[]{:S(2)}, u32[]{:S(2)}) collective-permute-start(bf16[256,512]{1,0:T(8,128)(2,1)} %get-tuple-element.175.rest_0_), channel_id=1, source_target_pairs={{0,2},{2,0},{1,3},{3,1},{4,6},{6,4},{5,7},{7,5},{8,10},{10,8},{9,1... | collective-permute-start | bytes 786440 | tf_op jit(solution)/shard_map/ppermute | solution.py:182
  120.0 11.9 %all-to-all-start = ((bf16[16,8,640]{2,1,0:T(8,128)(2,1)}), bf16[16,8,640]{2,1,0:T(8,128)(2,1)S(1)}, u32[]{:S(2)}, u32[]{:S(2)}) async-start(bf16[16,8,640]{2,1,0:T(8,128)(2,1)} %bitcast.61), calls=%async_computation | async-start | bytes 327680 | tf_op jit(solution)/shard_map/all_to_all | solution.py:758
  125.7 3.4 %collective-permute-start.27 = (bf16[160,512]{1,0:T(8,128)(2,1)S(1)}, bf16[160,512]{1,0:T(8,128)(2,1)S(1)}, u32[]{:S(2)}, u32[]{:S(2)}) collective-permute-start(bf16[160,512]{1,0:T(8,128)(2,1)S(1)} %pad_maximum_fusion.1), channel_id=1, source_target_pairs={{0,1},{1,0},{2,3},{3,2},{4,5},{5,4},{6,7},{7,6},{8,9},{9,8},{10,11... | collective-permute-start | bytes 491528 | tf_op jit(solution)/shard_map/ppermute | solution.py:182
  129.1 35.9 %copy-start.31 = (bf16[160,512]{1,0:T(8,128)(2,1)}, bf16[160,512]{1,0:T(8,128)(2,1)S(1)}, u32[]{:S(2)}) copy-start(bf16[160,512]{1,0:T(8,128)(2,1)S(1)} %collective-permute-done.27.pair_other_ref) | copy-start | bytes 491524
  129.1 26.2 %copy-start.13 = (bf16[2,1024,256]{2,1,0:T(8,128)(2,1)}, bf16[2,1024,256]{2,1,0:T(8,128)(2,1)S(1)}, u32[]{:S(2)}) copy-start(bf16[2,1024,256]{2,1,0:T(8,128)(2,1)S(1)} %collective-permute-done.29.rest_5_) | copy-start | bytes 3145732
  147.1 8.1 %copy-start.20 = (bf16[128,2048]{1,0:T(8,128)(2,1)S(1)}, bf16[128,2048]{1,0:T(8,128)(2,1)}, u32[]{:S(2)}) copy-start(bf16[128,2048]{1,0:T(8,128)(2,1)} %get-tuple-element.177) | copy-start | bytes 1572868
  147.1 5.7 %collective-permute-start.32 = (bf16[128,2048]{1,0:T(8,128)(2,1)}, bf16[128,2048]{1,0:T(8,128)(2,1)S(1)}, u32[]{:S(2)}, u32[]{:S(2)}) collective-permute-start(bf16[128,2048]{1,0:T(8,128)(2,1)} %get-tuple-element.180), channel_id=1, source_target_pairs={{0,1},{1,0},{2,3},{3,2},{4,5},{5,4},{6,7},{7,6},{8,9},{9,8},{10,11... | collective-permute-start | bytes 1572872 | tf_op jit(solution)/shard_map/ppermute | solution.py:182
  147.2 8.1 %collective-permute-start.31 = (bf16[128,2048]{1,0:T(8,128)(2,1)}, bf16[128,2048]{1,0:T(8,128)(2,1)S(1)}, u32[]{:S(2)}, u32[]{:S(2)}) collective-permute-start(bf16[128,2048]{1,0:T(8,128)(2,1)} %get-tuple-element.178), channel_id=1, source_target_pairs={{0,1},{1,0},{2,3},{3,2},{4,5},{5,4},{6,7},{7,6},{8,9},{9,8},{10,11... | collective-permute-start | bytes 1572872 | tf_op jit(solution)/shard_map/ppermute | solution.py:182
  147.7 12.9 %collective-permute-start.33 = (bf16[256,512]{1,0:T(8,128)(2,1)}, bf16[256,512]{1,0:T(8,128)(2,1)S(1)}, u32[]{:S(2)}, u32[]{:S(2)}) collective-permute-start(bf16[256,512]{1,0:T(8,128)(2,1)} %get-tuple-element.185), channel_id=1, source_target_pairs={{0,2},{2,0},{1,3},{3,1},{4,6},{6,4},{5,7},{7,5},{8,10},{10,8},{9,1... | collective-permute-start | bytes 786440 | tf_op jit(solution)/shard_map/ppermute | solution.py:182
  148.9 11.7 %all-to-all-start.1 = ((bf16[16,8,512]{2,1,0:T(8,128)(2,1)}), bf16[16,8,512]{2,1,0:T(8,128)(2,1)S(1)}, u32[]{:S(2)}, u32[]{:S(2)}) async-start(bf16[16,8,512]{2,1,0:T(8,128)(2,1)} %bitcast.63), calls=%async_computation.1 | async-start | bytes 262144 | tf_op jit(solution)/shard_map/all_to_all | solution.py:758
  163.4 1.6 collective-permute-start.34
  (12 other events, 21.9 us)

commit v4 on v3

--- a/solution.py
+++ b/solution.py
@@ -240,6 +240,45 @@
     )(core, values)
 
 
+def up_projection(patches, gain, weight):
+    rows, depth = patches.shape
+    vector = gain.shape[1]
+    width = weight.shape[1]
+    count = depth // vector
+
+    def kernel(patch_ref, gain_ref, weight_ref, out_ref, buffers, sems):
+        copies = [
+            pltpu.make_async_copy(weight_ref.at[j * vector : (j + 1) * vector], buffers.at[j], sems.at[j])
+            for j in range(count)
+        ]
+        for copy in copies:
+            copy.start()
+        total = jnp.zeros((rows, width), jnp.float32)
+        for j in range(count):
+            center = patch_ref[:, j * vector : (j + 1) * vector].astype(jnp.float32)
+            center = center - jnp.mean(center, axis=1, keepdims=True)
+            spread = jnp.mean(center * center, axis=1, keepdims=True)
+            normed = (center * lax.rsqrt(spread + epsilon) * gain_ref[...]).astype(jnp.bfloat16)
+            copies[j].wait()
+            total = total + jnp.dot(normed, buffers[j], preferred_element_type=jnp.float32)
+        out_ref[...] = (0.5 * total * (1.0 + lax.erf(total * math.sqrt(0.5)))).astype(jnp.bfloat16)
+
+    vmem = pl.BlockSpec(memory_space=pltpu.VMEM)
+    return pl.pallas_call(
+        kernel,
+        in_specs=[vmem, vmem, pl.BlockSpec(memory_space=pl.ANY)],
+        out_specs=vmem,
+        out_shape=jax.ShapeDtypeStruct((rows, width), jnp.bfloat16),
+        scratch_shapes=[
+            pltpu.VMEM((count, vector, width), jnp.bfloat16),
+            pltpu.SemaphoreType.DMA((count,)),
+        ],
+        compiler_params=vmem_params(56),
+        cost_estimate=brief(),
+        name="merge_up",
+    )(patches, gain, weight)
+
+
 def down_halves(inner_hidden, merge_down, core, block):
     rows, depth = inner_hidden.shape
     width = merge_down.shape[1]
@@ -363,7 +402,7 @@
     slots, tokens = picking.shape
 
     def kernel(mine_ref, received_ref, scale_ref, codes_ref, picking_ref, chip_ref, token_ref, slot_ref):
-        pairs = (mine_ref[...] + received_ref[...].astype(jnp.float32)) * scale_ref[:, :1]
+        pairs = (mine_ref[...] + received_ref[...].astype(jnp.float32)) * jnp.broadcast_to(scale_ref[...], (128, total)).T[:, :1]
         pairs = pairs.astype(jnp.bfloat16)
         chip_ref[...] = pairs[: 2 * rows]
         token_ref[...] = pairs[2 * rows :]
@@ -448,6 +487,7 @@
             high = min(size, low + 4)
             groups.append((piece, low, high, first + low))
         first += size
+    groups = groups[-1:] + groups[:-1]
 
     def kernel(
         table_ref, grad_ref, grad_other_ref, pair_ref, pair_other_ref, text_ref, visual_ref, visual_other_ref,
@@ -680,17 +720,7 @@
 
     beside0, below0 = both(kv_weight)
     far1, across = line(kv_weight, swapped), line(kv_weight, middle)
-    vectors = []
-    for j in range(patches.shape[1] // vit_gain.shape[0]):
-        piece = lax.slice_in_dim(patches, j * vit_gain.shape[0], (j + 1) * vit_gain.shape[0], axis=1)
-        center = piece.astype(f32)
-        center = center - jnp.mean(center, axis=-1, keepdims=True)
-        spread = jnp.mean(center * center, axis=-1, keepdims=True)
-        vectors.append((center * lax.rsqrt(spread + epsilon) * vit_gain).astype(bf16))
-    normed = jnp.concatenate(vectors, axis=1)
-    inner_hidden = jax.nn.gelu(
-        jnp.dot(normed, merge_up, preferred_element_type=f32), approximate=False
-    ).astype(bf16)
+    inner_hidden = up_projection(patches, vit_gain[None, :], merge_up)
     rows_in = text[0]
     beside0, below0, far1, across, inner_hidden, rows_in, core_word, table, gain = close(
         (beside0, below0, far1, across, inner_hidden, rows_in, core_word, table, gain)
@@ -792,7 +822,7 @@
     arrived = swap(jnp.concatenate([sibling_squares, own_squares, visual_squares]))
     square = jnp.concatenate([own_squares, sibling_squares, visual_squares]) + arrived
     scale = lax.rsqrt(square / width + epsilon)[:, None]
-    wide_scale = jnp.broadcast_to(scale, (scale.shape[0], 128))
+    wide_scale = scale.reshape(1, -1)
     own_visual, other_visual = of_core(visual, core), swap(of_core(visual, 1 - core))
     own_scale = jnp.concatenate([scale[:rows], of_core(scale[2 * rows :], core)], axis=0)
     corner2, corner3, part1, sums, other0, wide_scale, own_visual, other_visual, own_scale = close(

time: 177 us -> 176 us (level)
  matrix products: 6.22 us -> 0 us
  Pallas kernels: 55.1 us -> 60.9 us
  other arithmetic: 17.5 us -> 14 us
  waiting for transfers between devices: 41.2 us -> 43.2 us
    dot_general x1 -> x0, matrix products: 6.22 us -> none  [local_fast(): jnp.dot(normed, merge_up, preferred_element_type=f32)]
    pallas_call x0 -> x1, Pallas kernels: none -> 5.88 us  [up_projection(): pl.pallas_call(kernel, in_specs=[vmem, vmem, pl.BlockSpec(memory_space=pl...]
    reduce_sum x2 -> x0, other arithmetic: 2 us -> none  [the longest x1 1.52 us: local_fast(): center = center - jnp.mean(center, axis=-1, keepdims=True)]
    unnamed x78 -> x74, local copies, waits for them, and re-layouts: 4.56 us -> 4.53 us
  transfers between devices with their start and end apart: 37 -> 37, of which waited for: 16 -> 17; matrix products, arithmetic and copies ran while one was open for 21% -> 17% of each run, Pallas kernels for 15% -> 18%
where the time goes in v4:
time: 176 us; the launch traced here: 175 us
  Pallas kernels  60.9 us (35%)
  waiting for transfers between devices  43.2 us (25%)
  starting transfers between devices  35.5 us (20%)
  local copies, waits for them, and re-layouts  20.4 us (12%)
  other arithmetic  14 us (8%)
    ppermute x30, starting transfers between devices, neighbor(): return lax.ppermute(values, axis, [(d, d ^ offset) for d in range(count)])  21.5 us
    ppermute x30, waiting for transfers between devices, neighbor(): return lax.ppermute(values, axis, [(d, d ^ offset) for d in range(count)])  21.1 us
    ppermute x5, waiting for transfers between devices, line(): lax.ppermute(values, 'dp', [(2 * p + low, 2 * q + low) for p, q in pairs...  15.3 us
    pallas_call x1, Pallas kernels, attend_pair(): pl.pallas_call(kernel, grid=(steps,), in_specs=[part] * 4 + [vmem] * (7 +...  14.6 us
    pallas_call x3, Pallas kernels, project(): pl.pallas_call(kernel, in_specs=[smem()] + [vmem] * (4 + size + len(earli...  14.2 us
    pallas_call x1, Pallas kernels, project_back(): pl.pallas_call(kernel, in_specs=[smem()] + [vmem] * 10 + [pl.BlockSpec(me...  10.5 us
    all_to_all x2, starting transfers between devices, between_chips(): lax.all_to_all(shaped, ('dp', 'y'), split_axis=0, concat_axis=0, tiled=True)  7.62 us
    pallas_call x1, Pallas kernels, down_halves(): pl.pallas_call(kernel, in_specs=[smem(), vmem, pl.BlockSpec(memory_space=...  7.41 us
  transfers between devices with their start and end apart: 37, of which 17 were waited for; matrix products, arithmetic and copies ran while one was open for 17% of the time, Pallas kernels for 18%

profile of v4, /device:TPU:0, one launch (start us, length us, event | category | flops | bytes accessed | tf_op | source)
XLA Modules:
  0.0 175.4 jit_solution(10383803610396468954)
XLA Ops:
  0.6 3.0 %collective-permute-start = (bf16[256,1024]{1,0:T(8,128)(2,1)}, bf16[256,1024]{1,0:T(8,128)(2,1)}, u32[]{:S(2)}, u32[]{:S(2)}) collective-permute-start(bf16[256,1024]{1,0:T(8,128)(2,1)} %rest_0_.1), channel_id=1, source_target_pairs={{0,4},{4,0},{8,12},{12,8},{16,20},{20,16},{24,28},{28,24},{1,5},{5... | collective-permute-start | bytes 1572872 | tf_op jit(solution)/shard_map/ppermute | solution.py:182
  3.6 1.5 collective-permute-start.1
  5.2 1.6 collective-permute-start.2
  7.4 1.3 broadcast_in_dim.77.gain_ref
  8.7 5.9 %merge_up.1.hidden_ref = bf16[128,768]{1,0:T(8,128)(2,1)} custom-call(bf16[128,5120]{1,0:T(8,128)(2,1)} %patch_ref.1, f32[1,1280]{1,0:T(1,128)} %broadcast_in_dim.77.gain_ref, bf16[5120,768]{1,0:T(8,128)(2,1)} %weight_ref.2), custom_call_target="tpu_custom_call" | custom-call | flops 1 | bytes 1 | tf_op jit(solution)/shard_map/merge_up/pallas_call | solution.py:267
  14.7 0.7 stack.93.table_ref
  16.0 1.2 collective-permute-done.1.rest_4_
  17.2 1.2 collective-permute-done.2.rest_1_
  19.4 1.4 collective-permute-start.7
  20.9 1.3 collective-permute-start.8
  22.2 7.4 %merge_down.1 = (bf16[128,4096]{1,0:T(8,128)(2,1)}, bf16[128,4096]{1,0:T(8,128)(2,1)}) custom-call(s32[1]{0:T(128)} %bitcast.1.core_ref, bf16[128,768]{1,0:T(8,128)(2,1)} %merge_up.1.hidden_ref, bf16[768,8192]{1,0:T(8,128)(2,1)} %weight_ref.3), custom_call_target="tpu_custom_call" | custom-call | flops 1 | bytes 1 | tf_op jit(solution)/shard_map/merge_down/pallas_call | solution.py:305
  29.6 1.1 collective-permute-done.5.rest_3_
  31.2 7.2 %collective-permute-done.8 = bf16[256,1024]{1,0:T(8,128)(2,1)S(1)} collective-permute-done((bf16[256,1024]{1,0:T(8,128)(2,1)S(1)}, bf16[256,1024]{1,0:T(8,128)(2,1)S(1)}, u32[]{:S(2)}, u32[]{:S(2)}) %collective-permute-start.8) | collective-permute-done | bytes 524320 | tf_op jit(solution)/shard_map/ppermute | solution.py:697
  38.5 1.6 collective-permute-start.4
  40.1 3.9 %split_halves.1 = (bf16[128,4096]{1,0:T(8,128)(2,1)}, bf16[128,4096]{1,0:T(8,128)(2,1)}) custom-call(s32[1]{0:T(128)} %bitcast.1.core_ref, bf16[128,8192]{1,0:T(8,128)(2,1)} %bitcast.52), custom_call_target="tpu_custom_call" | custom-call | flops 1 | bytes 1 | tf_op jit(solution)/shard_map/split_halves/pallas_call | solution.py:231
  44.2 1.5 collective-permute-start.10
  45.6 1.6 collective-permute-start.9
  47.2 1.5 add_convert_fusion
  48.7 0.9 constant_dynamic-slice_fusion.8
  50.3 1.1 broadcast_select_fusion.1.rest_0_
  51.5 2.1 %collective-permute-done.4.rest_6_ = bf16[256,1024]{1,0:T(8,128)(2,1)} collective-permute-done((bf16[256,1024]{1,0:T(8,128)(2,1)}, bf16[256,1024]{1,0:T(8,128)(2,1)}, u32[]{:S(2)}, u32[]{:S(2)}) %collective-permute-start.4) | collective-permute-done | bytes 524320 | tf_op jit(solution)/shard_map/ppermute | solution.py:182
  53.6 6.9 %collective-permute-done.10 = bf16[256,1024]{1,0:T(8,128)(2,1)} collective-permute-done((bf16[256,1024]{1,0:T(8,128)(2,1)}, bf16[256,1024]{1,0:T(8,128)(2,1)}, u32[]{:S(2)}, u32[]{:S(2)}) %collective-permute-start.10) | collective-permute-done | bytes 524320 | tf_op jit(solution)/shard_map/ppermute | solution.py:697
  60.5 3.9 %collective-permute-done.13 = bf16[64,4096]{1,0:T(8,128)(2,1)} collective-permute-done((bf16[64,4096]{1,0:T(8,128)(2,1)}, bf16[64,4096]{1,0:T(8,128)(2,1)}, u32[]{:S(2)}, u32[]{:S(2)}) %collective-permute-start.13) | collective-permute-done | bytes 524320 | tf_op jit(solution)/shard_map/ppermute | solution.py:182
  64.4 1.5 collective-permute-start.14
  65.9 1.5 collective-permute-start.15
  70.5 1.0 constant_dynamic-slice_fusion.6
  72.0 1.0 constant_dynamic-slice_fusion.4
  73.1 1.9 %broadcast_select_fusion.rest_1_ = bf16[256,1024]{1,0:T(8,128)(2,1)} fusion(bf16[256,1024]{1,0:T(8,128)(2,1)} %collective-permute-done.7, bf16[256,1024]{1,0:T(8,128)(2,1)} %collective-permute-done.10, pred[]{:T(512)S(6)} %or.3), kind=kLoop, calls=%fused_computation.10 | loop fusion | flops 262144 | bytes 1572865 | tf_op jit(solution)/shard_map/jit(_where)/select_n | solution.py:758
  77.0 0.7 select_convert_fusion.codes_ref
  77.7 0.7 and_convert_fusion.picking_ref
  78.4 0.9 collective-permute-done.15.rest_4_
  79.8 1.5 collective-permute-start.20
  81.3 2.0 %add_convert_fusion.1.visual_ref = bf16[64,4096]{1,0:T(8,128)(2,1)} fusion(bf16[64,4096]{1,0:T(8,128)(2,1)} %collective-permute-done.13, bf16[64,4096]{1,0:T(8,128)(2,1)S(1)} %get-tuple-element.133), kind=kLoop, calls=%fused_computation.9 | loop fusion | flops 1048576 | bytes 1572864 | tf_op jit(solution)/shard_map/convert_element_type | solution.py:812
  83.3 6.6 %project_pairs.3 = (bf16[8,1024,256]{2,1,0:T(8,128)(2,1)}, f32[320,1024]{1,0:T(8,128)}) custom-call(s32[17]{0:T(128)} %stack.93.table_ref, bf16[128,4096]{1,0:T(8,128)(2,1)} %get-tuple-element.125.own_ref, bf16[128,4096]{1,0:T(8,128)(2,1)} %copy-done.4, bf16[64,4096]{1,0:T(8,128)(2,1)} %add_convert_fusion.1.visual_ref, f32[1,4096]{1,0:T(1,128)} %bitcast.49, ...), custom_call_target="tpu_custom_call" | custom-call | flops 1 | bytes 1 | tf_op jit(solution)/shard_map/project_pairs/pallas_call | solution.py:388
  89.9 3.1 %collective-permute-done.19.rest_3_ = bf16[256,1024]{1,0:T(8,128)(2,1)S(1)} collective-permute-done((bf16[256,1024]{1,0:T(8,128)(2,1)}, bf16[256,1024]{1,0:T(8,128)(2,1)S(1)}, u32[]{:S(2)}, u32[]{:S(2)}) %collective-permute-start.19) | collective-permute-done | bytes 524320 | tf_op jit(solution)/shard_map/ppermute | solution.py:182
  94.3 0.7 constant_dynamic-slice_fusion.2
  95.4 1.5 collective-permute-start.22
  96.9 6.3 %project_pairs.4 = (bf16[6,1024,256]{2,1,0:T(8,128)(2,1)}, f32[320,1024]{1,0:T(8,128)}) custom-call(s32[17]{0:T(128)} %stack.93.table_ref, bf16[128,4096]{1,0:T(8,128)(2,1)} %get-tuple-element.125.own_ref, bf16[128,4096]{1,0:T(8,128)(2,1)} %copy-done.4, bf16[64,4096]{1,0:T(8,128)(2,1)} %add_convert_fusion.1.visual_ref, f32[1,4096]{1,0:T(1,128)} %bitcast.50, ...), custom_call_target="tpu_custom_call" | custom-call | flops 1 | bytes 1 | tf_op jit(solution)/shard_map/project_pairs/pallas_call | solution.py:388
  103.9 3.9 %collective-permute-done.21.rest_0_ = bf16[256,1024]{1,0:T(8,128)(2,1)S(1)} collective-permute-done((bf16[256,1024]{1,0:T(8,128)(2,1)}, bf16[256,1024]{1,0:T(8,128)(2,1)S(1)}, u32[]{:S(2)}, u32[]{:S(2)}) %collective-permute-start.21) | collective-permute-done | bytes 524320 | tf_op jit(solution)/shard_map/ppermute | solution.py:182
  107.8 1.6 collective-permute-done.22.rest_1_
  109.5 1.3 copy-done.6
  110.8 1.4 project_pairs.5
  112.2 0.8 copy-done.8
  113.1 1.6 collective-permute-done.26.received_ref
  115.4 2.3 %finish_pairs.1 = (bf16[256,512]{1,0:T(8,128)(2,1)}, bf16[64,512]{1,0:T(8,128)(2,1)}, bf16[128,640]{1,0:T(8,128)(2,1)}) custom-call(f32[320,512]{1,0:T(8,128)} %copy-done.8, bf16[320,512]{1,0:T(8,128)(2,1)} %copy-done.26, f32[1,320]{1,0:T(1,128)} %reshape_broadcast_in_dim.3.scale_ref, bf16[64,128]{1,0:T(8,128)(2,1)} %select_convert_fusion.codes_ref, ...), custom_call_target="tpu_custom_call" | custom-call | flops 1 | bytes 1 | tf_op jit(solution)/shard_map/finish_pairs/pallas_call | solution.py:418
  117.7 1.5 collective-permute-start.30
  119.2 3.8 %all-to-all-start = ((bf16[16,8,640]{2,1,0:T(8,128)(2,1)}), bf16[16,8,640]{2,1,0:T(8,128)(2,1)S(1)}, u32[]{:S(2)}, u32[]{:S(2)}) async-start(bf16[16,8,640]{2,1,0:T(8,128)(2,1)} %bitcast.60), calls=%async_computation | async-start | bytes 327680 | tf_op jit(solution)/shard_map/all_to_all | solution.py:788
  123.0 1.0 fusion.7
  124.0 0.8 constant_dynamic-slice_fusion
  124.9 0.9 copy.23.row_s
  125.8 0.9 copy.24.pos_ref
  126.6 0.8 copy.25.doc_ref
  127.5 0.7 pad_maximum_fusion.pair_ref
  128.2 2.7 %all-to-all-done = bf16[16,8,640]{2,1,0:T(8,128)(2,1)S(1)} async-done(((bf16[16,8,640]{2,1,0:T(8,128)(2,1)}), bf16[16,8,640]{2,1,0:T(8,128)(2,1)S(1)}, u32[]{:S(2)}, u32[]{:S(2)}) %all-to-all-start) | async-done | bytes 163872 | tf_op jit(solution)/shard_map/all_to_all | solution.py:788
  131.6 14.6 %attend.1 = (bf16[128,2048]{1,0:T(8,128)(2,1)}, bf16[128,2048]{1,0:T(8,128)(2,1)}, bf16[128,2048]{1,0:T(8,128)(2,1)}, bf16[128,2048]{1,0:T(8,128)(2,1)}, bf16[25...) custom-call(bf16[128,2048]{1,0:T(8,128)(2,1)} %get-tuple-element.127.qa, ...), custom_call_target="tpu_custom_call" | custom-call | flops 1 | bytes 1 | tf_op jit(solution)/shard_map/attend/pallas_call | solution.py:657
  146.8 1.2 collective-permute-start.33
  148.0 3.8 %all-to-all-start.1 = ((bf16[16,8,512]{2,1,0:T(8,128)(2,1)}), bf16[16,8,512]{2,1,0:T(8,128)(2,1)S(1)}, u32[]{:S(2)}, u32[]{:S(2)}) async-start(bf16[16,8,512]{2,1,0:T(8,128)(2,1)} %bitcast.62), calls=%async_computation.1 | async-start | bytes 262144 | tf_op jit(solution)/shard_map/all_to_all | solution.py:788
  151.8 2.5 %maximum_select_fusion.1 = bf16[128,4096]{1,0:T(8,128)(2,1)} fusion(bf16[128,2048]{1,0:T(8,128)(2,1)S(1)} %collective-permute-done.32, bf16[128,2048]{1,0:T(8,128)(2,1)} %get-tuple-element.179, pred[]{:T(512)S(6)} %eq.81), kind=kLoop, calls=%fused_computation.7 | loop fusion | flops 4718592 | bytes 2097153 | tf_op jit(solution)/shard_map/jit(_where)/select_n | solution.py:850
  154.3 1.2 maximum_select_fusion
  155.5 4.1 %all-to-all-done.1 = bf16[16,8,512]{2,1,0:T(8,128)(2,1)S(1)} async-done(((bf16[16,8,512]{2,1,0:T(8,128)(2,1)}), bf16[16,8,512]{2,1,0:T(8,128)(2,1)S(1)}, u32[]{:S(2)}, u32[]{:S(2)}) %all-to-all-start.1) | async-done | bytes 131104 | tf_op jit(solution)/shard_map/all_to_all | solution.py:788
  160.4 2.1 %sum_grads.1 = (bf16[160,512]{1,0:T(8,128)(2,1)}, bf16[160,512]{1,0:T(8,128)(2,1)}) custom-call(s32[1]{0:T(128)} %bitcast.1.core_ref, bf16[256,512]{1,0:T(8,128)(2,1)} %get-tuple-element.183.grad_ref, bf16[128,512]{1,0:T(8,128)(2,1)} %bitcast.59, bf16[128,64]{1,0:T(8,128)(2,1)} %and_convert_fusion.picking_ref, bf16[256,512]{1,0:T(8,128)(2,1)} %copy-done.28), custom_call_target="tpu_custom_call" | custom-call | flops 1 | bytes 1 | tf_op jit(solution)/shard_map/sum_grads/pallas_call | solution.py:461
  162.5 0.8 copy.26.scale_ref
  163.2 0.9 collective-permute-done.34.grad_other_ref
  164.7 10.5 %project_back.1 = (bf16[128,8192]{1,0:T(8,128)(2,1)}, bf16[32,8192]{1,0:T(8,128)(2,1)}) custom-call(s32[17]{0:T(128)} %stack.93.table_ref, bf16[160,512]{1,0:T(8,128)(2,1)} %get-tuple-element.186.grad_ref, bf16[160,512]{1,0:T(8,128)(2,1)} %copy-done.31, bf16[160,512]{1,0:T(8,128)(2,1)} %pad_maximum_fusion.pair_ref, bf16[160,512]{1,0:T(8,128)(2,1)} %copy-done.30, ...), custom_call_target="tpu_custom_call" | custom-call | flops 1 | bytes 1 | tf_op jit(solution)/shard_map/project_back/pallas_call | solution.py:558
  (153 shorter events, 15.8 us)
Async XLA Ops:
  0.6 15.4 %collective-permute-start = (bf16[256,1024]{1,0:T(8,128)(2,1)}, bf16[256,1024]{1,0:T(8,128)(2,1)}, u32[]{:S(2)}, u32[]{:S(2)}) collective-permute-start(bf16[256,1024]{1,0:T(8,128)(2,1)} %rest_0_.1), channel_id=1, source_target_pairs={{0,4},{4,0},{8,12},{12,8},{16,20},{20,16},{24,28},{28,24},{1,5},{5... | collective-permute-start | bytes 1572872 | tf_op jit(solution)/shard_map/ppermute | solution.py:182
  3.6 13.6 %collective-permute-start.1 = (bf16[256,1024]{1,0:T(8,128)(2,1)}, bf16[256,1024]{1,0:T(8,128)(2,1)S(1)}, u32[]{:S(2)}, u32[]{:S(2)}) collective-permute-start(bf16[256,1024]{1,0:T(8,128)(2,1)} %rest_0_.1), channel_id=1, source_target_pairs={{0,2},{2,0},{1,3},{3,1},{4,6},{6,4},{5,7},{7,5},{8,10},{10,8},{9,1... | collective-permute-start | bytes 1572872 | tf_op jit(solution)/shard_map/ppermute | solution.py:182
  5.2 13.3 %collective-permute-start.2 = (bf16[256,1024]{1,0:T(8,128)(2,1)}, bf16[256,1024]{1,0:T(8,128)(2,1)S(1)}, u32[]{:S(2)}, u32[]{:S(2)}) collective-permute-start(bf16[256,1024]{1,0:T(8,128)(2,1)} %rest_0_.1), channel_id=1, source_target_pairs={{0,8},{4,12},{8,0},{12,4},{16,24},{20,28},{24,16},{28,20},{1,9},{5... | collective-permute-start | bytes 1572872 | tf_op jit(solution)/shard_map/ppermute | solution.py:697
  6.7 11.7 %collective-permute-start.3 = (bf16[256,1024]{1,0:T(8,128)(2,1)}, bf16[256,1024]{1,0:T(8,128)(2,1)S(1)}, u32[]{:S(2)}, u32[]{:S(2)}) collective-permute-start(bf16[256,1024]{1,0:T(8,128)(2,1)} %rest_0_.1), channel_id=1, source_target_pairs={{8,16},{12,20},{16,8},{20,12},{9,17},{13,21},{17,9},{21,13},{10,18... | collective-permute-start | bytes 1572872 | tf_op jit(solution)/shard_map/ppermute | solution.py:697
  8.7 6.0 %copy-start.32 = (f32[8192]{0:T(1024)S(1)}, f32[8192]{0:T(1024)}, u32[]{:S(2)}) copy-start(f32[8192]{0:T(1024)} %param.18) | copy-start | bytes 98308
  18.5 11.1 %copy-start.24 = (bf16[256,1024]{1,0:T(8,128)(2,1)}, bf16[256,1024]{1,0:T(8,128)(2,1)S(1)}, u32[]{:S(2)}) copy-start(bf16[256,1024]{1,0:T(8,128)(2,1)S(1)} %collective-permute-done.2.rest_1_) | copy-start | bytes 1572868
  18.5 11.1 %copy-start.20 = (bf16[256,1024]{1,0:T(8,128)(2,1)}, bf16[256,1024]{1,0:T(8,128)(2,1)S(1)}, u32[]{:S(2)}) copy-start(bf16[256,1024]{1,0:T(8,128)(2,1)S(1)} %collective-permute-done.3) | copy-start | bytes 1572868
  18.5 12.2 %collective-permute-start.5 = (bf16[256,1024]{1,0:T(8,128)(2,1)S(1)}, bf16[256,1024]{1,0:T(8,128)(2,1)S(1)}, u32[]{:S(2)}, u32[]{:S(2)}) collective-permute-start(bf16[256,1024]{1,0:T(8,128)(2,1)S(1)} %collective-permute-done.2.rest_1_), channel_id=1, source_target_pairs={{0,4},{4,0},{8,12},{12,8},{16,20},{20,16},{24,28},{28,24},{1,5},{5... | collective-permute-start | bytes 1572872 | tf_op jit(solution)/shard_map/ppermute | solution.py:182
  19.1 12.1 %collective-permute-start.6 = (bf16[256,1024]{1,0:T(8,128)(2,1)S(1)}, bf16[256,1024]{1,0:T(8,128)(2,1)}, u32[]{:S(2)}, u32[]{:S(2)}) collective-permute-start(bf16[256,1024]{1,0:T(8,128)(2,1)S(1)} %collective-permute-done.2.rest_1_), channel_id=1, source_target_pairs={{0,2},{2,0},{1,3},{3,1},{4,6},{6,4},{5,7},{7,5},{8,10},{10,8},{9,1... | collective-permute-start | bytes 1572872 | tf_op jit(solution)/shard_map/ppermute | solution.py:182
  19.4 11.7 %collective-permute-start.7 = (bf16[256,1024]{1,0:T(8,128)(2,1)S(1)}, bf16[256,1024]{1,0:T(8,128)(2,1)}, u32[]{:S(2)}, u32[]{:S(2)}) collective-permute-start(bf16[256,1024]{1,0:T(8,128)(2,1)S(1)} %collective-permute-done.2.rest_1_), channel_id=1, source_target_pairs={{8,16},{12,20},{16,8},{20,12},{9,17},{13,21},{17,9},{21,13},{10,18... | collective-permute-start | bytes 1572872 | tf_op jit(solution)/shard_map/ppermute | solution.py:697
  20.9 17.5 %collective-permute-start.8 = (bf16[256,1024]{1,0:T(8,128)(2,1)S(1)}, bf16[256,1024]{1,0:T(8,128)(2,1)S(1)}, u32[]{:S(2)}, u32[]{:S(2)}) collective-permute-start(bf16[256,1024]{1,0:T(8,128)(2,1)S(1)} %collective-permute-done.3), channel_id=1, source_target_pairs={{8,0},{12,4},{16,24},{20,28},{9,1},{13,5},{17,25},{21,29},{10,2},{... | collective-permute-start | bytes 1572872 | tf_op jit(solution)/shard_map/ppermute | solution.py:697
  29.6 17.6 %copy-start.13 = (bf16[128,4096]{1,0:T(8,128)(2,1)S(1)}, bf16[128,4096]{1,0:T(8,128)(2,1)}, u32[]{:S(2)}) copy-start(bf16[128,4096]{1,0:T(8,128)(2,1)} %get-tuple-element.114) | copy-start | bytes 3145732
  30.7 7.6 %copy-start.25 = (bf16[256,1024]{1,0:T(8,128)(2,1)}, bf16[256,1024]{1,0:T(8,128)(2,1)S(1)}, u32[]{:S(2)}) copy-start(bf16[256,1024]{1,0:T(8,128)(2,1)S(1)} %collective-permute-done.5.rest_3_) | copy-start | bytes 1572868
  38.3 5.6 %copy-start.21 = (bf16[256,1024]{1,0:T(8,128)(2,1)}, bf16[256,1024]{1,0:T(8,128)(2,1)S(1)}, u32[]{:S(2)}) copy-start(bf16[256,1024]{1,0:T(8,128)(2,1)S(1)} %collective-permute-done.8) | copy-start | bytes 1572868
  38.4 8.8 %collective-permute-start.12 = (bf16[128,4096]{1,0:T(8,128)(2,1)}, bf16[128,4096]{1,0:T(8,128)(2,1)}, u32[]{:S(2)}, u32[]{:S(2)}) collective-permute-start(bf16[128,4096]{1,0:T(8,128)(2,1)} %get-tuple-element.115), channel_id=1, source_target_pairs={{0,1},{1,0},{2,3},{3,2},{4,5},{5,4},{6,7},{7,6},{8,9},{9,8},{10,11... | collective-permute-start | bytes 3145736 | tf_op jit(solution)/shard_map/ppermute | solution.py:182
  38.5 15.1 %collective-permute-start.4 = (bf16[256,1024]{1,0:T(8,128)(2,1)}, bf16[256,1024]{1,0:T(8,128)(2,1)}, u32[]{:S(2)}, u32[]{:S(2)}) collective-permute-start(bf16[256,1024]{1,0:T(8,128)(2,1)} %collective-permute-done.rest_2_), channel_id=1, source_target_pairs={{0,2},{2,0},{1,3},{3,1},{4,6},{6,4},{5,7},{7,5},{8,10},{10,8},{9,1... | collective-permute-start | bytes 1572872 | tf_op jit(solution)/shard_map/ppermute | solution.py:182
  44.0 16.5 %collective-permute-start.11 = (bf16[128,4096]{1,0:T(8,128)(2,1)}, bf16[128,4096]{1,0:T(8,128)(2,1)S(1)}, u32[]{:S(2)}, u32[]{:S(2)}) collective-permute-start(bf16[128,4096]{1,0:T(8,128)(2,1)} %get-tuple-element.112), channel_id=1, source_target_pairs={{0,1},{1,0},{2,3},{3,2},{4,5},{5,4},{6,7},{7,6},{8,9},{9,8},{10,11... | collective-permute-start | bytes 3145736 | tf_op jit(solution)/shard_map/ppermute | solution.py:182
  44.2 16.3 %collective-permute-start.10 = (bf16[256,1024]{1,0:T(8,128)(2,1)}, bf16[256,1024]{1,0:T(8,128)(2,1)}, u32[]{:S(2)}, u32[]{:S(2)}) collective-permute-start(bf16[256,1024]{1,0:T(8,128)(2,1)} %collective-permute-done.7), channel_id=1, source_target_pairs={{8,0},{12,4},{16,24},{20,28},{9,1},{13,5},{17,25},{21,29},{10,2},{... | collective-permute-start | bytes 1572872 | tf_op jit(solution)/shard_map/ppermute | solution.py:697
  45.6 14.9 %collective-permute-start.9 = (bf16[256,1024]{1,0:T(8,128)(2,1)}, bf16[256,1024]{1,0:T(8,128)(2,1)}, u32[]{:S(2)}, u32[]{:S(2)}) collective-permute-start(bf16[256,1024]{1,0:T(8,128)(2,1)} %collective-permute-done.6.rest_5_), channel_id=1, source_target_pairs={{0,4},{4,0},{8,12},{12,8},{16,20},{20,16},{24,28},{28,24},{1,5},{5... | collective-permute-start | bytes 1572872 | tf_op jit(solution)/shard_map/ppermute | solution.py:182
  48.7 18.8 %copy-start.35 = (s32[32]{0:T(128)S(1)}, s32[32]{0:T(128)}, u32[]{:S(2)}) copy-start(s32[32]{0:T(128)} %param.16) | copy-start | bytes 388
  48.7 19.3 %copy-start.34 = (s32[1,512]{1,0:T(1,128)S(1)}, s32[1,512]{1,0:T(1,128)}, u32[]{:S(2)}) copy-start(s32[1,512]{1,0:T(1,128)} %param.23) | copy-start | bytes 6148
  48.7 20.0 %copy-start.36 = (s32[8]{0:T(128)S(1)}, s32[8]{0:T(128)}, u32[]{:S(2)}) copy-start(s32[8]{0:T(128)} %param.22) | copy-start | bytes 100
  48.7 21.8 %copy-start.14 = (bf16[1,128,4096]{2,1,0:T(8,128)(2,1)S(1)}, bf16[1,128,4096]{2,1,0:T(8,128)(2,1)}, u32[]{:S(2)}) copy-start(bf16[1,128,4096]{2,1,0:T(8,128)(2,1)} %param.20) | copy-start | bytes 3145732
  49.6 14.8 %collective-permute-start.13 = (bf16[64,4096]{1,0:T(8,128)(2,1)}, bf16[64,4096]{1,0:T(8,128)(2,1)}, u32[]{:S(2)}, u32[]{:S(2)}) collective-permute-start(bf16[64,4096]{1,0:T(8,128)(2,1)} %get-tuple-element.202), channel_id=1, source_target_pairs={{0,2},{2,0},{1,3},{3,1},{4,6},{6,4},{5,7},{7,5},{8,10},{10,8},{9,1... | collective-permute-start | bytes 1572872 | tf_op jit(solution)/shard_map/ppermute | solution.py:182
  50.3 74.5 %copy-start.33 = (f32[4,128]{1,0:T(4,128)}, f32[4,128]{1,0:T(4,128)S(1)}, u32[]{:S(2)}) copy-start(f32[4,128]{1,0:T(4,128)S(1)} %convert_add_fusion) | copy-start | bytes 6148
  51.5 21.6 %copy-start.11 = (bf16[256,1024]{1,0:T(8,128)(2,1)}, bf16[256,1024]{1,0:T(8,128)(2,1)S(1)}, u32[]{:S(2)}) copy-start(bf16[256,1024]{1,0:T(8,128)(2,1)S(1)} %broadcast_select_fusion.1.rest_0_) | copy-start | bytes 1572868
  60.5 14.7 %copy-start.4 = (bf16[128,4096]{1,0:T(8,128)(2,1)}, bf16[128,4096]{1,0:T(8,128)(2,1)S(1)}, u32[]{:S(2)}) copy-start(bf16[128,4096]{1,0:T(8,128)(2,1)S(1)} %collective-permute-done.11.sibling_ref) | copy-start | bytes 3145732
  64.4 14.0 %collective-permute-start.14 = (bf16[256,1024]{1,0:T(8,128)(2,1)S(1)}, bf16[256,1024]{1,0:T(8,128)(2,1)}, u32[]{:S(2)}, u32[]{:S(2)}) collective-permute-start(bf16[256,1024]{1,0:T(8,128)(2,1)S(1)} %broadcast_select_fusion.1.rest_0_), channel_id=1, source_target_pairs={{0,4},{4,0},{8,12},{12,8},{16,20},{20,16},{24,28},{28,24},{1,5},{5... | collective-permute-start | bytes 1572872 | tf_op jit(solution)/shard_map/ppermute | solution.py:182
  65.9 13.4 %collective-permute-start.15 = (bf16[256,1024]{1,0:T(8,128)(2,1)S(1)}, bf16[256,1024]{1,0:T(8,128)(2,1)}, u32[]{:S(2)}, u32[]{:S(2)}) collective-permute-start(bf16[256,1024]{1,0:T(8,128)(2,1)S(1)} %broadcast_select_fusion.1.rest_0_), channel_id=1, source_target_pairs={{0,2},{2,0},{1,3},{3,1},{4,6},{6,4},{5,7},{7,5},{8,10},{10,8},{9,1... | collective-permute-start | bytes 1572872 | tf_op jit(solution)/shard_map/ppermute | solution.py:182
  67.4 9.5 %collective-permute-start.18 = (s32[32]{0:T(128)S(1)}, s32[32]{0:T(128)S(1)}, u32[]{:S(2)}, u32[]{:S(2)}) collective-permute-start(s32[32]{0:T(128)S(1)} %copy-done.35), channel_id=1, source_target_pairs={{0,1},{1,0},{2,3},{3,2},{4,5},{5,4},{6,7},{7,6},{8,9},{9,8},{10,11... | collective-permute-start | bytes 392 | tf_op jit(solution)/shard_map/ppermute | solution.py:182
  71.5 3.7 %copy-start.2 = (bf16[128,4096]{1,0:T(8,128)(2,1)S(1)}, bf16[128,4096]{1,0:T(8,128)(2,1)}, u32[]{:S(2)}) copy-start(bf16[128,4096]{1,0:T(8,128)(2,1)} %get-tuple-element.125.own_ref) | copy-start | bytes 3145732
  71.5 6.9 %collective-permute-start.16 = (bf16[128,2048]{1,0:T(8,128)(2,1)}, bf16[128,2048]{1,0:T(8,128)(2,1)}, u32[]{:S(2)}, u32[]{:S(2)}) collective-permute-start(bf16[128,2048]{1,0:T(8,128)(2,1)} %get-tuple-element.200), channel_id=1, source_target_pairs={{0,1},{1,0},{2,3},{3,2},{4,5},{5,4},{6,7},{7,6},{8,9},{9,8},{10,11... | collective-permute-start | bytes 1572872 | tf_op jit(solution)/shard_map/ppermute | solution.py:182
  73.1 5.3 %collective-permute-start.17 = (bf16[128,2048]{1,0:T(8,128)(2,1)}, bf16[128,2048]{1,0:T(8,128)(2,1)}, u32[]{:S(2)}, u32[]{:S(2)}) collective-permute-start(bf16[128,2048]{1,0:T(8,128)(2,1)} %get-tuple-element.198), channel_id=1, source_target_pairs={{0,1},{1,0},{2,3},{3,2},{4,5},{5,4},{6,7},{7,6},{8,9},{9,8},{10,11... | collective-permute-start | bytes 1572872 | tf_op jit(solution)/shard_map/ppermute | solution.py:182
  79.3 13.8 %collective-permute-start.19 = (bf16[256,1024]{1,0:T(8,128)(2,1)}, bf16[256,1024]{1,0:T(8,128)(2,1)S(1)}, u32[]{:S(2)}, u32[]{:S(2)}) collective-permute-start(bf16[256,1024]{1,0:T(8,128)(2,1)} %broadcast_select_fusion.rest_1_), channel_id=1, source_target_pairs={{0,4},{4,0},{8,12},{12,8},{16,20},{20,16},{24,28},{28,24},{1,5},{5... | collective-permute-start | bytes 1572872 | tf_op jit(solution)/shard_map/ppermute | solution.py:182
  79.8 13.5 %collective-permute-start.20 = (bf16[256,1024]{1,0:T(8,128)(2,1)}, bf16[256,1024]{1,0:T(8,128)(2,1)S(1)}, u32[]{:S(2)}, u32[]{:S(2)}) collective-permute-start(bf16[256,1024]{1,0:T(8,128)(2,1)} %broadcast_select_fusion.rest_1_), channel_id=1, source_target_pairs={{0,2},{2,0},{1,3},{3,1},{4,6},{6,4},{5,7},{7,5},{8,10},{10,8},{9,1... | collective-permute-start | bytes 1572872 | tf_op jit(solution)/shard_map/ppermute | solution.py:182
  83.3 10.5 %copy-start = (bf16[64,4096]{1,0:T(8,128)(2,1)S(1)}, bf16[64,4096]{1,0:T(8,128)(2,1)}, u32[]{:S(2)}) copy-start(bf16[64,4096]{1,0:T(8,128)(2,1)} %add_convert_fusion.1.visual_ref) | copy-start | bytes 1572868
  93.0 3.9 %copy-start.18 = (bf16[256,1024]{1,0:T(8,128)(2,1)}, bf16[256,1024]{1,0:T(8,128)(2,1)S(1)}, u32[]{:S(2)}) copy-start(bf16[256,1024]{1,0:T(8,128)(2,1)S(1)} %collective-permute-done.19.rest_3_) | copy-start | bytes 1572868
  93.3 3.6 %copy-start.17 = (bf16[256,1024]{1,0:T(8,128)(2,1)}, bf16[256,1024]{1,0:T(8,128)(2,1)S(1)}, u32[]{:S(2)}) copy-start(bf16[256,1024]{1,0:T(8,128)(2,1)S(1)} %collective-permute-done.20.rest_5_) | copy-start | bytes 1572868
  93.3 16.2 %collective-permute-start.23 = (bf16[8,1024,256]{2,1,0:T(8,128)(2,1)}, bf16[8,1024,256]{2,1,0:T(8,128)(2,1)}, u32[]{:S(2)}, u32[]{:S(2)}) collective-permute-start(bf16[8,1024,256]{2,1,0:T(8,128)(2,1)} %get-tuple-element.150.rest_0_), channel_id=1, source_target_pairs={{0,1},{1,0},{2,3},{3,2},{4,5},{5,4},{6,7},{7,6},{8,9},{9,8},{10,11... | collective-permute-start | bytes 12582920 | tf_op jit(solution)/shard_map/ppermute | solution.py:182
  93.3 14.5 %collective-permute-start.21 = (bf16[256,1024]{1,0:T(8,128)(2,1)}, bf16[256,1024]{1,0:T(8,128)(2,1)S(1)}, u32[]{:S(2)}, u32[]{:S(2)}) collective-permute-start(bf16[256,1024]{1,0:T(8,128)(2,1)} %collective-permute-done.14.rest_2_), channel_id=1, source_target_pairs={{0,2},{2,0},{1,3},{3,1},{4,6},{6,4},{5,7},{7,5},{8,10},{10,8},{9,1... | collective-permute-start | bytes 1572872 | tf_op jit(solution)/shard_map/ppermute | solution.py:182
  94.0 9.2 %collective-permute-start.24 = (f32[320]{0:T(512)S(1)}, f32[320]{0:T(512)S(1)}, u32[]{:S(2)}, u32[]{:S(2)}) collective-permute-start(f32[320]{0:T(512)S(1)} %pad_maximum_fusion.2), channel_id=1, source_target_pairs={{0,1},{1,0},{2,3},{3,2},{4,5},{5,4},{6,7},{7,6},{8,9},{9,8},{10,11... | collective-permute-start | bytes 3848 | tf_op jit(solution)/shard_map/ppermute | solution.py:182
  95.0 14.4 %copy-start.1 = (bf16[64,4096]{1,0:T(8,128)(2,1)S(1)}, bf16[64,4096]{1,0:T(8,128)(2,1)}, u32[]{:S(2)}) copy-start(bf16[64,4096]{1,0:T(8,128)(2,1)} %add_convert_fusion.1.visual_ref) | copy-start | bytes 1572868
  95.0 14.4 %copy-start.3 = (bf16[128,4096]{1,0:T(8,128)(2,1)S(1)}, bf16[128,4096]{1,0:T(8,128)(2,1)}, u32[]{:S(2)}) copy-start(bf16[128,4096]{1,0:T(8,128)(2,1)} %get-tuple-element.125.own_ref) | copy-start | bytes 3145732
  95.0 14.4 %copy-start.5 = (bf16[128,4096]{1,0:T(8,128)(2,1)S(1)}, bf16[128,4096]{1,0:T(8,128)(2,1)}, u32[]{:S(2)}) copy-start(bf16[128,4096]{1,0:T(8,128)(2,1)} %copy-done.4) | copy-start | bytes 3145732
  95.0 14.4 %copy-start.9 = (f32[16,1,256]{2,1,0:T(1,128)S(1)}, f32[16,1,256]{2,1,0:T(1,128)}, u32[]{:S(2)}) copy-start(f32[16,1,256]{2,1,0:T(1,128)} %constant_dynamic-slice_fusion.10) | copy-start | bytes 49156
  95.0 14.4 %copy-start.10 = (s32[17]{0:T(128)S(1)}, s32[17]{0:T(128)}, u32[]{:S(2)}) copy-start(s32[17]{0:T(128)} %stack.93.table_ref) | copy-start | bytes 208
  95.0 12.8 %collective-permute-start.25 = (bf16[32,4096]{1,0:T(8,128)(2,1)S(1)}, bf16[32,4096]{1,0:T(8,128)(2,1)S(1)}, u32[]{:S(2)}, u32[]{:S(2)}) collective-permute-start(bf16[32,4096]{1,0:T(8,128)(2,1)S(1)} %get-tuple-element.204), channel_id=1, source_target_pairs={{0,1},{1,0},{2,3},{3,2},{4,5},{5,4},{6,7},{7,6},{8,9},{9,8},{10,11... | collective-permute-start | bytes 786440 | tf_op jit(solution)/shard_map/ppermute | solution.py:182
  95.4 14.1 %collective-permute-start.22 = (bf16[256,1024]{1,0:T(8,128)(2,1)S(1)}, bf16[256,1024]{1,0:T(8,128)(2,1)S(1)}, u32[]{:S(2)}, u32[]{:S(2)}) collective-permute-start(bf16[256,1024]{1,0:T(8,128)(2,1)S(1)} %collective-permute-done.20.rest_5_), channel_id=1, source_target_pairs={{0,4},{4,0},{8,12},{12,8},{16,20},{20,16},{24,28},{28,24},{1,5},{5... | collective-permute-start | bytes 1572872 | tf_op jit(solution)/shard_map/ppermute | solution.py:182
  107.8 4.4 %copy-start.27 = (bf16[32,4096]{1,0:T(8,128)(2,1)}, bf16[32,4096]{1,0:T(8,128)(2,1)S(1)}, u32[]{:S(2)}) copy-start(bf16[32,4096]{1,0:T(8,128)(2,1)S(1)} %collective-permute-done.25.visual_other_ref) | copy-start | bytes 786436
  113.1 33.1 %copy-start.7 = (bf16[2,1024,256]{2,1,0:T(8,128)(2,1)}, bf16[2,1024,256]{2,1,0:T(8,128)(2,1)S(1)}, u32[]{:S(2)}) copy-start(bf16[2,1024,256]{2,1,0:T(8,128)(2,1)S(1)} %get-tuple-element.174.rest_2_) | copy-start | bytes 3145732
  113.1 1.6 collective-permute-start.26
  114.7 13.5 %collective-permute-start.28 = (bf16[6,1024,256]{2,1,0:T(8,128)(2,1)}, bf16[6,1024,256]{2,1,0:T(8,128)(2,1)}, u32[]{:S(2)}, u32[]{:S(2)}) collective-permute-start(bf16[6,1024,256]{2,1,0:T(8,128)(2,1)} %get-tuple-element.172.rest_1_), channel_id=1, source_target_pairs={{0,1},{1,0},{2,3},{3,2},{4,5},{5,4},{6,7},{7,6},{8,9},{9,8},{10,11... | collective-permute-start | bytes 9437192 | tf_op jit(solution)/shard_map/ppermute | solution.py:182
  114.8 13.3 %collective-permute-start.29 = (bf16[2,1024,256]{2,1,0:T(8,128)(2,1)S(1)}, bf16[2,1024,256]{2,1,0:T(8,128)(2,1)S(1)}, u32[]{:S(2)}, u32[]{:S(2)}) collective-permute-start(bf16[2,1024,256]{2,1,0:T(8,128)(2,1)S(1)} %get-tuple-element.174.rest_2_), channel_id=1, source_target_pairs={{0,1},{1,0},{2,3},{3,2},{4,5},{5,4},{6,7},{7,6},{8,9},{9,8},{10,11... | collective-permute-start | bytes 3145736 | tf_op jit(solution)/shard_map/ppermute | solution.py:182
  117.7 10.5 %collective-permute-start.30 = (bf16[256,512]{1,0:T(8,128)(2,1)}, bf16[256,512]{1,0:T(8,128)(2,1)S(1)}, u32[]{:S(2)}, u32[]{:S(2)}) collective-permute-start(bf16[256,512]{1,0:T(8,128)(2,1)} %get-tuple-element.175.rest_0_), channel_id=1, source_target_pairs={{0,2},{2,0},{1,3},{3,1},{4,6},{6,4},{5,7},{7,5},{8,10},{10,8},{9,1... | collective-permute-start | bytes 786440 | tf_op jit(solution)/shard_map/ppermute | solution.py:182
  119.2 11.7 %all-to-all-start = ((bf16[16,8,640]{2,1,0:T(8,128)(2,1)}), bf16[16,8,640]{2,1,0:T(8,128)(2,1)S(1)}, u32[]{:S(2)}, u32[]{:S(2)}) async-start(bf16[16,8,640]{2,1,0:T(8,128)(2,1)} %bitcast.60), calls=%async_computation | async-start | bytes 327680 | tf_op jit(solution)/shard_map/all_to_all | solution.py:788
  124.8 3.4 %collective-permute-start.27 = (bf16[160,512]{1,0:T(8,128)(2,1)S(1)}, bf16[160,512]{1,0:T(8,128)(2,1)S(1)}, u32[]{:S(2)}, u32[]{:S(2)}) collective-permute-start(bf16[160,512]{1,0:T(8,128)(2,1)S(1)} %pad_maximum_fusion.1), channel_id=1, source_target_pairs={{0,1},{1,0},{2,3},{3,2},{4,5},{5,4},{6,7},{7,6},{8,9},{9,8},{10,11... | collective-permute-start | bytes 491528 | tf_op jit(solution)/shard_map/ppermute | solution.py:182
  128.2 35.9 %copy-start.30 = (bf16[160,512]{1,0:T(8,128)(2,1)}, bf16[160,512]{1,0:T(8,128)(2,1)S(1)}, u32[]{:S(2)}) copy-start(bf16[160,512]{1,0:T(8,128)(2,1)S(1)} %collective-permute-done.27.pair_other_ref) | copy-start | bytes 491524
  128.2 26.1 %copy-start.12 = (bf16[2,1024,256]{2,1,0:T(8,128)(2,1)}, bf16[2,1024,256]{2,1,0:T(8,128)(2,1)S(1)}, u32[]{:S(2)}) copy-start(bf16[2,1024,256]{2,1,0:T(8,128)(2,1)S(1)} %collective-permute-done.29.rest_5_) | copy-start | bytes 3145732
  146.2 8.1 %copy-start.19 = (bf16[128,2048]{1,0:T(8,128)(2,1)S(1)}, bf16[128,2048]{1,0:T(8,128)(2,1)}, u32[]{:S(2)}) copy-start(bf16[128,2048]{1,0:T(8,128)(2,1)} %get-tuple-element.177) | copy-start | bytes 1572868
  146.2 5.6 %collective-permute-start.32 = (bf16[128,2048]{1,0:T(8,128)(2,1)}, bf16[128,2048]{1,0:T(8,128)(2,1)S(1)}, u32[]{:S(2)}, u32[]{:S(2)}) collective-permute-start(bf16[128,2048]{1,0:T(8,128)(2,1)} %get-tuple-element.180), channel_id=1, source_target_pairs={{0,1},{1,0},{2,3},{3,2},{4,5},{5,4},{6,7},{7,6},{8,9},{9,8},{10,11... | collective-permute-start | bytes 1572872 | tf_op jit(solution)/shard_map/ppermute | solution.py:182
  146.3 8.0 %collective-permute-start.31 = (bf16[128,2048]{1,0:T(8,128)(2,1)}, bf16[128,2048]{1,0:T(8,128)(2,1)S(1)}, u32[]{:S(2)}, u32[]{:S(2)}) collective-permute-start(bf16[128,2048]{1,0:T(8,128)(2,1)} %get-tuple-element.178), channel_id=1, source_target_pairs={{0,1},{1,0},{2,3},{3,2},{4,5},{5,4},{6,7},{7,6},{8,9},{9,8},{10,11... | collective-permute-start | bytes 1572872 | tf_op jit(solution)/shard_map/ppermute | solution.py:182
  146.8 12.9 %collective-permute-start.33 = (bf16[256,512]{1,0:T(8,128)(2,1)}, bf16[256,512]{1,0:T(8,128)(2,1)S(1)}, u32[]{:S(2)}, u32[]{:S(2)}) collective-permute-start(bf16[256,512]{1,0:T(8,128)(2,1)} %get-tuple-element.185), channel_id=1, source_target_pairs={{0,2},{2,0},{1,3},{3,1},{4,6},{6,4},{5,7},{7,5},{8,10},{10,8},{9,1... | collective-permute-start | bytes 786440 | tf_op jit(solution)/shard_map/ppermute | solution.py:182
  148.0 11.6 %all-to-all-start.1 = ((bf16[16,8,512]{2,1,0:T(8,128)(2,1)}), bf16[16,8,512]{2,1,0:T(8,128)(2,1)S(1)}, u32[]{:S(2)}, u32[]{:S(2)}) async-start(bf16[16,8,512]{2,1,0:T(8,128)(2,1)} %bitcast.62), calls=%async_computation.1 | async-start | bytes 262144 | tf_op jit(solution)/shard_map/all_to_all | solution.py:788
  162.5 1.6 collective-permute-start.34
  (10 other events, 12.7 us)

commit v5 on v4

--- a/solution.py
+++ b/solution.py
@@ -722,15 +722,15 @@
     far1, across = line(kv_weight, swapped), line(kv_weight, middle)
     inner_hidden = up_projection(patches, vit_gain[None, :], merge_up)
     rows_in = text[0]
-    beside0, below0, far1, across, inner_hidden, rows_in, core_word, table, gain = close(
-        (beside0, below0, far1, across, inner_hidden, rows_in, core_word, table, gain)
+    inner_hidden, rows_in, core_word, table, gain, far1, across, beside0, below0 = close(
+        (inner_hidden, rows_in, core_word, table, gain, far1, across, beside0, below0)
     )
 
     beside1, below1 = both(far1)
     across2, ends1 = line(far1, middle), line(across, outward)
     merged, merged_other = down_halves(inner_hidden, merge_down, core_word, block)
-    beside1, below1, across2, ends1, merged, merged_other, rows_in, core_word = close(
-        (beside1, below1, across2, ends1, merged, merged_other, rows_in, core_word)
+    merged, merged_other, rows_in, core_word, ends1, across2, below1, beside1 = close(
+        (merged, merged_other, rows_in, core_word, ends1, across2, below1, beside1)
     )
 
     corner0, corner1 = neighbor(beside0, "y", 1), neighbor(below1, "dp", 1)

time: 176 us -> 178 us (1.011)
  starting transfers between devices: 35.5 us -> 37.4 us
    ppermute x5, waiting for transfers between devices: 15.3 us -> 11.6 us  [line(): lax.ppermute(values, 'dp', [(2 * p + low, 2 * q + low) for p, q in pairs...]
    all_to_all x2, starting transfers between devices: 7.62 us -> 11.3 us  [between_chips(): lax.all_to_all(shaped, ('dp', 'y'), split_axis=0, concat_axis=0, tiled=True)]
    ppermute x30, starting transfers between devices: 21.5 us -> 18.1 us  [neighbor(): return lax.ppermute(values, axis, [(d, d ^ offset) for d in range(count)])]
    ppermute x30, waiting for transfers between devices: 21.1 us -> 23.3 us  [neighbor(): return lax.ppermute(values, axis, [(d, d ^ offset) for d in range(count)])]
where the time goes in v5:
time: 178 us; the launch traced here: 177 us
  Pallas kernels  60.9 us (34%)
  waiting for transfers between devices  41.7 us (23%)
  starting transfers between devices  37.4 us (21%)
  local copies, waits for them, and re-layouts  22 us (12%)
  other arithmetic  14 us (8%)
    ppermute x30, waiting for transfers between devices, neighbor(): return lax.ppermute(values, axis, [(d, d ^ offset) for d in range(count)])  23.3 us
    ppermute x30, starting transfers between devices, neighbor(): return lax.ppermute(values, axis, [(d, d ^ offset) for d in range(count)])  18.1 us
    pallas_call x1, Pallas kernels, attend_pair(): pl.pallas_call(kernel, grid=(steps,), in_specs=[part] * 4 + [vmem] * (7 +...  14.6 us
    pallas_call x3, Pallas kernels, project(): pl.pallas_call(kernel, in_specs=[smem()] + [vmem] * (4 + size + len(earli...  14.2 us
    ppermute x5, waiting for transfers between devices, line(): lax.ppermute(values, 'dp', [(2 * p + low, 2 * q + low) for p, q in pairs...  11.6 us
    all_to_all x2, starting transfers between devices, between_chips(): lax.all_to_all(shaped, ('dp', 'y'), split_axis=0, concat_axis=0, tiled=True)  11.3 us
    pallas_call x1, Pallas kernels, project_back(): pl.pallas_call(kernel, in_specs=[smem()] + [vmem] * 10 + [pl.BlockSpec(me...  10.5 us
    ppermute x5, starting transfers between devices, line(): lax.ppermute(values, 'dp', [(2 * p + low, 2 * q + low) for p, q in pairs...  7.97 us
  transfers between devices with their start and end apart: 37, of which 17 were waited for; matrix products, arithmetic and copies ran while one was open for 17% of the time, Pallas kernels for 18%

profile of v5, /device:TPU:0, one launch (start us, length us, event | category | flops | bytes accessed | tf_op | source)
XLA Modules:
  0.0 177.3 jit_solution(6111226910350289810)
XLA Ops:
  0.6 3.1 %collective-permute-start = (bf16[256,1024]{1,0:T(8,128)(2,1)}, bf16[256,1024]{1,0:T(8,128)(2,1)S(1)}, u32[]{:S(2)}, u32[]{:S(2)}) collective-permute-start(bf16[256,1024]{1,0:T(8,128)(2,1)} %rest_0_.1), channel_id=1, source_target_pairs={{0,8},{4,12},{8,0},{12,4},{16,24},{20,28},{24,16},{28,20},{1,9},{5... | collective-permute-start | bytes 1572872 | tf_op jit(solution)/shard_map/ppermute | solution.py:697
  4.4 1.6 collective-permute-start.2
  6.0 1.5 collective-permute-start.3
  7.5 1.3 broadcast_in_dim.77.gain_ref
  8.8 5.9 %merge_up.1.hidden_ref = bf16[128,768]{1,0:T(8,128)(2,1)} custom-call(bf16[128,5120]{1,0:T(8,128)(2,1)} %patch_ref.1, f32[1,1280]{1,0:T(1,128)} %broadcast_in_dim.77.gain_ref, bf16[5120,768]{1,0:T(8,128)(2,1)} %weight_ref.2), custom_call_target="tpu_custom_call" | custom-call | flops 1 | bytes 1 | tf_op jit(solution)/shard_map/merge_up/pallas_call | solution.py:267
  16.1 2.1 %collective-permute-done.2.rest_2_ = bf16[256,1024]{1,0:T(8,128)(2,1)} collective-permute-done((bf16[256,1024]{1,0:T(8,128)(2,1)}, bf16[256,1024]{1,0:T(8,128)(2,1)}, u32[]{:S(2)}, u32[]{:S(2)}) %collective-permute-start.2) | collective-permute-done | bytes 524320 | tf_op jit(solution)/shard_map/ppermute | solution.py:182
  18.2 1.1 collective-permute-done.3.rest_4_
  19.3 0.8 copy-done.24
  20.1 1.3 collective-permute-start.5
  21.4 1.5 collective-permute-start.6
  22.8 1.5 collective-permute-start.7
  24.9 7.4 %merge_down.1 = (bf16[128,4096]{1,0:T(8,128)(2,1)}, bf16[128,4096]{1,0:T(8,128)(2,1)}) custom-call(s32[1]{0:T(128)} %bitcast.1.core_ref, bf16[128,768]{1,0:T(8,128)(2,1)} %merge_up.1.hidden_ref, bf16[768,8192]{1,0:T(8,128)(2,1)} %weight_ref.3), custom_call_target="tpu_custom_call" | custom-call | flops 1 | bytes 1 | tf_op jit(solution)/shard_map/merge_down/pallas_call | solution.py:305
  32.3 3.4 %collective-permute-done.5 = bf16[256,1024]{1,0:T(8,128)(2,1)S(1)} collective-permute-done((bf16[256,1024]{1,0:T(8,128)(2,1)S(1)}, bf16[256,1024]{1,0:T(8,128)(2,1)S(1)}, u32[]{:S(2)}, u32[]{:S(2)}) %collective-permute-start.5) | collective-permute-done | bytes 524320 | tf_op jit(solution)/shard_map/ppermute | solution.py:697
  36.3 0.8 copy-done.25
  37.2 1.0 collective-permute-start.4
  38.2 3.9 %split_halves.1 = (bf16[128,4096]{1,0:T(8,128)(2,1)}, bf16[128,4096]{1,0:T(8,128)(2,1)}) custom-call(s32[1]{0:T(128)} %bitcast.1.core_ref, bf16[128,8192]{1,0:T(8,128)(2,1)} %bitcast.52), custom_call_target="tpu_custom_call" | custom-call | flops 1 | bytes 1 | tf_op jit(solution)/shard_map/split_halves/pallas_call | solution.py:231
  42.4 1.5 collective-permute-start.10
  44.5 1.5 add_convert_fusion
  46.0 0.9 constant_dynamic-slice_fusion.8
  46.9 1.1 collective-permute-start.13
  48.2 1.1 broadcast_select_fusion.1.rest_0_
  49.3 3.0 %collective-permute-done.4.rest_6_ = bf16[256,1024]{1,0:T(8,128)(2,1)} collective-permute-done((bf16[256,1024]{1,0:T(8,128)(2,1)}, bf16[256,1024]{1,0:T(8,128)(2,1)}, u32[]{:S(2)}, u32[]{:S(2)}) %collective-permute-start.4) | collective-permute-done | bytes 524320 | tf_op jit(solution)/shard_map/ppermute | solution.py:182
  52.3 8.2 %collective-permute-done.10 = bf16[256,1024]{1,0:T(8,128)(2,1)} collective-permute-done((bf16[256,1024]{1,0:T(8,128)(2,1)}, bf16[256,1024]{1,0:T(8,128)(2,1)}, u32[]{:S(2)}, u32[]{:S(2)}) %collective-permute-start.10) | collective-permute-done | bytes 524320 | tf_op jit(solution)/shard_map/ppermute | solution.py:697
  60.6 2.6 %collective-permute-done.13 = bf16[64,4096]{1,0:T(8,128)(2,1)} collective-permute-done((bf16[64,4096]{1,0:T(8,128)(2,1)}, bf16[64,4096]{1,0:T(8,128)(2,1)}, u32[]{:S(2)}, u32[]{:S(2)}) %collective-permute-start.13) | collective-permute-done | bytes 524320 | tf_op jit(solution)/shard_map/ppermute | solution.py:182
  63.8 0.9 collective-permute-start.15
  67.8 1.0 constant_dynamic-slice_fusion.6
  69.3 1.0 constant_dynamic-slice_fusion.4
  70.4 1.9 %broadcast_select_fusion.rest_1_ = bf16[256,1024]{1,0:T(8,128)(2,1)} fusion(bf16[256,1024]{1,0:T(8,128)(2,1)} %collective-permute-done.6, bf16[256,1024]{1,0:T(8,128)(2,1)} %collective-permute-done.10, pred[]{:T(512)S(6)} %or.3), kind=kLoop, calls=%fused_computation.10 | loop fusion | flops 262144 | bytes 1572865 | tf_op jit(solution)/shard_map/jit(_where)/select_n | solution.py:758
  75.0 0.7 and_convert_fusion.picking_ref
  75.7 1.2 collective-permute-done.14.rest_2_
  77.2 1.4 collective-permute-start.19
  78.6 0.9 collective-permute-start.20
  79.5 2.0 %add_convert_fusion.1.visual_ref = bf16[64,4096]{1,0:T(8,128)(2,1)} fusion(bf16[64,4096]{1,0:T(8,128)(2,1)} %collective-permute-done.13, bf16[64,4096]{1,0:T(8,128)(2,1)S(1)} %get-tuple-element.133), kind=kLoop, calls=%fused_computation.9 | loop fusion | flops 1048576 | bytes 1572864 | tf_op jit(solution)/shard_map/convert_element_type | solution.py:812
  81.5 6.6 %project_pairs.3 = (bf16[8,1024,256]{2,1,0:T(8,128)(2,1)}, f32[320,1024]{1,0:T(8,128)}) custom-call(s32[17]{0:T(128)} %stack.93.table_ref, bf16[128,4096]{1,0:T(8,128)(2,1)} %get-tuple-element.125.own_ref, bf16[128,4096]{1,0:T(8,128)(2,1)} %copy-done.4, bf16[64,4096]{1,0:T(8,128)(2,1)} %add_convert_fusion.1.visual_ref, f32[1,4096]{1,0:T(1,128)} %bitcast.49, ...), custom_call_target="tpu_custom_call" | custom-call | flops 1 | bytes 1 | tf_op jit(solution)/shard_map/project_pairs/pallas_call | solution.py:388
  88.1 2.2 %collective-permute-done.19.rest_3_ = bf16[256,1024]{1,0:T(8,128)(2,1)S(1)} collective-permute-done((bf16[256,1024]{1,0:T(8,128)(2,1)}, bf16[256,1024]{1,0:T(8,128)(2,1)S(1)}, u32[]{:S(2)}, u32[]{:S(2)}) %collective-permute-start.19) | collective-permute-done | bytes 524320 | tf_op jit(solution)/shard_map/ppermute | solution.py:182
  90.3 1.2 collective-permute-done.20.rest_5_
  91.5 1.1 collective-permute-start.21
  93.1 0.7 constant_dynamic-slice_fusion.2
  94.8 6.3 %project_pairs.4 = (bf16[6,1024,256]{2,1,0:T(8,128)(2,1)}, f32[320,1024]{1,0:T(8,128)}) custom-call(s32[17]{0:T(128)} %stack.93.table_ref, bf16[128,4096]{1,0:T(8,128)(2,1)} %get-tuple-element.125.own_ref, bf16[128,4096]{1,0:T(8,128)(2,1)} %copy-done.4, bf16[64,4096]{1,0:T(8,128)(2,1)} %add_convert_fusion.1.visual_ref, f32[1,4096]{1,0:T(1,128)} %bitcast.50, ...), custom_call_target="tpu_custom_call" | custom-call | flops 1 | bytes 1 | tf_op jit(solution)/shard_map/project_pairs/pallas_call | solution.py:388
  101.8 4.3 %collective-permute-done.21.rest_0_ = bf16[256,1024]{1,0:T(8,128)(2,1)S(1)} collective-permute-done((bf16[256,1024]{1,0:T(8,128)(2,1)}, bf16[256,1024]{1,0:T(8,128)(2,1)S(1)}, u32[]{:S(2)}, u32[]{:S(2)}) %collective-permute-start.21) | collective-permute-done | bytes 524320 | tf_op jit(solution)/shard_map/ppermute | solution.py:182
  106.0 2.2 %collective-permute-done.22.rest_1_ = bf16[256,1024]{1,0:T(8,128)(2,1)S(1)} collective-permute-done((bf16[256,1024]{1,0:T(8,128)(2,1)S(1)}, bf16[256,1024]{1,0:T(8,128)(2,1)S(1)}, u32[]{:S(2)}, u32[]{:S(2)}) %collective-permute-start.22) | collective-permute-done | bytes 524320 | tf_op jit(solution)/shard_map/ppermute | solution.py:182
  108.3 1.3 copy-done.6
  109.6 1.4 project_pairs.5
  111.0 0.8 copy-done.8
  111.8 1.6 collective-permute-done.26.received_ref
  114.2 2.3 %finish_pairs.1 = (bf16[256,512]{1,0:T(8,128)(2,1)}, bf16[64,512]{1,0:T(8,128)(2,1)}, bf16[128,640]{1,0:T(8,128)(2,1)}) custom-call(f32[320,512]{1,0:T(8,128)} %copy-done.8, bf16[320,512]{1,0:T(8,128)(2,1)} %copy-done.26, f32[1,320]{1,0:T(1,128)} %reshape_broadcast_in_dim.3.scale_ref, bf16[64,128]{1,0:T(8,128)(2,1)} %select_convert_fusion.codes_ref, ...), custom_call_target="tpu_custom_call" | custom-call | flops 1 | bytes 1 | tf_op jit(solution)/shard_map/finish_pairs/pallas_call | solution.py:418
  116.5 0.9 collective-permute-start.30
  117.4 7.5 %all-to-all-start = ((bf16[16,8,640]{2,1,0:T(8,128)(2,1)}), bf16[16,8,640]{2,1,0:T(8,128)(2,1)S(1)}, u32[]{:S(2)}, u32[]{:S(2)}) async-start(bf16[16,8,640]{2,1,0:T(8,128)(2,1)} %bitcast.60), calls=%async_computation | async-start | bytes 327680 | tf_op jit(solution)/shard_map/all_to_all | solution.py:788
  124.9 1.0 fusion.7
  125.9 0.8 constant_dynamic-slice_fusion
  126.8 0.9 copy.23.row_s
  127.6 0.9 copy.24.pos_ref
  128.5 0.8 copy.25.doc_ref
  130.1 2.7 %all-to-all-done = bf16[16,8,640]{2,1,0:T(8,128)(2,1)S(1)} async-done(((bf16[16,8,640]{2,1,0:T(8,128)(2,1)}), bf16[16,8,640]{2,1,0:T(8,128)(2,1)S(1)}, u32[]{:S(2)}, u32[]{:S(2)}) %all-to-all-start) | async-done | bytes 163872 | tf_op jit(solution)/shard_map/all_to_all | solution.py:788
  133.5 14.6 %attend.1 = (bf16[128,2048]{1,0:T(8,128)(2,1)}, bf16[128,2048]{1,0:T(8,128)(2,1)}, bf16[128,2048]{1,0:T(8,128)(2,1)}, bf16[128,2048]{1,0:T(8,128)(2,1)}, bf16[25...) custom-call(bf16[128,2048]{1,0:T(8,128)(2,1)} %get-tuple-element.127.qa, ...), custom_call_target="tpu_custom_call" | custom-call | flops 1 | bytes 1 | tf_op jit(solution)/shard_map/attend/pallas_call | solution.py:657
  148.7 1.2 collective-permute-start.33
  149.9 3.8 %all-to-all-start.1 = ((bf16[16,8,512]{2,1,0:T(8,128)(2,1)}), bf16[16,8,512]{2,1,0:T(8,128)(2,1)S(1)}, u32[]{:S(2)}, u32[]{:S(2)}) async-start(bf16[16,8,512]{2,1,0:T(8,128)(2,1)} %bitcast.62), calls=%async_computation.1 | async-start | bytes 262144 | tf_op jit(solution)/shard_map/all_to_all | solution.py:788
  153.7 2.5 %maximum_select_fusion.1 = bf16[128,4096]{1,0:T(8,128)(2,1)} fusion(bf16[128,2048]{1,0:T(8,128)(2,1)S(1)} %collective-permute-done.32, bf16[128,2048]{1,0:T(8,128)(2,1)} %get-tuple-element.179, pred[]{:T(512)S(6)} %eq.81), kind=kLoop, calls=%fused_computation.7 | loop fusion | flops 4718592 | bytes 2097153 | tf_op jit(solution)/shard_map/jit(_where)/select_n | solution.py:850
  156.2 1.2 maximum_select_fusion
  157.4 4.1 %all-to-all-done.1 = bf16[16,8,512]{2,1,0:T(8,128)(2,1)S(1)} async-done(((bf16[16,8,512]{2,1,0:T(8,128)(2,1)}), bf16[16,8,512]{2,1,0:T(8,128)(2,1)S(1)}, u32[]{:S(2)}, u32[]{:S(2)}) %all-to-all-start.1) | async-done | bytes 131104 | tf_op jit(solution)/shard_map/all_to_all | solution.py:788
  162.2 2.1 %sum_grads.1 = (bf16[160,512]{1,0:T(8,128)(2,1)}, bf16[160,512]{1,0:T(8,128)(2,1)}) custom-call(s32[1]{0:T(128)} %bitcast.1.core_ref, bf16[256,512]{1,0:T(8,128)(2,1)} %get-tuple-element.183.grad_ref, bf16[128,512]{1,0:T(8,128)(2,1)} %bitcast.59, bf16[128,64]{1,0:T(8,128)(2,1)} %and_convert_fusion.picking_ref, bf16[256,512]{1,0:T(8,128)(2,1)} %copy-done.28), custom_call_target="tpu_custom_call" | custom-call | flops 1 | bytes 1 | tf_op jit(solution)/shard_map/sum_grads/pallas_call | solution.py:461
  164.3 0.8 copy.26.scale_ref
  165.1 0.9 collective-permute-done.34.grad_other_ref
  166.6 10.5 %project_back.1 = (bf16[128,8192]{1,0:T(8,128)(2,1)}, bf16[32,8192]{1,0:T(8,128)(2,1)}) custom-call(s32[17]{0:T(128)} %stack.93.table_ref, bf16[160,512]{1,0:T(8,128)(2,1)} %get-tuple-element.186.grad_ref, bf16[160,512]{1,0:T(8,128)(2,1)} %copy-done.31, bf16[160,512]{1,0:T(8,128)(2,1)} %pad_maximum_fusion.pair_ref, bf16[160,512]{1,0:T(8,128)(2,1)} %copy-done.30, ...), custom_call_target="tpu_custom_call" | custom-call | flops 1 | bytes 1 | tf_op jit(solution)/shard_map/project_back/pallas_call | solution.py:558
  (153 shorter events, 17.9 us)
Async XLA Ops:
  0.6 15.5 %collective-permute-start = (bf16[256,1024]{1,0:T(8,128)(2,1)}, bf16[256,1024]{1,0:T(8,128)(2,1)S(1)}, u32[]{:S(2)}, u32[]{:S(2)}) collective-permute-start(bf16[256,1024]{1,0:T(8,128)(2,1)} %rest_0_.1), channel_id=1, source_target_pairs={{0,8},{4,12},{8,0},{12,4},{16,24},{20,28},{24,16},{28,20},{1,9},{5... | collective-permute-start | bytes 1572872 | tf_op jit(solution)/shard_map/ppermute | solution.py:697
  3.7 12.4 %collective-permute-start.1 = (bf16[256,1024]{1,0:T(8,128)(2,1)}, bf16[256,1024]{1,0:T(8,128)(2,1)S(1)}, u32[]{:S(2)}, u32[]{:S(2)}) collective-permute-start(bf16[256,1024]{1,0:T(8,128)(2,1)} %rest_0_.1), channel_id=1, source_target_pairs={{8,16},{12,20},{16,8},{20,12},{9,17},{13,21},{17,9},{21,13},{10,18... | collective-permute-start | bytes 1572872 | tf_op jit(solution)/shard_map/ppermute | solution.py:697
  4.4 13.8 %collective-permute-start.2 = (bf16[256,1024]{1,0:T(8,128)(2,1)}, bf16[256,1024]{1,0:T(8,128)(2,1)}, u32[]{:S(2)}, u32[]{:S(2)}) collective-permute-start(bf16[256,1024]{1,0:T(8,128)(2,1)} %rest_0_.1), channel_id=1, source_target_pairs={{0,4},{4,0},{8,12},{12,8},{16,20},{20,16},{24,28},{28,24},{1,5},{5... | collective-permute-start | bytes 1572872 | tf_op jit(solution)/shard_map/ppermute | solution.py:182
  6.0 13.3 %collective-permute-start.3 = (bf16[256,1024]{1,0:T(8,128)(2,1)}, bf16[256,1024]{1,0:T(8,128)(2,1)S(1)}, u32[]{:S(2)}, u32[]{:S(2)}) collective-permute-start(bf16[256,1024]{1,0:T(8,128)(2,1)} %rest_0_.1), channel_id=1, source_target_pairs={{0,2},{2,0},{1,3},{3,1},{4,6},{6,4},{5,7},{7,5},{8,10},{10,8},{9,1... | collective-permute-start | bytes 1572872 | tf_op jit(solution)/shard_map/ppermute | solution.py:182
  8.8 6.0 %copy-start.32 = (f32[8192]{0:T(1024)S(1)}, f32[8192]{0:T(1024)}, u32[]{:S(2)}) copy-start(f32[8192]{0:T(1024)} %param.18) | copy-start | bytes 98308
  16.1 16.2 %copy-start.23 = (bf16[256,1024]{1,0:T(8,128)(2,1)}, bf16[256,1024]{1,0:T(8,128)(2,1)S(1)}, u32[]{:S(2)}) copy-start(bf16[256,1024]{1,0:T(8,128)(2,1)S(1)} %collective-permute-done.rest_1_) | copy-start | bytes 1572868
  16.1 16.2 %copy-start.20 = (bf16[256,1024]{1,0:T(8,128)(2,1)}, bf16[256,1024]{1,0:T(8,128)(2,1)S(1)}, u32[]{:S(2)}) copy-start(bf16[256,1024]{1,0:T(8,128)(2,1)S(1)} %collective-permute-done.1) | copy-start | bytes 1572868
  20.1 15.6 %collective-permute-start.5 = (bf16[256,1024]{1,0:T(8,128)(2,1)S(1)}, bf16[256,1024]{1,0:T(8,128)(2,1)S(1)}, u32[]{:S(2)}, u32[]{:S(2)}) collective-permute-start(bf16[256,1024]{1,0:T(8,128)(2,1)S(1)} %collective-permute-done.1), channel_id=1, source_target_pairs={{8,0},{12,4},{16,24},{20,28},{9,1},{13,5},{17,25},{21,29},{10,2},{... | collective-permute-start | bytes 1572872 | tf_op jit(solution)/shard_map/ppermute | solution.py:697
  21.4 14.3 %collective-permute-start.6 = (bf16[256,1024]{1,0:T(8,128)(2,1)S(1)}, bf16[256,1024]{1,0:T(8,128)(2,1)}, u32[]{:S(2)}, u32[]{:S(2)}) collective-permute-start(bf16[256,1024]{1,0:T(8,128)(2,1)S(1)} %collective-permute-done.rest_1_), channel_id=1, source_target_pairs={{8,16},{12,20},{16,8},{20,12},{9,17},{13,21},{17,9},{21,13},{10,18... | collective-permute-start | bytes 1572872 | tf_op jit(solution)/shard_map/ppermute | solution.py:697
  22.8 12.9 %collective-permute-start.7 = (bf16[256,1024]{1,0:T(8,128)(2,1)S(1)}, bf16[256,1024]{1,0:T(8,128)(2,1)}, u32[]{:S(2)}, u32[]{:S(2)}) collective-permute-start(bf16[256,1024]{1,0:T(8,128)(2,1)S(1)} %collective-permute-done.rest_1_), channel_id=1, source_target_pairs={{0,2},{2,0},{1,3},{3,1},{4,6},{6,4},{5,7},{7,5},{8,10},{10,8},{9,1... | collective-permute-start | bytes 1572872 | tf_op jit(solution)/shard_map/ppermute | solution.py:182
  24.3 12.0 %collective-permute-start.8 = (bf16[256,1024]{1,0:T(8,128)(2,1)S(1)}, bf16[256,1024]{1,0:T(8,128)(2,1)S(1)}, u32[]{:S(2)}, u32[]{:S(2)}) collective-permute-start(bf16[256,1024]{1,0:T(8,128)(2,1)S(1)} %collective-permute-done.rest_1_), channel_id=1, source_target_pairs={{0,4},{4,0},{8,12},{12,8},{16,20},{20,16},{24,28},{28,24},{1,5},{5... | collective-permute-start | bytes 1572872 | tf_op jit(solution)/shard_map/ppermute | solution.py:182
  32.3 12.2 %copy-start.13 = (bf16[128,4096]{1,0:T(8,128)(2,1)S(1)}, bf16[128,4096]{1,0:T(8,128)(2,1)}, u32[]{:S(2)}) copy-start(bf16[128,4096]{1,0:T(8,128)(2,1)} %get-tuple-element.114) | copy-start | bytes 3145732
  35.7 6.4 %copy-start.21 = (bf16[256,1024]{1,0:T(8,128)(2,1)}, bf16[256,1024]{1,0:T(8,128)(2,1)S(1)}, u32[]{:S(2)}) copy-start(bf16[256,1024]{1,0:T(8,128)(2,1)S(1)} %collective-permute-done.5) | copy-start | bytes 1572868
  37.1 7.3 %collective-permute-start.12 = (bf16[128,4096]{1,0:T(8,128)(2,1)}, bf16[128,4096]{1,0:T(8,128)(2,1)}, u32[]{:S(2)}, u32[]{:S(2)}) collective-permute-start(bf16[128,4096]{1,0:T(8,128)(2,1)} %get-tuple-element.115), channel_id=1, source_target_pairs={{0,1},{1,0},{2,3},{3,2},{4,5},{5,4},{6,7},{7,6},{8,9},{9,8},{10,11... | collective-permute-start | bytes 3145736 | tf_op jit(solution)/shard_map/ppermute | solution.py:182
  37.2 15.1 %collective-permute-start.4 = (bf16[256,1024]{1,0:T(8,128)(2,1)}, bf16[256,1024]{1,0:T(8,128)(2,1)}, u32[]{:S(2)}, u32[]{:S(2)}) collective-permute-start(bf16[256,1024]{1,0:T(8,128)(2,1)} %collective-permute-done.2.rest_2_), channel_id=1, source_target_pairs={{0,2},{2,0},{1,3},{3,1},{4,6},{6,4},{5,7},{7,5},{8,10},{10,8},{9,1... | collective-permute-start | bytes 1572872 | tf_op jit(solution)/shard_map/ppermute | solution.py:182
  42.1 18.4 %collective-permute-start.11 = (bf16[128,4096]{1,0:T(8,128)(2,1)}, bf16[128,4096]{1,0:T(8,128)(2,1)S(1)}, u32[]{:S(2)}, u32[]{:S(2)}) collective-permute-start(bf16[128,4096]{1,0:T(8,128)(2,1)} %get-tuple-element.112), channel_id=1, source_target_pairs={{0,1},{1,0},{2,3},{3,2},{4,5},{5,4},{6,7},{7,6},{8,9},{9,8},{10,11... | collective-permute-start | bytes 3145736 | tf_op jit(solution)/shard_map/ppermute | solution.py:182
  42.4 18.2 %collective-permute-start.10 = (bf16[256,1024]{1,0:T(8,128)(2,1)}, bf16[256,1024]{1,0:T(8,128)(2,1)}, u32[]{:S(2)}, u32[]{:S(2)}) collective-permute-start(bf16[256,1024]{1,0:T(8,128)(2,1)} %collective-permute-done.6), channel_id=1, source_target_pairs={{8,0},{12,4},{16,24},{20,28},{9,1},{13,5},{17,25},{21,29},{10,2},{... | collective-permute-start | bytes 1572872 | tf_op jit(solution)/shard_map/ppermute | solution.py:697
  43.8 16.7 %collective-permute-start.9 = (bf16[256,1024]{1,0:T(8,128)(2,1)}, bf16[256,1024]{1,0:T(8,128)(2,1)}, u32[]{:S(2)}, u32[]{:S(2)}) collective-permute-start(bf16[256,1024]{1,0:T(8,128)(2,1)} %collective-permute-done.7.rest_5_), channel_id=1, source_target_pairs={{0,4},{4,0},{8,12},{12,8},{16,20},{20,16},{24,28},{28,24},{1,5},{5... | collective-permute-start | bytes 1572872 | tf_op jit(solution)/shard_map/ppermute | solution.py:182
  45.9 18.8 %copy-start.35 = (s32[32]{0:T(128)S(1)}, s32[32]{0:T(128)}, u32[]{:S(2)}) copy-start(s32[32]{0:T(128)} %param.16) | copy-start | bytes 388
  46.0 19.3 %copy-start.34 = (s32[1,512]{1,0:T(1,128)S(1)}, s32[1,512]{1,0:T(1,128)}, u32[]{:S(2)}) copy-start(s32[1,512]{1,0:T(1,128)} %param.23) | copy-start | bytes 6148
  46.0 20.0 %copy-start.36 = (s32[8]{0:T(128)S(1)}, s32[8]{0:T(128)}, u32[]{:S(2)}) copy-start(s32[8]{0:T(128)} %param.22) | copy-start | bytes 100
  46.0 21.8 %copy-start.14 = (bf16[1,128,4096]{2,1,0:T(8,128)(2,1)S(1)}, bf16[1,128,4096]{2,1,0:T(8,128)(2,1)}, u32[]{:S(2)}) copy-start(bf16[1,128,4096]{2,1,0:T(8,128)(2,1)} %param.20) | copy-start | bytes 3145732
  46.9 16.3 %collective-permute-start.13 = (bf16[64,4096]{1,0:T(8,128)(2,1)}, bf16[64,4096]{1,0:T(8,128)(2,1)}, u32[]{:S(2)}, u32[]{:S(2)}) collective-permute-start(bf16[64,4096]{1,0:T(8,128)(2,1)} %get-tuple-element.202), channel_id=1, source_target_pairs={{0,2},{2,0},{1,3},{3,1},{4,6},{6,4},{5,7},{7,5},{8,10},{10,8},{9,1... | collective-permute-start | bytes 1572872 | tf_op jit(solution)/shard_map/ppermute | solution.py:182
  48.2 78.5 %copy-start.33 = (f32[4,128]{1,0:T(4,128)}, f32[4,128]{1,0:T(4,128)S(1)}, u32[]{:S(2)}) copy-start(f32[4,128]{1,0:T(4,128)S(1)} %convert_add_fusion) | copy-start | bytes 6148
  49.3 21.0 %copy-start.11 = (bf16[256,1024]{1,0:T(8,128)(2,1)}, bf16[256,1024]{1,0:T(8,128)(2,1)S(1)}, u32[]{:S(2)}) copy-start(bf16[256,1024]{1,0:T(8,128)(2,1)S(1)} %broadcast_select_fusion.1.rest_0_) | copy-start | bytes 1572868
  60.6 12.0 %copy-start.4 = (bf16[128,4096]{1,0:T(8,128)(2,1)}, bf16[128,4096]{1,0:T(8,128)(2,1)S(1)}, u32[]{:S(2)}) copy-start(bf16[128,4096]{1,0:T(8,128)(2,1)S(1)} %collective-permute-done.11.sibling_ref) | copy-start | bytes 3145732
  63.2 13.7 %collective-permute-start.14 = (bf16[256,1024]{1,0:T(8,128)(2,1)S(1)}, bf16[256,1024]{1,0:T(8,128)(2,1)}, u32[]{:S(2)}, u32[]{:S(2)}) collective-permute-start(bf16[256,1024]{1,0:T(8,128)(2,1)S(1)} %broadcast_select_fusion.1.rest_0_), channel_id=1, source_target_pairs={{0,4},{4,0},{8,12},{12,8},{16,20},{20,16},{24,28},{28,24},{1,5},{5... | collective-permute-start | bytes 1572872 | tf_op jit(solution)/shard_map/ppermute | solution.py:182
  63.8 13.4 %collective-permute-start.15 = (bf16[256,1024]{1,0:T(8,128)(2,1)S(1)}, bf16[256,1024]{1,0:T(8,128)(2,1)}, u32[]{:S(2)}, u32[]{:S(2)}) collective-permute-start(bf16[256,1024]{1,0:T(8,128)(2,1)S(1)} %broadcast_select_fusion.1.rest_0_), channel_id=1, source_target_pairs={{0,2},{2,0},{1,3},{3,1},{4,6},{6,4},{5,7},{7,5},{8,10},{10,8},{9,1... | collective-permute-start | bytes 1572872 | tf_op jit(solution)/shard_map/ppermute | solution.py:182
  64.7 9.5 %collective-permute-start.18 = (s32[32]{0:T(128)S(1)}, s32[32]{0:T(128)S(1)}, u32[]{:S(2)}, u32[]{:S(2)}) collective-permute-start(s32[32]{0:T(128)S(1)} %copy-done.35), channel_id=1, source_target_pairs={{0,1},{1,0},{2,3},{3,2},{4,5},{5,4},{6,7},{7,6},{8,9},{9,8},{10,11... | collective-permute-start | bytes 392 | tf_op jit(solution)/shard_map/ppermute | solution.py:182
  68.8 3.7 %copy-start.2 = (bf16[128,4096]{1,0:T(8,128)(2,1)S(1)}, bf16[128,4096]{1,0:T(8,128)(2,1)}, u32[]{:S(2)}) copy-start(bf16[128,4096]{1,0:T(8,128)(2,1)} %get-tuple-element.125.own_ref) | copy-start | bytes 3145732
  68.8 6.9 %collective-permute-start.16 = (bf16[128,2048]{1,0:T(8,128)(2,1)}, bf16[128,2048]{1,0:T(8,128)(2,1)}, u32[]{:S(2)}, u32[]{:S(2)}) collective-permute-start(bf16[128,2048]{1,0:T(8,128)(2,1)} %get-tuple-element.200), channel_id=1, source_target_pairs={{0,1},{1,0},{2,3},{3,2},{4,5},{5,4},{6,7},{7,6},{8,9},{9,8},{10,11... | collective-permute-start | bytes 1572872 | tf_op jit(solution)/shard_map/ppermute | solution.py:182
  70.3 5.3 %collective-permute-start.17 = (bf16[128,2048]{1,0:T(8,128)(2,1)}, bf16[128,2048]{1,0:T(8,128)(2,1)}, u32[]{:S(2)}, u32[]{:S(2)}) collective-permute-start(bf16[128,2048]{1,0:T(8,128)(2,1)} %get-tuple-element.198), channel_id=1, source_target_pairs={{0,1},{1,0},{2,3},{3,2},{4,5},{5,4},{6,7},{7,6},{8,9},{9,8},{10,11... | collective-permute-start | bytes 1572872 | tf_op jit(solution)/shard_map/ppermute | solution.py:182
  77.2 13.1 %collective-permute-start.19 = (bf16[256,1024]{1,0:T(8,128)(2,1)}, bf16[256,1024]{1,0:T(8,128)(2,1)S(1)}, u32[]{:S(2)}, u32[]{:S(2)}) collective-permute-start(bf16[256,1024]{1,0:T(8,128)(2,1)} %broadcast_select_fusion.rest_1_), channel_id=1, source_target_pairs={{0,4},{4,0},{8,12},{12,8},{16,20},{20,16},{24,28},{28,24},{1,5},{5... | collective-permute-start | bytes 1572872 | tf_op jit(solution)/shard_map/ppermute | solution.py:182
  78.6 12.9 %collective-permute-start.20 = (bf16[256,1024]{1,0:T(8,128)(2,1)}, bf16[256,1024]{1,0:T(8,128)(2,1)S(1)}, u32[]{:S(2)}, u32[]{:S(2)}) collective-permute-start(bf16[256,1024]{1,0:T(8,128)(2,1)} %broadcast_select_fusion.rest_1_), channel_id=1, source_target_pairs={{0,2},{2,0},{1,3},{3,1},{4,6},{6,4},{5,7},{7,5},{8,10},{10,8},{9,1... | collective-permute-start | bytes 1572872 | tf_op jit(solution)/shard_map/ppermute | solution.py:182
  81.5 11.1 %copy-start = (bf16[64,4096]{1,0:T(8,128)(2,1)S(1)}, bf16[64,4096]{1,0:T(8,128)(2,1)}, u32[]{:S(2)}) copy-start(bf16[64,4096]{1,0:T(8,128)(2,1)} %add_convert_fusion.1.visual_ref) | copy-start | bytes 1572868
  90.3 4.5 %copy-start.18 = (bf16[256,1024]{1,0:T(8,128)(2,1)}, bf16[256,1024]{1,0:T(8,128)(2,1)S(1)}, u32[]{:S(2)}) copy-start(bf16[256,1024]{1,0:T(8,128)(2,1)S(1)} %collective-permute-done.19.rest_3_) | copy-start | bytes 1572868
  91.5 3.3 %copy-start.17 = (bf16[256,1024]{1,0:T(8,128)(2,1)}, bf16[256,1024]{1,0:T(8,128)(2,1)S(1)}, u32[]{:S(2)}) copy-start(bf16[256,1024]{1,0:T(8,128)(2,1)S(1)} %collective-permute-done.20.rest_5_) | copy-start | bytes 1572868
  91.5 16.8 %collective-permute-start.23 = (bf16[8,1024,256]{2,1,0:T(8,128)(2,1)}, bf16[8,1024,256]{2,1,0:T(8,128)(2,1)}, u32[]{:S(2)}, u32[]{:S(2)}) collective-permute-start(bf16[8,1024,256]{2,1,0:T(8,128)(2,1)} %get-tuple-element.150.rest_0_), channel_id=1, source_target_pairs={{0,1},{1,0},{2,3},{3,2},{4,5},{5,4},{6,7},{7,6},{8,9},{9,8},{10,11... | collective-permute-start | bytes 12582920 | tf_op jit(solution)/shard_map/ppermute | solution.py:182
  91.5 14.5 %collective-permute-start.21 = (bf16[256,1024]{1,0:T(8,128)(2,1)}, bf16[256,1024]{1,0:T(8,128)(2,1)S(1)}, u32[]{:S(2)}, u32[]{:S(2)}) collective-permute-start(bf16[256,1024]{1,0:T(8,128)(2,1)} %collective-permute-done.14.rest_2_), channel_id=1, source_target_pairs={{0,2},{2,0},{1,3},{3,1},{4,6},{6,4},{5,7},{7,5},{8,10},{10,8},{9,1... | collective-permute-start | bytes 1572872 | tf_op jit(solution)/shard_map/ppermute | solution.py:182
  92.8 8.3 %collective-permute-start.24 = (f32[320]{0:T(512)S(1)}, f32[320]{0:T(512)S(1)}, u32[]{:S(2)}, u32[]{:S(2)}) collective-permute-start(f32[320]{0:T(512)S(1)} %pad_maximum_fusion.2), channel_id=1, source_target_pairs={{0,1},{1,0},{2,3},{3,2},{4,5},{5,4},{6,7},{7,6},{8,9},{9,8},{10,11... | collective-permute-start | bytes 3848 | tf_op jit(solution)/shard_map/ppermute | solution.py:182
  93.8 14.4 %copy-start.1 = (bf16[64,4096]{1,0:T(8,128)(2,1)S(1)}, bf16[64,4096]{1,0:T(8,128)(2,1)}, u32[]{:S(2)}) copy-start(bf16[64,4096]{1,0:T(8,128)(2,1)} %add_convert_fusion.1.visual_ref) | copy-start | bytes 1572868
  93.8 14.4 %copy-start.3 = (bf16[128,4096]{1,0:T(8,128)(2,1)S(1)}, bf16[128,4096]{1,0:T(8,128)(2,1)}, u32[]{:S(2)}) copy-start(bf16[128,4096]{1,0:T(8,128)(2,1)} %get-tuple-element.125.own_ref) | copy-start | bytes 3145732
  93.8 14.4 %copy-start.5 = (bf16[128,4096]{1,0:T(8,128)(2,1)S(1)}, bf16[128,4096]{1,0:T(8,128)(2,1)}, u32[]{:S(2)}) copy-start(bf16[128,4096]{1,0:T(8,128)(2,1)} %copy-done.4) | copy-start | bytes 3145732
  93.8 14.4 %copy-start.9 = (f32[16,1,256]{2,1,0:T(1,128)S(1)}, f32[16,1,256]{2,1,0:T(1,128)}, u32[]{:S(2)}) copy-start(f32[16,1,256]{2,1,0:T(1,128)} %constant_dynamic-slice_fusion.10) | copy-start | bytes 49156
  93.8 14.4 %copy-start.10 = (s32[17]{0:T(128)S(1)}, s32[17]{0:T(128)}, u32[]{:S(2)}) copy-start(s32[17]{0:T(128)} %stack.93.table_ref) | copy-start | bytes 208
  93.8 12.2 %collective-permute-start.25 = (bf16[32,4096]{1,0:T(8,128)(2,1)S(1)}, bf16[32,4096]{1,0:T(8,128)(2,1)S(1)}, u32[]{:S(2)}, u32[]{:S(2)}) collective-permute-start(bf16[32,4096]{1,0:T(8,128)(2,1)S(1)} %get-tuple-element.204), channel_id=1, source_target_pairs={{0,1},{1,0},{2,3},{3,2},{4,5},{5,4},{6,7},{7,6},{8,9},{9,8},{10,11... | collective-permute-start | bytes 786440 | tf_op jit(solution)/shard_map/ppermute | solution.py:182
  94.2 14.1 %collective-permute-start.22 = (bf16[256,1024]{1,0:T(8,128)(2,1)S(1)}, bf16[256,1024]{1,0:T(8,128)(2,1)S(1)}, u32[]{:S(2)}, u32[]{:S(2)}) collective-permute-start(bf16[256,1024]{1,0:T(8,128)(2,1)S(1)} %collective-permute-done.20.rest_5_), channel_id=1, source_target_pairs={{0,4},{4,0},{8,12},{12,8},{16,20},{20,16},{24,28},{28,24},{1,5},{5... | collective-permute-start | bytes 1572872 | tf_op jit(solution)/shard_map/ppermute | solution.py:182
  106.0 5.0 %copy-start.27 = (bf16[32,4096]{1,0:T(8,128)(2,1)}, bf16[32,4096]{1,0:T(8,128)(2,1)S(1)}, u32[]{:S(2)}) copy-start(bf16[32,4096]{1,0:T(8,128)(2,1)S(1)} %collective-permute-done.25.visual_other_ref) | copy-start | bytes 786436
  111.8 36.2 %copy-start.7 = (bf16[2,1024,256]{2,1,0:T(8,128)(2,1)}, bf16[2,1024,256]{2,1,0:T(8,128)(2,1)S(1)}, u32[]{:S(2)}) copy-start(bf16[2,1024,256]{2,1,0:T(8,128)(2,1)S(1)} %get-tuple-element.174.rest_2_) | copy-start | bytes 3145732
  111.8 1.6 collective-permute-start.26
  113.5 16.6 %collective-permute-start.28 = (bf16[6,1024,256]{2,1,0:T(8,128)(2,1)}, bf16[6,1024,256]{2,1,0:T(8,128)(2,1)}, u32[]{:S(2)}, u32[]{:S(2)}) collective-permute-start(bf16[6,1024,256]{2,1,0:T(8,128)(2,1)} %get-tuple-element.172.rest_1_), channel_id=1, source_target_pairs={{0,1},{1,0},{2,3},{3,2},{4,5},{5,4},{6,7},{7,6},{8,9},{9,8},{10,11... | collective-permute-start | bytes 9437192 | tf_op jit(solution)/shard_map/ppermute | solution.py:182
  113.6 16.4 %collective-permute-start.29 = (bf16[2,1024,256]{2,1,0:T(8,128)(2,1)S(1)}, bf16[2,1024,256]{2,1,0:T(8,128)(2,1)S(1)}, u32[]{:S(2)}, u32[]{:S(2)}) collective-permute-start(bf16[2,1024,256]{2,1,0:T(8,128)(2,1)S(1)} %get-tuple-element.174.rest_2_), channel_id=1, source_target_pairs={{0,1},{1,0},{2,3},{3,2},{4,5},{5,4},{6,7},{7,6},{8,9},{9,8},{10,11... | collective-permute-start | bytes 3145736 | tf_op jit(solution)/shard_map/ppermute | solution.py:182
  116.5 13.6 %collective-permute-start.30 = (bf16[256,512]{1,0:T(8,128)(2,1)}, bf16[256,512]{1,0:T(8,128)(2,1)S(1)}, u32[]{:S(2)}, u32[]{:S(2)}) collective-permute-start(bf16[256,512]{1,0:T(8,128)(2,1)} %get-tuple-element.175.rest_0_), channel_id=1, source_target_pairs={{0,2},{2,0},{1,3},{3,1},{4,6},{6,4},{5,7},{7,5},{8,10},{10,8},{9,1... | collective-permute-start | bytes 786440 | tf_op jit(solution)/shard_map/ppermute | solution.py:182
  117.4 15.4 %all-to-all-start = ((bf16[16,8,640]{2,1,0:T(8,128)(2,1)}), bf16[16,8,640]{2,1,0:T(8,128)(2,1)S(1)}, u32[]{:S(2)}, u32[]{:S(2)}) async-start(bf16[16,8,640]{2,1,0:T(8,128)(2,1)} %bitcast.60), calls=%async_computation | async-start | bytes 327680 | tf_op jit(solution)/shard_map/all_to_all | solution.py:788
  126.7 3.4 %collective-permute-start.27 = (bf16[160,512]{1,0:T(8,128)(2,1)S(1)}, bf16[160,512]{1,0:T(8,128)(2,1)S(1)}, u32[]{:S(2)}, u32[]{:S(2)}) collective-permute-start(bf16[160,512]{1,0:T(8,128)(2,1)S(1)} %pad_maximum_fusion.1), channel_id=1, source_target_pairs={{0,1},{1,0},{2,3},{3,2},{4,5},{5,4},{6,7},{7,6},{8,9},{9,8},{10,11... | collective-permute-start | bytes 491528 | tf_op jit(solution)/shard_map/ppermute | solution.py:182
  130.0 35.9 %copy-start.30 = (bf16[160,512]{1,0:T(8,128)(2,1)}, bf16[160,512]{1,0:T(8,128)(2,1)S(1)}, u32[]{:S(2)}) copy-start(bf16[160,512]{1,0:T(8,128)(2,1)S(1)} %collective-permute-done.27.pair_other_ref) | copy-start | bytes 491524
  130.1 26.1 %copy-start.12 = (bf16[2,1024,256]{2,1,0:T(8,128)(2,1)}, bf16[2,1024,256]{2,1,0:T(8,128)(2,1)S(1)}, u32[]{:S(2)}) copy-start(bf16[2,1024,256]{2,1,0:T(8,128)(2,1)S(1)} %collective-permute-done.29.rest_5_) | copy-start | bytes 3145732
  130.1 2.7 %copy-start.29 = (bf16[256,512]{1,0:T(8,128)(2,1)}, bf16[256,512]{1,0:T(8,128)(2,1)S(1)}, u32[]{:S(2)}) copy-start(bf16[256,512]{1,0:T(8,128)(2,1)S(1)} %collective-permute-done.30.rest_1_) | copy-start | bytes 786436
  148.1 8.1 %copy-start.19 = (bf16[128,2048]{1,0:T(8,128)(2,1)S(1)}, bf16[128,2048]{1,0:T(8,128)(2,1)}, u32[]{:S(2)}) copy-start(bf16[128,2048]{1,0:T(8,128)(2,1)} %get-tuple-element.177) | copy-start | bytes 1572868
  148.1 5.6 %collective-permute-start.32 = (bf16[128,2048]{1,0:T(8,128)(2,1)}, bf16[128,2048]{1,0:T(8,128)(2,1)S(1)}, u32[]{:S(2)}, u32[]{:S(2)}) collective-permute-start(bf16[128,2048]{1,0:T(8,128)(2,1)} %get-tuple-element.180), channel_id=1, source_target_pairs={{0,1},{1,0},{2,3},{3,2},{4,5},{5,4},{6,7},{7,6},{8,9},{9,8},{10,11... | collective-permute-start | bytes 1572872 | tf_op jit(solution)/shard_map/ppermute | solution.py:182
  148.2 8.0 %collective-permute-start.31 = (bf16[128,2048]{1,0:T(8,128)(2,1)}, bf16[128,2048]{1,0:T(8,128)(2,1)S(1)}, u32[]{:S(2)}, u32[]{:S(2)}) collective-permute-start(bf16[128,2048]{1,0:T(8,128)(2,1)} %get-tuple-element.178), channel_id=1, source_target_pairs={{0,1},{1,0},{2,3},{3,2},{4,5},{5,4},{6,7},{7,6},{8,9},{9,8},{10,11... | collective-permute-start | bytes 1572872 | tf_op jit(solution)/shard_map/ppermute | solution.py:182
  148.7 12.8 %collective-permute-start.33 = (bf16[256,512]{1,0:T(8,128)(2,1)}, bf16[256,512]{1,0:T(8,128)(2,1)S(1)}, u32[]{:S(2)}, u32[]{:S(2)}) collective-permute-start(bf16[256,512]{1,0:T(8,128)(2,1)} %get-tuple-element.185), channel_id=1, source_target_pairs={{0,2},{2,0},{1,3},{3,1},{4,6},{6,4},{5,7},{7,5},{8,10},{10,8},{9,1... | collective-permute-start | bytes 786440 | tf_op jit(solution)/shard_map/ppermute | solution.py:182
  149.9 11.6 %all-to-all-start.1 = ((bf16[16,8,512]{2,1,0:T(8,128)(2,1)}), bf16[16,8,512]{2,1,0:T(8,128)(2,1)S(1)}, u32[]{:S(2)}, u32[]{:S(2)}) async-start(bf16[16,8,512]{2,1,0:T(8,128)(2,1)} %bitcast.62), calls=%async_computation.1 | async-start | bytes 262144 | tf_op jit(solution)/shard_map/all_to_all | solution.py:788
  164.3 1.6 collective-permute-start.34
  (10 other events, 9.3 us)
